TPU v7x, 32 devices: a whole 2x2x4 slice. The times are simulated.
32 devices in a mesh: group: 2 (over y), expert: 4 (over z), dp: 2 (over x), sub: 2 (over core).
Axes of the slice: x: 2, y: 2, z: 4, core: 2. Of those that a mesh axis runs over, the one named last changes fastest.
Arguments:
- layer_input: bfloat16 [1024, 2048], P(('group', 'expert', 'dp', 'sub')), parts along dimension 0, may hold values from -6 to 6
- output_grad: bfloat16 [1024, 2048], P(('group', 'expert', 'dp', 'sub')), parts along dimension 0, may hold values from -6 to 6
- routes: int32 [1024, 8], P(('group', 'expert', 'dp', 'sub')), parts along dimension 0, may hold values from 0 to 7, as said below
- routing_weight: float32 [1024, 8], P(('group', 'expert', 'dp', 'sub')), parts along dimension 0, may hold values from 0.02 to 0.5
- gate_proj: bfloat16 [8, 2048, 768], P(('expert', 'dp'), None, 'sub'), may hold values from -0.125 to 0.125
- up_proj: bfloat16 [8, 2048, 768], P(('expert', 'dp'), None, 'sub'), may hold values from -0.125 to 0.125
- down_proj: bfloat16 [8, 768, 2048], P(('expert', 'dp'), 'sub'), may hold values from -0.21875 to 0.21875
Outputs:
- input_grad: bfloat16 [1024, 2048], P(('group', 'expert', 'dp', 'sub')), parts along dimension 0
- routing_grad: float32 [1024, 8], P(('group', 'expert', 'dp', 'sub')), parts along dimension 0
- gate_grads: bfloat16 [16, 2048, 768], P(('group', 'expert', 'dp'), None, 'sub'), parts along dimension 0
- up_grads: bfloat16 [16, 2048, 768], P(('group', 'expert', 'dp'), None, 'sub'), parts along dimension 0
- down_grads: bfloat16 [16, 768, 2048], P(('group', 'expert', 'dp'), 'sub'), parts along dimension 0
There are 2 independent parts, one for each index of `group`. A program takes and returns all parts, laid end to end along the dimension named above; an argument that names none is the same for every part. Nothing has to cross between parts.
Inputs may be any that keep to these rules, and one draw needn't show every extreme that they name: `routes`: the expert numbers form 8 groups of 1 consecutive numbers, and each token names exactly one expert of every group, in any order. The tokens of one device name each expert at most 32 times; in every group one expert, the same on all devices of a part, is named exactly 32 times by the tokens of every device.
All inputs are finite; a program needn't handle non-finite values.
Results may differ from a plain program's by a relative error of at most 0.0064.
Values may be sent and summed in bfloat16 or wider, within the bound.
No kernel may reach another device: no remote copies, remote signals or barrier semaphores. Data moves between devices by JAX's collectives and lax.ppermute only.
A program may use at most 128 MiB of HBM per device.

v0:
```python
import jax
import jax.numpy as jnp
from jax import lax
from jax.sharding import PartitionSpec as P


def expert_rows(inputs, gate_w, up_w, down_w):
    rows_x, rows_e = inputs
    leading = rows_x.shape[:-1]
    model_width = rows_x.shape[-1]
    hidden = gate_w.shape[1]
    flat_x = rows_x.reshape(-1, model_width)
    flat_e = rows_e.reshape(-1, model_width)
    contract = (((1,), (1,)), ((), ()))
    pre_gate = jnp.dot(flat_x, gate_w, preferred_element_type=jnp.float32)
    pre_up = jnp.dot(flat_x, up_w, preferred_element_type=jnp.float32)
    sigmoid_gate = jax.nn.sigmoid(pre_gate)
    silu_gate = pre_gate * sigmoid_gate
    hidden_act = silu_gate * pre_up
    hidden_low = hidden_act.astype(jnp.bfloat16)
    back_hidden = lax.dot_general(flat_e, down_w, contract, preferred_element_type=jnp.float32)
    product = jnp.sum(hidden_act * back_hidden, axis=1)
    silu_slope = sigmoid_gate * (1.0 + pre_gate * (1.0 - sigmoid_gate))
    diff_gate = (back_hidden * pre_up * silu_slope).astype(jnp.bfloat16)
    diff_up = (back_hidden * silu_gate).astype(jnp.bfloat16)
    row_grad = lax.dot_general(
        diff_gate, gate_w, contract, preferred_element_type=jnp.float32
    ) + lax.dot_general(diff_up, up_w, contract, preferred_element_type=jnp.float32)
    return (
        row_grad.reshape(leading + (model_width,)),
        product.reshape(leading),
        rows_x,
        rows_e,
        hidden_low.reshape(leading + (hidden,)),
        diff_gate.reshape(leading + (hidden,)),
        diff_up.reshape(leading + (hidden,)),
    )


def per_device(layer_input, output_grad, routes, routing_weight, gate_proj, up_proj, down_proj):
    tok_count, model_width = layer_input.shape
    top_count = routes.shape[1]
    positions = lax.axis_size(("expert", "dp"))
    capacity = min(tok_count, 2 * tok_count * top_count // positions)
    row_count = tok_count * top_count
    slot_count = positions * capacity
    target = routes.reshape(-1)
    member = (target[:, None] == jnp.arange(positions, dtype=jnp.int32)[None, :]).astype(jnp.int32)
    earlier = jnp.cumsum(member, axis=0) - member
    slot_rank = jnp.sum(earlier * member, axis=1)
    slot_index = target * capacity + slot_rank
    source = (
        jnp.full((slot_count,), row_count, jnp.int32)
        .at[slot_index]
        .set(jnp.arange(row_count, dtype=jnp.int32))
    )
    filled = source < row_count
    picked = jnp.minimum(source, row_count - 1)
    token_index = picked // top_count
    row_scale = jnp.where(filled, routing_weight.reshape(-1)[picked], 0.0)
    send_x = jnp.where(
        filled[:, None], layer_input[token_index], jnp.zeros((), layer_input.dtype)
    ).reshape(positions, 1, capacity, model_width)
    send_e = (
        (row_scale[:, None] * output_grad[token_index].astype(jnp.float32))
        .astype(jnp.bfloat16)
        .reshape(positions, 1, capacity, model_width)
    )
    gate_w = gate_proj[0]
    up_w = up_proj[0]
    down_w = down_proj[0]
    hidden = gate_w.shape[1]
    paired = (
        lax.all_gather(send_x, "sub", axis=1, tiled=True),
        lax.all_gather(send_e, "sub", axis=1, tiled=True),
    )
    results = expert_rows(
        (
            lax.all_to_all(paired[0], ("expert", "dp"), split_axis=0, concat_axis=0, tiled=True),
            lax.all_to_all(paired[1], ("expert", "dp"), split_axis=0, concat_axis=0, tiled=True),
        ),
        gate_w,
        up_w,
        down_w,
    )
    row_part, product_part, rows_x, rows_e, hidden_low, diff_gate, diff_up = results
    returned = (
        lax.all_to_all(row_part, ("expert", "dp"), split_axis=0, concat_axis=0, tiled=True),
        lax.all_to_all(product_part, ("expert", "dp"), split_axis=0, concat_axis=0, tiled=True),
    )
    summed = (
        lax.psum_scatter(returned[0], "sub", scatter_dimension=1, tiled=True),
        lax.psum_scatter(returned[1], "sub", scatter_dimension=1, tiled=True),
    )
    back_rows = summed[0].astype(jnp.bfloat16)
    back_products = summed[1].astype(jnp.bfloat16)
    per_row = (
        back_rows.reshape(slot_count, model_width)[slot_index]
        .astype(jnp.float32)
        .reshape(tok_count, top_count, model_width)
    )
    input_grad = jnp.sum(per_row, axis=1).astype(jnp.bfloat16)
    routing_grad = (
        back_products.reshape(slot_count)[slot_index]
        .astype(jnp.float32)
        .reshape(tok_count, top_count)
        / routing_weight
    )
    over_rows = (((0,), (0,)), ((), ()))
    flat_x = rows_x.reshape(-1, model_width)
    flat_e = rows_e.reshape(-1, model_width)
    gate_grads = lax.dot_general(
        flat_x, diff_gate.reshape(-1, hidden), over_rows, preferred_element_type=jnp.float32
    ).astype(jnp.bfloat16)[None]
    up_grads = lax.dot_general(
        flat_x, diff_up.reshape(-1, hidden), over_rows, preferred_element_type=jnp.float32
    ).astype(jnp.bfloat16)[None]
    down_grads = lax.dot_general(
        hidden_low.reshape(-1, hidden), flat_e, over_rows, preferred_element_type=jnp.float32
    ).astype(jnp.bfloat16)[None]
    return (input_grad, routing_grad, gate_grads, up_grads, down_grads)


def solution(mesh):
    placed = (
        P(("group", "expert", "dp", "sub"), None),
        P(("group", "expert", "dp", "sub"), None),
        P(("group", "expert", "dp", "sub"), None),
        P(("group", "expert", "dp", "sub"), None),
        P(("expert", "dp"), None, "sub"),
        P(("expert", "dp"), None, "sub"),
        P(("expert", "dp"), "sub", None),
    )
    return jax.shard_map(
        per_device,
        mesh=mesh,
        in_specs=placed,
        out_specs=(
            P(("group", "expert", "dp", "sub"), None),
            P(("group", "expert", "dp", "sub"), None),
            P(("group", "expert", "dp"), None, "sub"),
            P(("group", "expert", "dp"), None, "sub"),
            P(("group", "expert", "dp"), "sub", None),
        ),
        check_vma=False,
    )
```

profile of v0, /device:TPU:0, one launch (start us, length us, event | category | flops | bytes accessed | tf_op | source)
XLA Modules:
  0.0 285.8 jit_solution(18414120001281675781)
XLA Ops:
  7.2 0.8 broadcast_multiply_fusion
  9.2 0.8 copy.31
  11.0 1.4 scatter_custom_fusion
  12.4 1.9 gather_fusion
  14.5 1.4 gather_fusion.2
  15.9 1.1 broadcast_select_fusion
  17.0 13.4 %all-gather.5.cloned.1.call-done = bf16[8,2,32,2048]{3,2,1,0:T(8,128)(2,1)} async-done(((bf16[8,1,32,2048]{3,2,1,0:T(8,128)(2,1)}), bf16[8,2,32,2048]{3,2,1,0:T(8,128)(2,1)}) %all-gather.5.cloned.1.call-update) | async-done | bytes 2097168 | tf_op jit(solution)/shard_map/all_gather | solution.py:74
  30.4 5.8 %all-to-all-start.1 = ((bf16[8,2,32,2048]{3,2,1,0:T(8,128)(2,1)}), bf16[8,2,32,2048]{3,2,1,0:T(8,128)(2,1)}, u32[]{:S(2)}, u32[]{:S(2)}) async-start(bf16[8,2,32,2048]{3,2,1,0:T(8,128)(2,1)} %all-gather.5.cloned.1.call-done), calls=%async_computation.1 | async-start | bytes 4194304 | tf_op jit(solution)/shard_map/all_to_all | solution.py:79
  36.3 1.4 gather_fusion.1
  37.7 1.2 fusion.3
  38.9 12.2 %all-gather.3.cloned.1.call-done = bf16[8,2,32,2048]{3,2,1,0:T(8,128)(2,1)} async-done(((bf16[8,1,32,2048]{3,2,1,0:T(8,128)(2,1)}), bf16[8,2,32,2048]{3,2,1,0:T(8,128)(2,1)}) %all-gather.3.cloned.1.call-update) | async-done | bytes 2097168 | tf_op jit(solution)/shard_map/all_gather | solution.py:75
  51.2 33.8 %all-to-all-done.1 = bf16[8,2,32,2048]{3,2,1,0:T(8,128)(2,1)} async-done(((bf16[8,2,32,2048]{3,2,1,0:T(8,128)(2,1)}), bf16[8,2,32,2048]{3,2,1,0:T(8,128)(2,1)}, u32[]{:S(2)}, u32[]{:S(2)}) %all-to-all-start.1) | async-done | bytes 2097184 | tf_op jit(solution)/shard_map/all_to_all | solution.py:79
  85.0 4.4 %all-to-all-start = ((bf16[8,2,32,2048]{3,2,1,0:T(8,128)(2,1)}), bf16[8,2,32,2048]{3,2,1,0:T(8,128)(2,1)}, u32[]{:S(2)}, u32[]{:S(2)}) async-start(bf16[8,2,32,2048]{3,2,1,0:T(8,128)(2,1)} %all-gather.3.cloned.1.call-done), calls=%async_computation | async-start | bytes 4194304 | tf_op jit(solution)/shard_map/all_to_all | solution.py:80
  89.4 3.5 %fusion.9 = f32[512,384]{0,1:T(8,128)} fusion(bf16[512,2048]{1,0:T(8,128)(2,1)} %bitcast.10, bf16[1,2048,384]{2,1,0:T(8,128)(2,1)S(1)} %copy-done.3), kind=kOutput, calls=%fused_computation.21 | convolution fusion | flops 805306368 | bytes 4456448 | tf_op jit(solution)/shard_map/dot_general | solution.py:16
  92.9 44.3 %all-to-all-done = bf16[8,2,32,2048]{3,2,1,0:T(8,128)(2,1)} async-done(((bf16[8,2,32,2048]{3,2,1,0:T(8,128)(2,1)}), bf16[8,2,32,2048]{3,2,1,0:T(8,128)(2,1)}, u32[]{:S(2)}, u32[]{:S(2)}) %all-to-all-start) | async-done | bytes 2097184 | tf_op jit(solution)/shard_map/all_to_all | solution.py:80
  137.2 3.1 %fusion.11 = f32[512,384]{0,1:T(8,128)S(1)} fusion(bf16[512,2048]{1,0:T(8,128)(2,1)} %bitcast.6, bf16[1,384,2048]{2,1,0:T(8,128)(2,1)} %param.13), kind=kOutput, calls=%fused_computation.23 | convolution fusion | flops 805306368 | bytes 4456448 | tf_op jit(solution)/shard_map/dot_general | solution.py:21
  140.4 4.5 %multiply_convert_fusion.1 = (bf16[512,384]{0,1:T(8,128)(2,1)S(1)}, f32[512]{0:T(512)}, bf16[512,384]{0,1:T(8,128)(2,1)}, f32[512,384]{0,1:T(8,128)}) fusion(f32[512,384]{0,1:T(8,128)S(1)} %fusion.11, f32[512,384]{0,1:T(8,128)S(1)} %copy-done.9, bf16[512,2048]{1,0:T(8,128)(2,1)} %bitcast.10, bf16[1,2048,384]{2,1,0:T(8,128)(2,1)S(1)} %copy-done), kind=kOutput, calls=%fused_computation.29 | convolution fusion | flops 808451584 | bytes 6817792 | tf_op jit(solution)/shard_map/dot_general | solution.py:15
  144.9 1.4 reshape.137
  146.2 3.9 %all-to-all-start.3 = ((f32[8,2,32]{2,1,0:T(2,128)}), f32[8,2,32]{2,1,0:T(2,128)}, u32[]{:S(2)}, u32[]{:S(2)}) async-start(f32[8,2,32]{2,1,0:T(2,128)} %reshape.137), calls=%async_computation.3 | async-start | bytes 16384 | tf_op jit(solution)/shard_map/all_to_all | solution.py:89
  150.1 1.3 fusion.4
  151.5 3.3 %convolution_add_fusion = f32[512,2048]{1,0:T(8,128)} fusion(f32[512,2048]{1,0:T(8,128)S(1)} %fusion.4, bf16[512,384]{0,1:T(8,128)(2,1)S(1)} %copy-done.4, bf16[1,2048,384]{2,1,0:T(8,128)(2,1)S(1)} %copy-done.3), kind=kOutput, calls=%fused_computation.6 | convolution fusion | flops 806354944 | bytes 10354688 | tf_op jit(solution)/shard_map/dot_general | solution.py:28
  154.8 1.9 all-to-all-done.3
  156.7 4.9 %all-to-all-start.2 = ((f32[8,2,32,2048]{3,2,1,0:T(8,128)}), f32[8,2,32,2048]{3,2,1,0:T(8,128)}, u32[]{:S(2)}, u32[]{:S(2)}) async-start(f32[8,2,32,2048]{3,2,1,0:T(8,128)} %bitcast.66), calls=%async_computation.2 | async-start | bytes 8388608 | tf_op jit(solution)/shard_map/all_to_all | solution.py:88
  162.2 4.1 %fusion = bf16[1,2048,384]{2,1,0:T(8,128)(2,1)} fusion(bf16[512,2048]{1,0:T(8,128)(2,1)} %bitcast.10, bf16[512,384]{0,1:T(8,128)(2,1)S(1)} %get-tuple-element.24), kind=kOutput, calls=%fused_computation.10 | convolution fusion | flops 806092800 | bytes 4063232 | tf_op jit(solution)/shard_map/dot_general | solution.py:112
  166.3 4.2 %fusion.1 = bf16[1,2048,384]{2,1,0:T(8,128)(2,1)} fusion(bf16[512,2048]{1,0:T(8,128)(2,1)} %bitcast.10, bf16[512,384]{0,1:T(8,128)(2,1)S(1)} %copy-done.5), kind=kOutput, calls=%fused_computation.11 | convolution fusion | flops 806092800 | bytes 4063232 | tf_op jit(solution)/shard_map/dot_general | solution.py:115
  170.4 3.8 %fusion.2 = bf16[1,384,2048]{2,1,0:T(8,128)(2,1)} fusion(bf16[512,2048]{1,0:T(8,128)(2,1)} %bitcast.6, f32[512,384]{0,1:T(8,128)S(1)} %copy-done.10, f32[512,384]{0,1:T(8,128)S(1)} %copy-done.11), kind=kOutput, calls=%fused_computation.12 | convolution fusion | flops 807272448 | bytes 5242880 | tf_op jit(solution)/shard_map/dot_general | solution.py:118
  174.9 78.7 %all-to-all-done.2 = f32[8,2,32,2048]{3,2,1,0:T(8,128)} async-done(((f32[8,2,32,2048]{3,2,1,0:T(8,128)}), f32[8,2,32,2048]{3,2,1,0:T(8,128)}, u32[]{:S(2)}, u32[]{:S(2)}) %all-to-all-start.2) | async-done | bytes 4194336 | tf_op jit(solution)/shard_map/all_to_all | solution.py:88
  253.6 15.1 %all-reduce.4 = (bf16[8,2,32]{2,0,1:T(8,128)(2,1)S(1)}, bf16[8,2,32,2048]{3,2,1,0:T(8,128)(2,1)}) all-reduce(f32[8,2,32]{2,0,1:T(8,128)S(1)} %copy.34, f32[8,2,32,2048]{3,2,1,0:T(8,128)} %all-to-all-done.2), channel_id=3, replica_groups=mesh['group'=2,'expert'=4,'dp'=2,'sub'=2] {'sub'}, use_global_device_ids=true, to_apply=%region_7.8.clone | all-reduce | flops 1049088 | bytes 6294528
  269.4 1.9 dynamic-slice_convert_fusion
  271.4 1.9 gather_fusion.4
  273.3 2.3 gather_fusion.3
  275.6 2.6 bitcast_reduce_fusion
  (55 shorter events, 5.3 us)
Async XLA Ops:
  7.2 133.2 %copy-start = (bf16[1,2048,384]{2,1,0:T(8,128)(2,1)S(1)}, bf16[1,2048,384]{2,1,0:T(8,128)(2,1)}, u32[]{:S(2)}) copy-start(bf16[1,2048,384]{2,1,0:T(8,128)(2,1)} %param.11) | copy-start | bytes 4718596
  7.2 7.3 %copy-start.1 = (bf16[32,2048]{1,0:T(8,128)(2,1)S(1)}, bf16[32,2048]{1,0:T(8,128)(2,1)}, u32[]{:S(2)}) copy-start(bf16[32,2048]{1,0:T(8,128)(2,1)} %param.7) | copy-start | bytes 393220
  7.2 23.2 %all-gather.5.cloned.1.call-start = ((), (), s32[]{:S(2)}) async-start(), calls=%async_computation.5 | async-start | bytes 3145728 | tf_op jit(solution)/shard_map/all_gather | solution.py:74
  11.0 3.5 %copy-start.6 = (s32[256,1]{0,1:T(1,128)}, s32[256,1]{0,1:T(1,128)S(1)}, u32[]{:S(2)}) copy-start(s32[256,1]{0,1:T(1,128)S(1)} %compare_select_fusion) | copy-start | bytes 3076
  17.0 19.3 %copy-start.2 = (bf16[32,2048]{1,0:T(8,128)(2,1)S(1)}, bf16[32,2048]{1,0:T(8,128)(2,1)}, u32[]{:S(2)}) copy-start(bf16[32,2048]{1,0:T(8,128)(2,1)} %param.8) | copy-start | bytes 393220
  30.4 54.6 %all-to-all-start.1 = ((bf16[8,2,32,2048]{3,2,1,0:T(8,128)(2,1)}), bf16[8,2,32,2048]{3,2,1,0:T(8,128)(2,1)}, u32[]{:S(2)}, u32[]{:S(2)}) async-start(bf16[8,2,32,2048]{3,2,1,0:T(8,128)(2,1)} %all-gather.5.cloned.1.call-done), calls=%async_computation.1 | async-start | bytes 4194304 | tf_op jit(solution)/shard_map/all_to_all | solution.py:79
  36.2 15.0 %all-gather.3.cloned.1.call-start = ((), (), s32[]{:S(2)}) async-start(), calls=%async_computation.4 | async-start | bytes 3145728 | tf_op jit(solution)/shard_map/all_gather | solution.py:75
  38.9 50.5 %copy-start.3 = (bf16[1,2048,384]{2,1,0:T(8,128)(2,1)S(1)}, bf16[1,2048,384]{2,1,0:T(8,128)(2,1)}, u32[]{:S(2)}) copy-start(bf16[1,2048,384]{2,1,0:T(8,128)(2,1)} %param.12) | copy-start | bytes 4718596
  85.0 52.2 %all-to-all-start = ((bf16[8,2,32,2048]{3,2,1,0:T(8,128)(2,1)}), bf16[8,2,32,2048]{3,2,1,0:T(8,128)(2,1)}, u32[]{:S(2)}, u32[]{:S(2)}) async-start(bf16[8,2,32,2048]{3,2,1,0:T(8,128)(2,1)} %all-gather.3.cloned.1.call-done), calls=%async_computation | async-start | bytes 4194304 | tf_op jit(solution)/shard_map/all_to_all | solution.py:80
  137.2 3.1 %copy-start.9 = (f32[512,384]{0,1:T(8,128)S(1)}, f32[512,384]{0,1:T(8,128)}, u32[]{:S(2)}) copy-start(f32[512,384]{0,1:T(8,128)} %fusion.9) | copy-start | bytes 2359300
  146.2 10.4 %all-to-all-start.3 = ((f32[8,2,32]{2,1,0:T(2,128)}), f32[8,2,32]{2,1,0:T(2,128)}, u32[]{:S(2)}, u32[]{:S(2)}) async-start(f32[8,2,32]{2,1,0:T(2,128)} %reshape.137), calls=%async_computation.3 | async-start | bytes 16384 | tf_op jit(solution)/shard_map/all_to_all | solution.py:89
  150.1 1.3 copy-start.4
  156.7 4.9 %copy-start.8 = (u32[32]{0:T(128)S(1)}, u32[32]{0:T(128)}, u32[]{:S(2)}) copy-start(u32[32]{0:T(128)} %constant.40) | copy-start | bytes 388
  156.7 5.5 %copy-start.7 = (s32[256,1]{0,1:T(1,128)S(1)}, s32[256,1]{0,1:T(1,128)}, u32[]{:S(2)}) copy-start(s32[256,1]{0,1:T(1,128)} %copy-done.6) | copy-start | bytes 3076
  156.7 97.0 %all-to-all-start.2 = ((f32[8,2,32,2048]{3,2,1,0:T(8,128)}), f32[8,2,32,2048]{3,2,1,0:T(8,128)}, u32[]{:S(2)}, u32[]{:S(2)}) async-start(f32[8,2,32,2048]{3,2,1,0:T(8,128)} %bitcast.66), calls=%async_computation.2 | async-start | bytes 8388608 | tf_op jit(solution)/shard_map/all_to_all | solution.py:88
  162.1 4.1 %copy-start.5 = (bf16[512,384]{0,1:T(8,128)(2,1)S(1)}, bf16[512,384]{0,1:T(8,128)(2,1)}, u32[]{:S(2)}) copy-start(bf16[512,384]{0,1:T(8,128)(2,1)} %get-tuple-element.26) | copy-start | bytes 1179652
  166.2 4.2 %copy-start.10 = (f32[512,384]{0,1:T(8,128)S(1)}, f32[512,384]{0,1:T(8,128)}, u32[]{:S(2)}) copy-start(f32[512,384]{0,1:T(8,128)} %fusion.9) | copy-start | bytes 2359300
  166.3 4.2 %copy-start.11 = (f32[512,384]{0,1:T(8,128)S(1)}, f32[512,384]{0,1:T(8,128)}, u32[]{:S(2)}) copy-start(f32[512,384]{0,1:T(8,128)} %get-tuple-element.29) | copy-start | bytes 2359300
Sparse Core Ops, SparseCore 0:
  17.1 13.2 all-gather.4
  39.2 11.9 all-gather.2
where the time goes:
time: 287 us; the launch traced here: 286 us
  waiting for transfers between devices  184 us (64%)
  matrix products  27.7 us (10%)
  starting transfers between devices  19 us (7%)
  local copies, waits for them, and re-layouts  18.7 us (7%)
  blocking collectives  15.1 us (5%)
  between operations  14.3 us (5%)
  other arithmetic  6.49 us (2%)
    all_to_all x1, waiting for transfers between devices, per_device(): lax.all_to_all(row_part, ('expert', 'dp'), split_axis=0, concat_axis=0, t...  78.7 us
    all_to_all x1, waiting for transfers between devices, per_device(): lax.all_to_all(paired[1], ('expert', 'dp'), split_axis=0, concat_axis=0,...  44.3 us
    all_to_all x1, waiting for transfers between devices, per_device(): lax.all_to_all(paired[0], ('expert', 'dp'), split_axis=0, concat_axis=0,...  33.8 us
    unnamed x1, blocking collectives  15.1 us
    all_gather x1, waiting for transfers between devices, per_device(): lax.all_gather(send_x, 'sub', axis=1, tiled=True)  13.4 us
    all_gather x1, waiting for transfers between devices, per_device(): lax.all_gather(send_e, 'sub', axis=1, tiled=True)  12.2 us
    all_to_all x1, starting transfers between devices, per_device(): lax.all_to_all(paired[0], ('expert', 'dp'), split_axis=0, concat_axis=0,...  5.77 us
  transfers between devices with their start and end apart: 6, of which 6 were waited for; matrix products, arithmetic and copies ran while one was open for 8% of the time, Pallas kernels for 0%

commit v1 on v0

--- a/solution.py
+++ b/solution.py
@@ -1,7 +1,289 @@
+import functools
+
 import jax
 import jax.numpy as jnp
 from jax import lax
+from jax.experimental import pallas as pl
+from jax.experimental.pallas import tpu as pltpu
 from jax.sharding import PartitionSpec as P
+
+F32 = jnp.float32
+BF16 = jnp.bfloat16
+SIDE = 128
+NT = (((1,), (1,)), ((), ()))
+TN = (((0,), (0,)), ((), ()))
+VMEM_LIMIT = 40 * 1024 * 1024
+
+
+def whole(shape):
+    return pl.BlockSpec(shape, lambda *_: (0,) * len(shape))
+
+
+def split_columns(values, count, lane):
+    high = values.astype(BF16)
+    low = (values - high.astype(F32)).astype(BF16)
+    zero = jnp.zeros_like(high)
+    return jnp.where(lane < count, high, jnp.where(lane < 2 * count, low, zero))
+
+
+def pack_kernel(x_ref, e_ref, routes_ref, weight_ref, out_ref):
+    tok_count, width = x_ref.shape
+    top_count = routes_ref.shape[1]
+    out_ref[:tok_count, :width] = x_ref[...]
+    out_ref[tok_count:, :width] = e_ref[...]
+    routes = routes_ref[...]
+    weight = weight_ref[...]
+    lane = lax.broadcasted_iota(jnp.int32, (tok_count, SIDE), 1)
+    expert = lax.rem(lane, top_count)
+    table = jnp.zeros((tok_count, SIDE), F32)
+    for k in range(top_count):
+        table += jnp.where(routes[:, k : k + 1] == expert, weight[:, k : k + 1], 0.0)
+    out_ref[:tok_count, width:] = split_columns(table, top_count, lane)
+    out_ref[tok_count:, width:] = jnp.zeros((tok_count, SIDE), BF16)
+
+
+def pack(x, e, routes, weight):
+    tok_count, width = x.shape
+    return pl.pallas_call(
+        pack_kernel,
+        out_shape=jax.ShapeDtypeStruct((2 * tok_count, width + SIDE), BF16),
+        name="pack_tokens",
+    )(x, e, routes, weight)
+
+
+def rows_kernel(shards, steps, expert_ref, *refs):
+    shard_refs = refs[:shards]
+    gate_a, gate_b, up_a, up_b, down_a, down_b = refs[shards : shards + 6]
+    keep_ref, send_ref, xe_ref, own_ref, other_ref, weight_ref, total_ref, product_ref = refs[shards + 6 :]
+    step = pl.program_id(0)
+    tok_count = shard_refs[0].shape[0] // 2
+    rows = shards * tok_count
+    half = rows // 2
+    width = xe_ref.shape[1]
+    experts = expert_ref[1]
+
+    @pl.when(step == 0)
+    def _():
+        lane = lax.broadcasted_iota(jnp.int32, (tok_count, SIDE), 1)
+        wanted = (lane == expert_ref[0]) | (lane == expert_ref[0] + experts)
+        for i, ref in enumerate(shard_refs):
+            here = slice(i * tok_count, (i + 1) * tok_count)
+            xe_ref[here, :] = ref[:tok_count, :width]
+            xe_ref[rows + i * tok_count : rows + (i + 1) * tok_count, :] = ref[tok_count:, :width]
+            table = ref[:tok_count, width:].astype(F32)
+            weight_ref[here, :] = jnp.sum(jnp.where(wanted, table, 0.0), axis=1, keepdims=True)
+
+    x = xe_ref[:rows, :]
+    e = xe_ref[rows:, :]
+    block = gate_a.shape[-1]
+    gate_w = jnp.concatenate([gate_a[0], gate_b[0]], axis=1)
+    up_w = jnp.concatenate([up_a[0], up_b[0]], axis=1)
+    down_w = jnp.concatenate([down_a[0], down_b[0]], axis=0)
+    pre_gate = jnp.dot(x, gate_w, preferred_element_type=F32)
+    pre_up = jnp.dot(x, up_w, preferred_element_type=F32)
+    back = lax.dot_general(e, down_w, NT, preferred_element_type=F32)
+    sig = jax.nn.sigmoid(pre_gate)
+    silu = pre_gate * sig
+    hidden = silu * pre_up
+    product = jnp.sum(hidden * back, axis=1, keepdims=True)
+    weight = weight_ref[...]
+    scaled_back = back * weight
+    diff_gate = (scaled_back * pre_up * (sig * (1.0 + pre_gate * (1.0 - sig)))).astype(BF16)
+    diff_up = (scaled_back * silu).astype(BF16)
+    hidden_low = (hidden * weight).astype(BF16)
+    for i, ref in enumerate((own_ref, other_ref)):
+        here = slice(i * block, (i + 1) * block)
+        ref[:, :block] = diff_gate[:, here]
+        ref[:, block : 2 * block] = diff_up[:, here]
+        ref[:, 2 * block :] = hidden_low[:, here]
+    part = lax.dot_general(diff_gate, gate_w, NT, preferred_element_type=F32) + lax.dot_general(
+        diff_up, up_w, NT, preferred_element_type=F32
+    )
+
+    @pl.when(step == 0)
+    def _():
+        total_ref[...] = part
+        product_ref[...] = product
+
+    @pl.when(step > 0)
+    def _():
+        total_ref[...] += part
+        product_ref[...] += product
+
+    @pl.when(step == steps - 1)
+    def _():
+        lane = lax.broadcasted_iota(jnp.int32, (rows, SIDE), 1)
+        place = lax.rem(lane, experts) == expert_ref[0]
+        side = split_columns(jnp.where(place, product_ref[...], 0.0), experts, lane)
+        keep_ref[:, :width] = total_ref[:half, :]
+        keep_ref[:, width:] = side[:half].astype(F32)
+        send_ref[:, :width] = total_ref[half:, :].astype(BF16)
+        send_ref[:, width:] = side[half:]
+
+
+def expert_rows_chunk(name, shards, expert_info, weights):
+    count = len(shards)
+    tok_count = shards[0].shape[0] // 2
+    wide = shards[0].shape[1]
+    width = wide - SIDE
+    rows = count * tok_count
+    half_hidden = weights[0].shape[2]
+    block = 128
+    steps = half_hidden // block
+    column = pl.BlockSpec((1, width, block), lambda j: (0, 0, j))
+    row = pl.BlockSpec((1, block, width), lambda j: (0, j, 0))
+    flops = 5 * 2 * rows * width * 2 * half_hidden
+    return pl.pallas_call(
+        functools.partial(rows_kernel, count, steps),
+        grid=(steps,),
+        in_specs=[pl.BlockSpec(memory_space=pltpu.SMEM)]
+        + [whole(shards[0].shape)] * count
+        + [column, column, column, column, row, row],
+        out_specs=[
+            whole((rows // 2, wide)),
+            whole((rows // 2, wide)),
+            whole((2 * rows, width)),
+            pl.BlockSpec((rows, 3 * block), lambda j: (0, j)),
+            pl.BlockSpec((rows, 3 * block), lambda j: (0, j)),
+        ],
+        out_shape=[
+            jax.ShapeDtypeStruct((rows // 2, wide), F32),
+            jax.ShapeDtypeStruct((rows // 2, wide), BF16),
+            jax.ShapeDtypeStruct((2 * rows, width), BF16),
+            jax.ShapeDtypeStruct((rows, 3 * half_hidden), BF16),
+            jax.ShapeDtypeStruct((rows, 3 * half_hidden), BF16),
+        ],
+        scratch_shapes=[
+            pltpu.VMEM((rows, 1), F32),
+            pltpu.VMEM((rows, width), F32),
+            pltpu.VMEM((rows, 1), F32),
+        ],
+        compiler_params=pltpu.CompilerParams(vmem_limit_bytes=VMEM_LIMIT),
+        cost_estimate=pl.CostEstimate(
+            flops=flops, bytes_accessed=12 * width * half_hidden + 20 * rows * width, transcendentals=rows * half_hidden * 2
+        ),
+        name=name,
+    )(expert_info, *shards, *weights)
+
+
+def grads_kernel(parts, steps, *refs):
+    x_refs = refs[:parts]
+    e_refs = refs[parts : 2 * parts]
+    diff_refs = refs[2 * parts : 3 * parts]
+    gate_ref, up_ref, down_ref, diffs, hidden_t = refs[3 * parts :]
+    block = 128
+    hidden = gate_ref.shape[2]
+
+    @pl.when(pl.program_id(0) == 0)
+    def _():
+        start = 0
+        lows = []
+        for ref in diff_refs:
+            rows = ref.shape[0]
+            for j in range(hidden // block):
+                base = 3 * block * j
+                diffs[start : start + rows, j * block : (j + 1) * block] = ref[:, base : base + block]
+                diffs[start : start + rows, hidden + j * block : hidden + (j + 1) * block] = ref[
+                    :, base + block : base + 2 * block
+                ]
+            lows.append(
+                jnp.concatenate(
+                    [ref[:, 3 * block * j + 2 * block : 3 * block * (j + 1)] for j in range(hidden // block)], axis=1
+                )
+            )
+            start += rows
+        hidden_t[...] = jnp.concatenate(lows, axis=0).T
+
+    x = jnp.concatenate([ref[...] for ref in x_refs], axis=0)
+    e = jnp.concatenate([ref[...] for ref in e_refs], axis=0)
+    both = lax.dot_general(x, diffs[...], TN, preferred_element_type=F32).astype(BF16)
+    gate_ref[0] = both[:, :hidden]
+    up_ref[0] = both[:, hidden:]
+    down_ref[0] = jnp.dot(hidden_t[...], e, preferred_element_type=F32).astype(BF16)
+
+
+def weight_grads(xe_parts, diff_parts):
+    count = len(xe_parts)
+    width = xe_parts[0].shape[1]
+    hidden = diff_parts[0].shape[1] // 3
+    total = sum(part.shape[0] for part in diff_parts)
+    block = 256
+    steps = width // block
+    x_specs = [pl.BlockSpec((part.shape[0] // 2, block), lambda i: (0, i)) for part in xe_parts]
+    e_specs = [pl.BlockSpec((part.shape[0] // 2, block), lambda i: (1, i)) for part in xe_parts]
+    return pl.pallas_call(
+        functools.partial(grads_kernel, count, steps),
+        grid=(steps,),
+        in_specs=x_specs + e_specs + [whole(part.shape) for part in diff_parts],
+        out_specs=[
+            pl.BlockSpec((1, block, hidden), lambda i: (0, i, 0)),
+            pl.BlockSpec((1, block, hidden), lambda i: (0, i, 0)),
+            pl.BlockSpec((1, hidden, block), lambda i: (0, 0, i)),
+        ],
+        out_shape=[
+            jax.ShapeDtypeStruct((1, width, hidden), BF16),
+            jax.ShapeDtypeStruct((1, width, hidden), BF16),
+            jax.ShapeDtypeStruct((1, hidden, width), BF16),
+        ],
+        scratch_shapes=[pltpu.VMEM((total, 2 * hidden), BF16), pltpu.VMEM((hidden, total), BF16)],
+        compiler_params=pltpu.CompilerParams(vmem_limit_bytes=VMEM_LIMIT),
+        cost_estimate=pl.CostEstimate(
+            flops=6 * total * width * hidden, bytes_accessed=4 * total * width + 6 * width * hidden, transcendentals=0
+        ),
+        name="weight_grads",
+    )(*xe_parts, *xe_parts, *diff_parts)
+
+
+def swap(value, axis):
+    return lax.ppermute(value, axis, [(0, 1), (1, 0)])
+
+
+def far(value, axis, distance):
+    return lax.ppermute(value, axis, [(i, i ^ distance) for i in range(lax.axis_size(axis))])
+
+
+def every_token_to_every_expert(
+    layer_input, output_grad, routes, routing_weight, gate_proj, up_proj, down_proj
+):
+    tok_count, width = layer_input.shape
+    top_count = routes.shape[1]
+    lines = lax.axis_size("expert")
+    expert = lax.axis_index("expert") * lax.axis_size("dp") + lax.axis_index("dp")
+    expert_info = jnp.stack([expert, jnp.int32(top_count)]).astype(jnp.int32)
+    packed = pack(layer_input, output_grad, routes, routing_weight)
+    order = [k for k in range(1, lines) if k != 1] + [1] if lines > 1 else []
+    columns = {0: packed}
+    for k in order:
+        columns[k] = far(packed, "expert", k)
+    across = {k: swap(columns[k], "dp") for k in range(lines)}
+    other_weights = [swap(array, "sub") for array in (gate_proj, up_proj, down_proj)]
+    weights = (gate_proj, other_weights[0], up_proj, other_weights[1], down_proj, other_weights[2])
+    last = lines - 1
+    chunks = [list(range(last)), [last]] if lines > 1 else [[0]]
+    own_sum = None
+    arrived = []
+    xe_parts, diff_parts = [], []
+    for number, chunk in enumerate(chunks):
+        shards = [columns[k] for k in chunk] + [across[k] for k in chunk]
+        keep, send, xe, own_diff, other_diff = expert_rows_chunk("rows_%d" % number, shards, expert_info, weights)
+        summed = keep + swap(send, "dp").astype(F32)
+        for i, k in enumerate(chunk):
+            block = summed[i * tok_count : (i + 1) * tok_count]
+            if k == 0:
+                own_sum = block
+            else:
+                arrived.append(far(block.astype(BF16), "expert", k))
+        xe_parts += [xe, swap(xe, "sub")]
+        diff_parts += [own_diff, swap(other_diff, "sub")]
+    total = own_sum
+    for block in arrived:
+        total = total + block.astype(F32)
+    input_grad = total[:, :width].astype(BF16)
+    products = total[:, width : width + top_count] + total[:, width + top_count : width + 2 * top_count]
+    chosen = routes[:, :, None] == jnp.arange(top_count, dtype=jnp.int32)[None, None, :]
+    routing_grad = jnp.sum(jnp.where(chosen, products[:, None, :], 0.0), axis=2)
+    gate_grads, up_grads, down_grads = weight_grads(xe_parts, diff_parts)
+    return (input_grad, routing_grad, gate_grads, up_grads, down_grads)
 
 
 def expert_rows(inputs, gate_w, up_w, down_w):
@@ -37,7 +319,7 @@
     )
 
 
-def per_device(layer_input, output_grad, routes, routing_weight, gate_proj, up_proj, down_proj):
+def chosen_experts(layer_input, output_grad, routes, routing_weight, gate_proj, up_proj, down_proj):
     tok_count, model_width = layer_input.shape
     top_count = routes.shape[1]
     positions = lax.axis_size(("expert", "dp"))
@@ -121,6 +403,15 @@
     return (input_grad, routing_grad, gate_grads, up_grads, down_grads)
 
 
+def per_device(layer_input, output_grad, routes, routing_weight, gate_proj, up_proj, down_proj):
+    args = (layer_input, output_grad, routes, routing_weight, gate_proj, up_proj, down_proj)
+    lines = lax.axis_size("expert")
+    pairs = lax.axis_size("dp") == 2 and lax.axis_size("sub") == 2 and lines & (lines - 1) == 0
+    if pairs and 2 * lines == routes.shape[1] and gate_proj.shape[0] == 1:
+        return every_token_to_every_expert(*args)
+    return chosen_experts(*args)
+
+
 def solution(mesh):
     placed = (
         P(("group", "expert", "dp", "sub"), None),

time: 287 us -> 98.8 us (0.34)
  waiting for transfers between devices: 184 us -> 33.4 us
  Pallas kernels: 0 us -> 28.7 us
  matrix products: 27.7 us -> 0 us
  blocking collectives: 15.1 us -> 0 us
  between operations: 14.3 us -> 0.77 us
  local copies, waits for them, and re-layouts: 18.7 us -> 13 us
  other arithmetic: 6.49 us -> 0.95 us
    all_to_all x4 -> x0, waiting for transfers between devices: 159 us -> none  [the longest x1 78.7 us: per_device(): lax.all_to_all(row_part, ('expert', 'dp'), split_axis=0, concat_axis=0, t...]
    ppermute x0 -> x19, waiting for transfers between devices: none -> 33.4 us  [the longest x6 25.8 us: far(): lax.ppermute(value, axis, [(i, i ^ distance) for i in range(lax.axis_size...]
    pallas_call x0 -> x4, Pallas kernels: none -> 28.7 us  [the longest x2 19.3 us: expert_rows_chunk(): pl.pallas_call(functools.partial(rows_kernel, count, steps), grid=(steps,...]
    dot_general x8 -> x0, matrix products: 27.7 us -> none  [the longest x1 4.48 us: expert_rows(): pre_gate = jnp.dot(flat_x, gate_w, preferred_element_type=jnp.float32)]
    all_gather x2 -> x0, waiting for transfers between devices: 25.6 us -> none  [the longest x1 13.4 us: per_device(): lax.all_gather(send_x, 'sub', axis=1, tiled=True)]
    ppermute x0 -> x19, starting transfers between devices: none -> 20.9 us  [the longest x6 12.3 us: far(): lax.ppermute(value, axis, [(i, i ^ distance) for i in range(lax.axis_size...]
    all_to_all x4 -> x0, starting transfers between devices: 18.9 us -> none  [the longest x1 5.77 us: per_device(): lax.all_to_all(paired[0], ('expert', 'dp'), split_axis=0, concat_axis=0,...]
    unnamed x1 -> x0, blocking collectives: 15.1 us -> none
  transfers between devices with their start and end apart: 6 -> 19, of which waited for: 6 -> 7; matrix products, arithmetic and copies ran while one was open for 8% -> 5% of each run, Pallas kernels for 0% -> 22%
where the time goes in v1:
time: 98.8 us; the launch traced here: 97.8 us
  waiting for transfers between devices  33.4 us (34%)
  Pallas kernels  28.7 us (29%)
  starting transfers between devices  20.9 us (21%)
  local copies, waits for them, and re-layouts  13 us (13%)
    ppermute x6, waiting for transfers between devices, far(): lax.ppermute(value, axis, [(i, i ^ distance) for i in range(lax.axis_size...  25.8 us
    pallas_call x2, Pallas kernels, expert_rows_chunk(): pl.pallas_call(functools.partial(rows_kernel, count, steps), grid=(steps,...  19.3 us
    ppermute x6, starting transfers between devices, far(): lax.ppermute(value, axis, [(i, i ^ distance) for i in range(lax.axis_size...  12.3 us
    unnamed x34, local copies, waits for them, and re-layouts  12.3 us
    ppermute x13, starting transfers between devices, swap(): return lax.ppermute(value, axis, [(0, 1), (1, 0)])  8.59 us
    pallas_call x1, Pallas kernels, weight_grads(): pl.pallas_call(functools.partial(grads_kernel, count, steps), grid=(steps...  7.61 us
    ppermute x13, waiting for transfers between devices, swap(): return lax.ppermute(value, axis, [(0, 1), (1, 0)])  7.6 us
  transfers between devices with their start and end apart: 19, of which 7 were waited for; matrix products, arithmetic and copies ran while one was open for 5% of the time, Pallas kernels for 22%

profile of v1, /device:TPU:0, one launch (start us, length us, event | category | flops | bytes accessed | tf_op | source)
XLA Modules:
  0.0 97.8 jit_solution(3048189735317724718)
XLA Ops:
  1.7 1.4 %copy.15.routes_ref = s32[32,8]{1,0:T(8,128)} copy(s32[32,8]{0,1:T(8,128)} %param.9) | data formatting | bytes 2048 | tf_op args[2]
  3.0 1.4 %copy.16.weight_ref = f32[32,8]{1,0:T(8,128)} copy(f32[32,8]{0,1:T(8,128)} %param.10) | data formatting | bytes 2048 | tf_op args[3]
  4.4 1.8 %pack_tokens.1.refs_0_ = bf16[64,2176]{1,0:T(8,128)(2,1)} custom-call(bf16[32,2048]{1,0:T(8,128)(2,1)} %x_ref.1, bf16[32,2048]{1,0:T(8,128)(2,1)} %e_ref.1, s32[32,8]{1,0:T(8,128)} %copy.15.routes_ref, f32[32,8]{1,0:T(8,128)} %copy.16.weight_ref), custom_call_target="tpu_custom_call" | custom-call | tf_op jit(solution)/shard_map/pack_tokens/pallas_call | solution.py:47
  6.2 2.7 %collective-permute-start = (bf16[64,2176]{1,0:T(8,128)(2,1)}, bf16[64,2176]{1,0:T(8,128)(2,1)}, u32[]{:S(2)}, u32[]{:S(2)}) collective-permute-start(bf16[64,2176]{1,0:T(8,128)(2,1)} %pack_tokens.1.refs_0_), channel_id=1, source_target_pairs={{0,4},{4,0},{8,12},{12,8},{1,5},{5,1},{9,13},{13,9},{2,6},{6,2},{1... | collective-permute-start | bytes 835592 | tf_op jit(solution)/shard_map/ppermute | solution.py:242
  8.9 2.5 %collective-permute-start.11 = (bf16[64,2176]{1,0:T(8,128)(2,1)}, bf16[64,2176]{1,0:T(8,128)(2,1)S(1)}, u32[]{:S(2)}, u32[]{:S(2)}) collective-permute-start(bf16[64,2176]{1,0:T(8,128)(2,1)} %pack_tokens.1.refs_0_), channel_id=1, source_target_pairs={{0,12},{4,8},{8,4},{12,0},{1,13},{5,9},{9,5},{13,1},{2,14},{6,10},... | collective-permute-start | bytes 835592 | tf_op jit(solution)/shard_map/ppermute | solution.py:242
  11.3 5.1 %collective-permute-done.refs_1_ = bf16[64,2176]{1,0:T(8,128)(2,1)} collective-permute-done((bf16[64,2176]{1,0:T(8,128)(2,1)}, bf16[64,2176]{1,0:T(8,128)(2,1)}, u32[]{:S(2)}, u32[]{:S(2)}) %collective-permute-start) | collective-permute-done | bytes 278560 | tf_op jit(solution)/shard_map/ppermute | solution.py:242
  16.4 3.2 %collective-permute-start.1 = (bf16[64,2176]{1,0:T(8,128)(2,1)}, bf16[64,2176]{1,0:T(8,128)(2,1)}, u32[]{:S(2)}, u32[]{:S(2)}) collective-permute-start(bf16[64,2176]{1,0:T(8,128)(2,1)} %pack_tokens.1.refs_0_), channel_id=1, source_target_pairs={{0,8},{4,12},{8,0},{12,4},{1,9},{5,13},{9,1},{13,5},{2,10},{6,14},... | collective-permute-start | bytes 835592 | tf_op jit(solution)/shard_map/ppermute | solution.py:242
  19.7 5.4 %collective-permute-done.11.refs_0_ = bf16[64,2176]{1,0:T(8,128)(2,1)S(1)} collective-permute-done((bf16[64,2176]{1,0:T(8,128)(2,1)}, bf16[64,2176]{1,0:T(8,128)(2,1)S(1)}, u32[]{:S(2)}, u32[]{:S(2)}) %collective-permute-start.11) | collective-permute-done | bytes 278560 | tf_op jit(solution)/shard_map/ppermute | solution.py:242
  25.1 1.5 %collective-permute-start.12 = (bf16[64,2176]{1,0:T(8,128)(2,1)S(1)}, bf16[64,2176]{1,0:T(8,128)(2,1)S(1)}, u32[]{:S(2)}, u32[]{:S(2)}) collective-permute-start(bf16[64,2176]{1,0:T(8,128)(2,1)S(1)} %collective-permute-done.11.refs_0_), channel_id=1, source_target_pairs={{0,2},{2,0},{1,3},{3,1},{4,6},{6,4},{5,7},{7,5},{8,10},{10,8},{9,1... | collective-permute-start | bytes 835592 | tf_op jit(solution)/shard_map/ppermute | solution.py:238
  26.6 10.1 %collective-permute-done.1.refs_2_ = bf16[64,2176]{1,0:T(8,128)(2,1)} collective-permute-done((bf16[64,2176]{1,0:T(8,128)(2,1)}, bf16[64,2176]{1,0:T(8,128)(2,1)}, u32[]{:S(2)}, u32[]{:S(2)}) %collective-permute-start.1) | collective-permute-done | bytes 278560 | tf_op jit(solution)/shard_map/ppermute | solution.py:242
  36.7 1.5 %collective-permute-start.2 = (bf16[64,2176]{1,0:T(8,128)(2,1)}, bf16[64,2176]{1,0:T(8,128)(2,1)}, u32[]{:S(2)}, u32[]{:S(2)}) collective-permute-start(bf16[64,2176]{1,0:T(8,128)(2,1)} %pack_tokens.1.refs_0_), channel_id=1, source_target_pairs={{0,2},{2,0},{1,3},{3,1},{4,6},{6,4},{5,7},{7,5},{8,10},{10,8},{9,1... | collective-permute-start | bytes 835592 | tf_op jit(solution)/shard_map/ppermute | solution.py:238
  38.2 0.7 copy-done.10
  39.4 1.5 %collective-permute-start.4 = (bf16[64,2176]{1,0:T(8,128)(2,1)}, bf16[64,2176]{1,0:T(8,128)(2,1)}, u32[]{:S(2)}, u32[]{:S(2)}) collective-permute-start(bf16[64,2176]{1,0:T(8,128)(2,1)} %collective-permute-done.1.refs_2_), channel_id=1, source_target_pairs={{0,2},{2,0},{1,3},{3,1},{4,6},{6,4},{5,7},{7,5},{8,10},{10,8},{9,1... | collective-permute-start | bytes 835592 | tf_op jit(solution)/shard_map/ppermute | solution.py:238
  41.0 2.0 %copy-done = bf16[1,2048,384]{2,1,0:T(8,128)(2,1)S(1)} copy-done((bf16[1,2048,384]{2,1,0:T(8,128)(2,1)S(1)}, bf16[1,2048,384]{2,1,0:T(8,128)(2,1)}, u32[]{:S(2)}) %copy-start) | copy-done | bytes 1572888
  43.0 1.4 %copy-done.2 = bf16[1,2048,384]{2,1,0:T(8,128)(2,1)S(1)} copy-done((bf16[1,2048,384]{2,1,0:T(8,128)(2,1)S(1)}, bf16[1,2048,384]{2,1,0:T(8,128)(2,1)}, u32[]{:S(2)}) %copy-start.2) | copy-done | bytes 1572888
  44.4 1.4 %copy-done.4 = bf16[1,384,2048]{2,1,0:T(8,128)(2,1)S(1)} copy-done((bf16[1,384,2048]{2,1,0:T(8,128)(2,1)S(1)}, bf16[1,384,2048]{2,1,0:T(8,128)(2,1)}, u32[]{:S(2)}) %copy-start.4) | copy-done | bytes 1572888
  45.8 1.0 copy-done.11
  46.8 9.1 %rows_1.1 = (f32[32,2176]{1,0:T(8,128)S(1)}, bf16[32,2176]{1,0:T(8,128)(2,1)S(1)}, bf16[128,2048]{1,0:T(8,128)(2,1)}, bf16[64,1152]{1,0:T(8,128)(2,1)S(1)}, bf16[64,1152]{1,0:T(8,128)(2,1)}) custom-call(s32[2]{0:T(128)S(1)} %pad_add_fusion.expert_ref, bf16[64,2176]{1,0:T(8,128)(2,1)S(1)} %collective-permute-done.11.refs_0_, bf16[64,2176]{1,0:T(8,128)(2,1)S(1)} %copy-done.11, ...), custom_call_target="tpu_custom_call" | custom-call | flops 1006632960 | bytes 12058624 | tf_op jit(solution)/shard_map/rows_1/pallas_call | solution.py:136
  55.9 0.7 copy-done.13
  57.6 1.4 %copy-done.7 = bf16[1,2048,384]{2,1,0:T(8,128)(2,1)S(1)} copy-done((bf16[1,2048,384]{2,1,0:T(8,128)(2,1)S(1)}, bf16[1,2048,384]{2,1,0:T(8,128)(2,1)}, u32[]{:S(2)}) %copy-start.7) | copy-done | bytes 1572888
  59.0 10.2 %rows_0.1 = (f32[96,2176]{1,0:T(8,128)S(1)}, bf16[96,2176]{1,0:T(8,128)(2,1)S(1)}, bf16[384,2048]{1,0:T(8,128)(2,1)S(1)}, bf16[192,1152]{1,0:T(8,128)(2,1)S(1)}, bf16[192,1152]{1,0:T(8,128)(2,1)}) custom-call(s32[2]{0:T(128)S(1)} %pad_add_fusion.expert_ref, bf16[64,2176]{1,0:T(8,128)(2,1)S(1)} %copy-done.12, bf16[64,2176]{1,0:T(8,128)(2,1)} %collective-permute-done.refs_1_, ...), custom_call_target="tpu_custom_call" | custom-call | flops 3019898880 | bytes 17301504 | tf_op jit(solution)/shard_map/rows_0/pallas_call | solution.py:136
  69.2 1.5 %collective-permute-start.8 = (bf16[96,2176]{1,0:T(8,128)(2,1)S(1)}, bf16[96,2176]{1,0:T(8,128)(2,1)S(1)}, u32[]{:S(2)}, u32[]{:S(2)}) collective-permute-start(bf16[96,2176]{1,0:T(8,128)(2,1)S(1)} %get-tuple-element.19), channel_id=1, source_target_pairs={{0,2},{2,0},{1,3},{3,1},{4,6},{6,4},{5,7},{7,5},{8,10},{10,8},{9,1... | collective-permute-start | bytes 1253384 | tf_op jit(solution)/shard_map/ppermute | solution.py:238
  70.7 2.2 %collective-permute-start.14 = (bf16[32,2176]{1,0:T(8,128)(2,1)S(1)}, bf16[32,2176]{1,0:T(8,128)(2,1)S(1)}, u32[]{:S(2)}, u32[]{:S(2)}) collective-permute-start(bf16[32,2176]{1,0:T(8,128)(2,1)S(1)} %add_convert_fusion), channel_id=1, source_target_pairs={{0,12},{4,8},{8,4},{12,0},{1,13},{5,9},{9,5},{13,1},{2,14},{6,10},... | collective-permute-start | bytes 417800 | tf_op jit(solution)/shard_map/ppermute | solution.py:242
  73.0 7.1 %collective-permute-done.8 = bf16[96,2176]{1,0:T(8,128)(2,1)S(1)} collective-permute-done((bf16[96,2176]{1,0:T(8,128)(2,1)S(1)}, bf16[96,2176]{1,0:T(8,128)(2,1)S(1)}, u32[]{:S(2)}, u32[]{:S(2)}) %collective-permute-start.8) | collective-permute-done | bytes 417824 | tf_op jit(solution)/shard_map/ppermute | solution.py:238
  80.2 0.8 collective-permute-start.10
  81.0 0.9 collective-permute-start.9
  82.4 4.3 %collective-permute-done.10 = bf16[32,2176]{1,0:T(8,128)(2,1)S(1)} collective-permute-done((bf16[32,2176]{1,0:T(8,128)(2,1)S(1)}, bf16[32,2176]{1,0:T(8,128)(2,1)S(1)}, u32[]{:S(2)}, u32[]{:S(2)}) %collective-permute-start.10) | collective-permute-done | bytes 139296 | tf_op jit(solution)/shard_map/ppermute | solution.py:242
  86.7 0.9 collective-permute-done.9
  87.8 0.7 slice.41
  88.5 0.6 select_reduce_fusion
  89.2 1.0 %copy-done.9 = bf16[192,1152]{1,0:T(8,128)(2,1)S(1)} copy-done((bf16[192,1152]{1,0:T(8,128)(2,1)S(1)}, bf16[192,1152]{1,0:T(8,128)(2,1)}, u32[]{:S(2)}) %copy-start.9) | copy-done | bytes 442392
  90.2 7.6 %weight_grads.1 = (bf16[1,2048,384]{2,1,0:T(8,128)(2,1)}, bf16[1,2048,384]{2,1,0:T(8,128)(2,1)}, bf16[1,384,2048]{2,1,0:T(8,128)(2,1)}) custom-call(bf16[384,2048]{1,0:T(8,128)(2,1)S(1)} %get-tuple-element.22.refs_0_.refs_4_, bf16[384,2048]{1,0:T(8,128)(2,1)S(1)} %collective-permute-done.15.refs_1_.refs_5_, ...), custom_call_target="tpu_custom_call" | custom-call | flops 2415919104 | bytes 8912896 | tf_op jit(solution)/shard_map/weight_grads/pallas_call | solution.py:214
  (53 shorter events, 3.6 us)
Async XLA Ops:
  0.6 38.8 %collective-permute-start.5 = (bf16[1,2048,384]{2,1,0:T(8,128)(2,1)}, bf16[1,2048,384]{2,1,0:T(8,128)(2,1)S(1)}, u32[]{:S(2)}, u32[]{:S(2)}) collective-permute-start(bf16[1,2048,384]{2,1,0:T(8,128)(2,1)} %refs_2_.1), channel_id=1, source_target_pairs={{0,1},{1,0},{2,3},{3,2},{4,5},{5,4},{6,7},{7,6},{8,9},{9,8},{10,11... | collective-permute-start | bytes 4718600 | tf_op jit(solution)/shard_map/ppermute | solution.py:238
  1.1 39.8 %collective-permute-start.6 = (bf16[1,2048,384]{2,1,0:T(8,128)(2,1)}, bf16[1,2048,384]{2,1,0:T(8,128)(2,1)S(1)}, u32[]{:S(2)}, u32[]{:S(2)}) collective-permute-start(bf16[1,2048,384]{2,1,0:T(8,128)(2,1)} %refs_4_.1), channel_id=1, source_target_pairs={{0,1},{1,0},{2,3},{3,2},{4,5},{5,4},{6,7},{7,6},{8,9},{9,8},{10,11... | collective-permute-start | bytes 4718600 | tf_op jit(solution)/shard_map/ppermute | solution.py:238
  1.2 39.8 %collective-permute-start.7 = (bf16[1,384,2048]{2,1,0:T(8,128)(2,1)}, bf16[1,384,2048]{2,1,0:T(8,128)(2,1)}, u32[]{:S(2)}, u32[]{:S(2)}) collective-permute-start(bf16[1,384,2048]{2,1,0:T(8,128)(2,1)} %refs_6_.3), channel_id=1, source_target_pairs={{0,1},{1,0},{2,3},{3,2},{4,5},{5,4},{6,7},{7,6},{8,9},{9,8},{10,11... | collective-permute-start | bytes 4718600 | tf_op jit(solution)/shard_map/ppermute | solution.py:238
  6.2 10.2 %collective-permute-start = (bf16[64,2176]{1,0:T(8,128)(2,1)}, bf16[64,2176]{1,0:T(8,128)(2,1)}, u32[]{:S(2)}, u32[]{:S(2)}) collective-permute-start(bf16[64,2176]{1,0:T(8,128)(2,1)} %pack_tokens.1.refs_0_), channel_id=1, source_target_pairs={{0,4},{4,0},{8,12},{12,8},{1,5},{5,1},{9,13},{13,9},{2,6},{6,2},{1... | collective-permute-start | bytes 835592 | tf_op jit(solution)/shard_map/ppermute | solution.py:242
  8.9 16.2 %collective-permute-start.11 = (bf16[64,2176]{1,0:T(8,128)(2,1)}, bf16[64,2176]{1,0:T(8,128)(2,1)S(1)}, u32[]{:S(2)}, u32[]{:S(2)}) collective-permute-start(bf16[64,2176]{1,0:T(8,128)(2,1)} %pack_tokens.1.refs_0_), channel_id=1, source_target_pairs={{0,12},{4,8},{8,4},{12,0},{1,13},{5,9},{9,5},{13,1},{2,14},{6,10},... | collective-permute-start | bytes 835592 | tf_op jit(solution)/shard_map/ppermute | solution.py:242
  16.4 20.2 %collective-permute-start.1 = (bf16[64,2176]{1,0:T(8,128)(2,1)}, bf16[64,2176]{1,0:T(8,128)(2,1)}, u32[]{:S(2)}, u32[]{:S(2)}) collective-permute-start(bf16[64,2176]{1,0:T(8,128)(2,1)} %pack_tokens.1.refs_0_), channel_id=1, source_target_pairs={{0,8},{4,12},{8,0},{12,4},{1,9},{5,13},{9,1},{13,5},{2,10},{6,14},... | collective-permute-start | bytes 835592 | tf_op jit(solution)/shard_map/ppermute | solution.py:242
  25.1 13.1 %collective-permute-start.12 = (bf16[64,2176]{1,0:T(8,128)(2,1)S(1)}, bf16[64,2176]{1,0:T(8,128)(2,1)S(1)}, u32[]{:S(2)}, u32[]{:S(2)}) collective-permute-start(bf16[64,2176]{1,0:T(8,128)(2,1)S(1)} %collective-permute-done.11.refs_0_), channel_id=1, source_target_pairs={{0,2},{2,0},{1,3},{3,1},{4,6},{6,4},{5,7},{7,5},{8,10},{10,8},{9,1... | collective-permute-start | bytes 835592 | tf_op jit(solution)/shard_map/ppermute | solution.py:238
  36.7 20.4 %collective-permute-start.2 = (bf16[64,2176]{1,0:T(8,128)(2,1)}, bf16[64,2176]{1,0:T(8,128)(2,1)}, u32[]{:S(2)}, u32[]{:S(2)}) collective-permute-start(bf16[64,2176]{1,0:T(8,128)(2,1)} %pack_tokens.1.refs_0_), channel_id=1, source_target_pairs={{0,2},{2,0},{1,3},{3,1},{4,6},{6,4},{5,7},{7,5},{8,10},{10,8},{9,1... | collective-permute-start | bytes 835592 | tf_op jit(solution)/shard_map/ppermute | solution.py:238
  38.9 18.2 %collective-permute-start.3 = (bf16[64,2176]{1,0:T(8,128)(2,1)}, bf16[64,2176]{1,0:T(8,128)(2,1)}, u32[]{:S(2)}, u32[]{:S(2)}) collective-permute-start(bf16[64,2176]{1,0:T(8,128)(2,1)} %collective-permute-done.refs_1_), channel_id=1, source_target_pairs={{0,2},{2,0},{1,3},{3,1},{4,6},{6,4},{5,7},{7,5},{8,10},{10,8},{9,1... | collective-permute-start | bytes 835592 | tf_op jit(solution)/shard_map/ppermute | solution.py:238
  39.4 18.2 %collective-permute-start.4 = (bf16[64,2176]{1,0:T(8,128)(2,1)}, bf16[64,2176]{1,0:T(8,128)(2,1)}, u32[]{:S(2)}, u32[]{:S(2)}) collective-permute-start(bf16[64,2176]{1,0:T(8,128)(2,1)} %collective-permute-done.1.refs_2_), channel_id=1, source_target_pairs={{0,2},{2,0},{1,3},{3,1},{4,6},{6,4},{5,7},{7,5},{8,10},{10,8},{9,1... | collective-permute-start | bytes 835592 | tf_op jit(solution)/shard_map/ppermute | solution.py:238
  41.0 14.9 %copy-start.6 = (bf16[1,2048,384]{2,1,0:T(8,128)(2,1)}, bf16[1,2048,384]{2,1,0:T(8,128)(2,1)S(1)}, u32[]{:S(2)}) copy-start(bf16[1,2048,384]{2,1,0:T(8,128)(2,1)S(1)} %collective-permute-done.6.refs_9_.refs_5_) | copy-start | bytes 4718596
  41.0 2.0 %copy-start = (bf16[1,2048,384]{2,1,0:T(8,128)(2,1)S(1)}, bf16[1,2048,384]{2,1,0:T(8,128)(2,1)}, u32[]{:S(2)}) copy-start(bf16[1,2048,384]{2,1,0:T(8,128)(2,1)} %refs_2_.1) | copy-start | bytes 4718596
  43.0 1.4 %copy-start.2 = (bf16[1,2048,384]{2,1,0:T(8,128)(2,1)S(1)}, bf16[1,2048,384]{2,1,0:T(8,128)(2,1)}, u32[]{:S(2)}) copy-start(bf16[1,2048,384]{2,1,0:T(8,128)(2,1)} %refs_4_.1) | copy-start | bytes 4718596
  44.4 1.4 %copy-start.4 = (bf16[1,384,2048]{2,1,0:T(8,128)(2,1)S(1)}, bf16[1,384,2048]{2,1,0:T(8,128)(2,1)}, u32[]{:S(2)}) copy-start(bf16[1,384,2048]{2,1,0:T(8,128)(2,1)} %refs_6_.3) | copy-start | bytes 4718596
  46.8 10.9 %copy-start.1 = (bf16[1,2048,384]{2,1,0:T(8,128)(2,1)S(1)}, bf16[1,2048,384]{2,1,0:T(8,128)(2,1)}, u32[]{:S(2)}) copy-start(bf16[1,2048,384]{2,1,0:T(8,128)(2,1)} %refs_2_.1) | copy-start | bytes 4718596
  46.8 10.9 %copy-start.3 = (bf16[1,2048,384]{2,1,0:T(8,128)(2,1)S(1)}, bf16[1,2048,384]{2,1,0:T(8,128)(2,1)}, u32[]{:S(2)}) copy-start(bf16[1,2048,384]{2,1,0:T(8,128)(2,1)} %refs_4_.1) | copy-start | bytes 4718596
  46.8 10.9 %copy-start.5 = (bf16[1,384,2048]{2,1,0:T(8,128)(2,1)S(1)}, bf16[1,384,2048]{2,1,0:T(8,128)(2,1)}, u32[]{:S(2)}) copy-start(bf16[1,384,2048]{2,1,0:T(8,128)(2,1)} %refs_6_.3) | copy-start | bytes 4718596
  46.8 10.9 %copy-start.12 = (bf16[64,2176]{1,0:T(8,128)(2,1)S(1)}, bf16[64,2176]{1,0:T(8,128)(2,1)}, u32[]{:S(2)}) copy-start(bf16[64,2176]{1,0:T(8,128)(2,1)} %pack_tokens.1.refs_0_) | copy-start | bytes 835588
  56.6 14.1 %collective-permute-start.13 = (bf16[32,2176]{1,0:T(8,128)(2,1)S(1)}, bf16[32,2176]{1,0:T(8,128)(2,1)S(1)}, u32[]{:S(2)}, u32[]{:S(2)}) collective-permute-start(bf16[32,2176]{1,0:T(8,128)(2,1)S(1)} %get-tuple-element.21), channel_id=1, source_target_pairs={{0,2},{2,0},{1,3},{3,1},{4,6},{6,4},{5,7},{7,5},{8,10},{10,8},{9,1... | collective-permute-start | bytes 417800 | tf_op jit(solution)/shard_map/ppermute | solution.py:238
  57.6 1.4 %copy-start.7 = (bf16[1,2048,384]{2,1,0:T(8,128)(2,1)S(1)}, bf16[1,2048,384]{2,1,0:T(8,128)(2,1)}, u32[]{:S(2)}) copy-start(bf16[1,2048,384]{2,1,0:T(8,128)(2,1)} %copy-done.6) | copy-start | bytes 4718596
  69.2 11.0 %copy-start.8 = (bf16[192,1152]{1,0:T(8,128)(2,1)}, bf16[192,1152]{1,0:T(8,128)(2,1)S(1)}, u32[]{:S(2)}) copy-start(bf16[192,1152]{1,0:T(8,128)(2,1)S(1)} %get-tuple-element.24.refs_8_) | copy-start | bytes 1327108
  69.2 10.8 %collective-permute-start.8 = (bf16[96,2176]{1,0:T(8,128)(2,1)S(1)}, bf16[96,2176]{1,0:T(8,128)(2,1)S(1)}, u32[]{:S(2)}, u32[]{:S(2)}) collective-permute-start(bf16[96,2176]{1,0:T(8,128)(2,1)S(1)} %get-tuple-element.19), channel_id=1, source_target_pairs={{0,2},{2,0},{1,3},{3,1},{4,6},{6,4},{5,7},{7,5},{8,10},{10,8},{9,1... | collective-permute-start | bytes 1253384 | tf_op jit(solution)/shard_map/ppermute | solution.py:238
  70.7 18.5 %collective-permute-start.15 = (bf16[384,2048]{1,0:T(8,128)(2,1)S(1)}, bf16[384,2048]{1,0:T(8,128)(2,1)S(1)}, u32[]{:S(2)}, u32[]{:S(2)}) collective-permute-start(bf16[384,2048]{1,0:T(8,128)(2,1)S(1)} %get-tuple-element.22.refs_0_.refs_4_), channel_id=1, source_target_pairs={{0,1},{1,0},{2,3},{3,2},{4,5},{5,4},{6,7},{7,6},{8,9},{9,8},{10,11... | collective-permute-start | bytes 4718600 | tf_op jit(solution)/shard_map/ppermute | solution.py:238
  70.7 11.2 %collective-permute-start.14 = (bf16[32,2176]{1,0:T(8,128)(2,1)S(1)}, bf16[32,2176]{1,0:T(8,128)(2,1)S(1)}, u32[]{:S(2)}, u32[]{:S(2)}) collective-permute-start(bf16[32,2176]{1,0:T(8,128)(2,1)S(1)} %add_convert_fusion), channel_id=1, source_target_pairs={{0,12},{4,8},{8,4},{12,0},{1,13},{5,9},{9,5},{13,1},{2,14},{6,10},... | collective-permute-start | bytes 417800 | tf_op jit(solution)/shard_map/ppermute | solution.py:242
  80.0 8.5 %copy-start.15 = (s32[32,8]{0,1:T(8,128)S(1)}, s32[32,8]{0,1:T(8,128)}, u32[]{:S(2)}) copy-start(s32[32,8]{0,1:T(8,128)} %param.9) | copy-start | bytes 3076
  80.1 9.0 %copy-start.14 = (bf16[64,1152]{1,0:T(8,128)(2,1)S(1)}, bf16[64,1152]{1,0:T(8,128)(2,1)}, u32[]{:S(2)}) copy-start(bf16[64,1152]{1,0:T(8,128)(2,1)} %copy-done.13) | copy-start | bytes 442372
  80.2 6.5 %collective-permute-start.10 = (bf16[32,2176]{1,0:T(8,128)(2,1)S(1)}, bf16[32,2176]{1,0:T(8,128)(2,1)S(1)}, u32[]{:S(2)}, u32[]{:S(2)}) collective-permute-start(bf16[32,2176]{1,0:T(8,128)(2,1)S(1)} %get-tuple-element.34), channel_id=1, source_target_pairs={{0,8},{4,12},{8,0},{12,4},{1,9},{5,13},{9,1},{13,5},{2,10},{6,14},... | collective-permute-start | bytes 417800 | tf_op jit(solution)/shard_map/ppermute | solution.py:242
  81.0 6.6 %collective-permute-start.9 = (bf16[32,2176]{1,0:T(8,128)(2,1)S(1)}, bf16[32,2176]{1,0:T(8,128)(2,1)S(1)}, u32[]{:S(2)}, u32[]{:S(2)}) collective-permute-start(bf16[32,2176]{1,0:T(8,128)(2,1)S(1)} %get-tuple-element.33), channel_id=1, source_target_pairs={{0,4},{4,0},{8,12},{12,8},{1,5},{5,1},{9,13},{13,9},{2,6},{6,2},{1... | collective-permute-start | bytes 417800 | tf_op jit(solution)/shard_map/ppermute | solution.py:242
  81.9 7.2 %collective-permute-start.16 = (bf16[128,2048]{1,0:T(8,128)(2,1)}, bf16[128,2048]{1,0:T(8,128)(2,1)}, u32[]{:S(2)}, u32[]{:S(2)}) collective-permute-start(bf16[128,2048]{1,0:T(8,128)(2,1)} %get-tuple-element.23.refs_2_.refs_6_), channel_id=1, source_target_pairs={{0,1},{1,0},{2,3},{3,2},{4,5},{5,4},{6,7},{7,6},{8,9},{9,8},{10,11... | collective-permute-start | bytes 1572872 | tf_op jit(solution)/shard_map/ppermute | solution.py:238
  81.9 7.2 %collective-permute-start.17 = (bf16[192,1152]{1,0:T(8,128)(2,1)}, bf16[192,1152]{1,0:T(8,128)(2,1)}, u32[]{:S(2)}, u32[]{:S(2)}) collective-permute-start(bf16[192,1152]{1,0:T(8,128)(2,1)} %get-tuple-element.25), channel_id=1, source_target_pairs={{0,1},{1,0},{2,3},{3,2},{4,5},{5,4},{6,7},{7,6},{8,9},{9,8},{10,11... | collective-permute-start | bytes 1327112 | tf_op jit(solution)/shard_map/ppermute | solution.py:238
  86.7 2.4 %collective-permute-start.18 = (bf16[64,1152]{1,0:T(8,128)(2,1)}, bf16[64,1152]{1,0:T(8,128)(2,1)S(1)}, u32[]{:S(2)}, u32[]{:S(2)}) collective-permute-start(bf16[64,1152]{1,0:T(8,128)(2,1)} %get-tuple-element.27), channel_id=1, source_target_pairs={{0,1},{1,0},{2,3},{3,2},{4,5},{5,4},{6,7},{7,6},{8,9},{9,8},{10,11... | collective-permute-start | bytes 442376 | tf_op jit(solution)/shard_map/ppermute | solution.py:238
  89.2 1.0 %copy-start.9 = (bf16[192,1152]{1,0:T(8,128)(2,1)S(1)}, bf16[192,1152]{1,0:T(8,128)(2,1)}, u32[]{:S(2)}) copy-start(bf16[192,1152]{1,0:T(8,128)(2,1)} %copy-done.8) | copy-start | bytes 1327108
  (3 other events, 2.3 us)

commit v2 on v0

--- a/solution.py
+++ b/solution.py
@@ -1,7 +1,348 @@
+import functools
+
 import jax
 import jax.numpy as jnp
 from jax import lax
+from jax.experimental import pallas as pl
+from jax.experimental.pallas import tpu as pltpu
 from jax.sharding import PartitionSpec as P
+
+F32 = jnp.float32
+BF16 = jnp.bfloat16
+SIDE = 128
+NT = (((1,), (1,)), ((), ()))
+TN = (((0,), (0,)), ((), ()))
+MIB = 1024 * 1024
+
+
+def split_columns(values, count, lane):
+    high = values.astype(BF16)
+    low = (values - high.astype(F32)).astype(BF16)
+    zero = jnp.zeros_like(high)
+    return jnp.where(lane < count, high, jnp.where(lane < 2 * count, low, zero))
+
+
+def in_vmem(count):
+    return [pl.BlockSpec(memory_space=pltpu.VMEM)] * count
+
+
+def in_hbm(count):
+    return [pl.BlockSpec(memory_space=pl.ANY)] * count
+
+
+def held(*arrays):
+    return [pltpu.with_memory_space_constraint(array, pltpu.VMEM) for array in arrays]
+
+
+def left(*arrays):
+    return [pltpu.with_memory_space_constraint(array, pltpu.HBM) for array in arrays]
+
+
+def pack_kernel(x_ref, e_ref, routes_ref, weight_ref, out_ref, routes_held, weight_held, sems):
+    tok_count, width = x_ref.shape
+    top_count = routes_ref.shape[0]
+    copies = [
+        pltpu.make_async_copy(routes_ref, routes_held, sems.at[0]),
+        pltpu.make_async_copy(weight_ref, weight_held, sems.at[1]),
+        pltpu.make_async_copy(x_ref, out_ref.at[pl.ds(0, tok_count), pl.ds(0, width)], sems.at[2]),
+        pltpu.make_async_copy(e_ref, out_ref.at[pl.ds(tok_count, tok_count), pl.ds(0, width)], sems.at[3]),
+    ]
+    for copy in copies:
+        copy.start()
+    out_ref[tok_count:, width:] = jnp.zeros((tok_count, SIDE), BF16)
+    lane = lax.broadcasted_iota(jnp.int32, (tok_count, SIDE), 1)
+    expert = lax.rem(lax.broadcasted_iota(jnp.int32, (SIDE, tok_count), 0), top_count)
+    copies[0].wait()
+    copies[1].wait()
+    routes = routes_held[...]
+    weight = weight_held[...]
+    table = jnp.zeros((SIDE, tok_count), F32)
+    for k in range(top_count):
+        table += jnp.where(routes[k : k + 1, :] == expert, weight[k : k + 1, :], 0.0)
+    out_ref[:tok_count, width:] = split_columns(table.T, top_count, lane)
+    copies[2].wait()
+    copies[3].wait()
+
+
+def pack(x, e, routes, weight):
+    tok_count, width = x.shape
+    top_count = routes.shape[1]
+    return pl.pallas_call(
+        pack_kernel,
+        in_specs=in_hbm(4),
+        out_specs=in_vmem(1)[0],
+        out_shape=pltpu.VMEM((2 * tok_count, width + SIDE), BF16),
+        scratch_shapes=[
+            pltpu.VMEM((top_count, tok_count), jnp.int32),
+            pltpu.VMEM((top_count, tok_count), F32),
+            pltpu.SemaphoreType.DMA((4,)),
+        ],
+        compiler_params=pltpu.CompilerParams(vmem_limit_bytes=4 * MIB),
+        name="pack_tokens",
+    )(*left(x, e, routes.T, weight.T))
+
+
+def stage_kernel(gate_ref, up_ref, wide_ref, sems):
+    _, width, hidden = gate_ref.shape
+    pieces = sems.shape[1]
+    block = width // pieces
+    copies = []
+    for i in range(pieces):
+        here = pl.ds(i * block, block)
+        copies += [
+            pltpu.make_async_copy(gate_ref.at[0, here], wide_ref.at[here, pl.ds(0, hidden)], sems.at[0, i]),
+            pltpu.make_async_copy(up_ref.at[0, here], wide_ref.at[here, pl.ds(hidden, hidden)], sems.at[1, i]),
+        ]
+    for copy in copies:
+        copy.start()
+    for copy in copies:
+        copy.wait()
+
+
+def stage(gate_w, up_w):
+    _, width, hidden = gate_w.shape
+    return pl.pallas_call(
+        stage_kernel,
+        in_specs=in_hbm(2),
+        out_specs=in_vmem(1)[0],
+        out_shape=pltpu.VMEM((width, 2 * hidden), BF16),
+        scratch_shapes=[pltpu.SemaphoreType.DMA((2, 4))],
+        compiler_params=pltpu.CompilerParams(vmem_limit_bytes=8 * MIB),
+        cost_estimate=pl.CostEstimate(flops=1, bytes_accessed=1, transcendentals=0),
+        name="stage_weights",
+    )(*left(gate_w, up_w))
+
+
+def rows_kernel(shards, expert_ref, *refs):
+    shard_refs = refs[:shards]
+    wide_ref, down_ref, keep_ref, send_ref, xe_ref, diff_ref, tall_ref, table_ref, sems = refs[shards:]
+    tok_count = shard_refs[0].shape[0] // 2
+    rows = shards * tok_count
+    half = rows // 2
+    hidden, width = tall_ref.shape
+    experts = expert_ref[1]
+    x_copies, e_copies = [], []
+    for i, ref in enumerate(shard_refs):
+        here = pl.ds(i * tok_count, tok_count)
+        x_copies.append((ref.at[pl.ds(0, tok_count), pl.ds(0, width)], xe_ref.at[here]))
+        e_copies.append(
+            (ref.at[pl.ds(tok_count, tok_count), pl.ds(0, width)], xe_ref.at[pl.ds(rows + i * tok_count, tok_count)])
+        )
+        e_copies.append((ref.at[pl.ds(0, tok_count), pl.ds(width, SIDE)], table_ref.at[here]))
+    e_copies.append((down_ref.at[0], tall_ref))
+    copies = [pltpu.make_async_copy(src, dst, sems.at[i]) for i, (src, dst) in enumerate(x_copies + e_copies)]
+    for copy in copies:
+        copy.start()
+    lane = lax.broadcasted_iota(jnp.int32, (rows, SIDE), 1)
+    wanted = (lane == expert_ref[0]) | (lane == expert_ref[0] + experts)
+    for copy in copies[:shards]:
+        copy.wait()
+    pre = jnp.dot(xe_ref[:rows, :], wide_ref[...], preferred_element_type=F32)
+    for copy in copies[shards:]:
+        copy.wait()
+    weight = jnp.sum(jnp.where(wanted, table_ref[...].astype(F32), 0.0), axis=1, keepdims=True)
+    back = lax.dot_general(xe_ref[rows:, :], tall_ref[...], NT, preferred_element_type=F32)
+    pre_gate, pre_up = pre[:, :hidden], pre[:, hidden:]
+    sig = jax.nn.sigmoid(pre_gate)
+    silu = pre_gate * sig
+    act = silu * pre_up
+    product = jnp.sum(act * back, axis=1, keepdims=True)
+    back = back * weight
+    diff_gate = (back * pre_up * (sig * (1.0 + pre_gate * (1.0 - sig)))).astype(BF16)
+    diff_up = (back * silu).astype(BF16)
+    diff = jnp.concatenate([diff_gate, diff_up], axis=1)
+    diff_ref[:, : 2 * hidden] = diff
+    diff_ref[:, 2 * hidden :] = (act * weight).astype(BF16)
+    block = 512
+    for c in range(0, width, block):
+        part = lax.dot_general(diff, wide_ref[c : c + block, :], NT, preferred_element_type=F32)
+        keep_ref[:, c : c + block] = part[:half]
+        send_ref[:, c : c + block] = part[half:].astype(BF16)
+    place = lax.rem(lane, experts) == expert_ref[0]
+    side = split_columns(jnp.where(place, product, 0.0), experts, lane)
+    keep_ref[:, width:] = side[:half].astype(F32)
+    send_ref[:, width:] = side[half:]
+
+
+def expert_rows_chunk(name, shards, expert_info, weights):
+    count = len(shards)
+    tok_count = shards[0].shape[0] // 2
+    wide = shards[0].shape[1]
+    width = wide - SIDE
+    rows = count * tok_count
+    hidden = weights[1].shape[1]
+    return pl.pallas_call(
+        functools.partial(rows_kernel, count),
+        in_specs=[pl.BlockSpec(memory_space=pltpu.SMEM)] + in_hbm(count) + in_vmem(1) + in_hbm(1),
+        out_specs=in_vmem(4),
+        out_shape=[
+            pltpu.VMEM((rows // 2, wide), F32),
+            pltpu.VMEM((rows // 2, wide), BF16),
+            pltpu.VMEM((2 * rows, width), BF16),
+            pltpu.VMEM((rows, 3 * hidden), BF16),
+        ],
+        scratch_shapes=[
+            pltpu.VMEM((hidden, width), BF16),
+            pltpu.VMEM((rows, SIDE), BF16),
+            pltpu.SemaphoreType.DMA((3 * count + 1,)),
+        ],
+        compiler_params=pltpu.CompilerParams(vmem_limit_bytes=16 * MIB),
+        cost_estimate=pl.CostEstimate(flops=1, bytes_accessed=1, transcendentals=0),
+        name=name,
+    )(expert_info, *(left(*shards) if count > 4 else shards), weights[0], *left(weights[1]))
+
+
+def grads_kernel(parts, first, *refs):
+    xe_refs = refs[:parts]
+    diff_refs = refs[parts : 2 * parts]
+    gate_out, up_out, down_out, x_ref, e_ref, both_ref, down_ref, in_sems, out_sems = refs[-9:]
+    hidden = gate_out.shape[2]
+    span = x_ref.shape[1]
+    block = span // in_sems.shape[0]
+    arriving = []
+    for i, c in enumerate(range(0, span, block)):
+        copies = []
+        start = 0
+        for j, ref in enumerate(xe_refs):
+            rows = ref.shape[0] // 2
+            for k, dst in enumerate((x_ref, e_ref)):
+                copies.append(
+                    pltpu.make_async_copy(
+                        ref.at[pl.ds(k * rows, rows), pl.ds(first + c, block)],
+                        dst.at[pl.ds(start, rows), pl.ds(c, block)],
+                        in_sems.at[i, 2 * j + k],
+                    )
+                )
+            start += rows
+        for copy in copies:
+            copy.start()
+        arriving.append(copies)
+    diffs = jnp.concatenate([ref[:, : 2 * hidden] for ref in diff_refs], axis=0)
+    hidden_t = jnp.concatenate([ref[:, 2 * hidden :] for ref in diff_refs], axis=0).T
+    leaving = []
+    for i, c in enumerate(range(0, span, block)):
+        for copy in arriving[i]:
+            copy.wait()
+        here, there = pl.ds(c, block), pl.ds(first + c, block)
+        both_ref[c : c + block, :] = lax.dot_general(
+            x_ref[:, c : c + block], diffs, TN, preferred_element_type=F32
+        ).astype(BF16)
+        down_ref[:, c : c + block] = jnp.dot(
+            hidden_t, e_ref[:, c : c + block], preferred_element_type=F32
+        ).astype(BF16)
+        copies = [
+            pltpu.make_async_copy(both_ref.at[here, pl.ds(0, hidden)], gate_out.at[0, there], out_sems.at[i, 0]),
+            pltpu.make_async_copy(both_ref.at[here, pl.ds(hidden, hidden)], up_out.at[0, there], out_sems.at[i, 1]),
+            pltpu.make_async_copy(down_ref.at[:, here], down_out.at[0, :, there], out_sems.at[i, 2]),
+        ]
+        for copy in copies:
+            copy.start()
+        leaving += copies
+    for copy in leaving:
+        copy.wait()
+
+
+def weight_grads(name, first, span, xe_parts, diff_parts, grads):
+    count = len(xe_parts)
+    width = xe_parts[0].shape[1]
+    hidden = diff_parts[0].shape[1] // 3
+    total = sum(part.shape[0] for part in diff_parts)
+    blocks = span // 256
+    return pl.pallas_call(
+        functools.partial(grads_kernel, count, first),
+        in_specs=in_hbm(count) + in_vmem(count) + in_hbm(len(grads)),
+        out_specs=in_hbm(3),
+        out_shape=[
+            jax.ShapeDtypeStruct((1, width, hidden), BF16),
+            jax.ShapeDtypeStruct((1, width, hidden), BF16),
+            jax.ShapeDtypeStruct((1, hidden, width), BF16),
+        ],
+        input_output_aliases={2 * count + i: i for i in range(len(grads))},
+        scratch_shapes=[
+            pltpu.VMEM((total, span), BF16),
+            pltpu.VMEM((total, span), BF16),
+            pltpu.VMEM((span, 2 * hidden), BF16),
+            pltpu.VMEM((hidden, span), BF16),
+            pltpu.SemaphoreType.DMA((blocks, 2 * count)),
+            pltpu.SemaphoreType.DMA((blocks, 3)),
+        ],
+        compiler_params=pltpu.CompilerParams(vmem_limit_bytes=16 * MIB),
+        cost_estimate=pl.CostEstimate(
+            flops=6 * total * span * hidden, bytes_accessed=4 * total * span + 6 * span * hidden, transcendentals=0
+        ),
+        name=name,
+    )(*xe_parts, *diff_parts, *grads)
+
+
+def swap(value, axis):
+    return lax.ppermute(value, axis, [(0, 1), (1, 0)])
+
+
+def far(value, axis, distance):
+    return lax.ppermute(value, axis, [(i, i ^ distance) for i in range(lax.axis_size(axis))])
+
+
+def together(*values):
+    return lax.optimization_barrier(values)
+
+
+def every_token_to_every_expert(
+    layer_input, output_grad, routes, routing_weight, gate_proj, up_proj, down_proj
+):
+    tok_count, width = layer_input.shape
+    top_count = routes.shape[1]
+    lines = lax.axis_size("expert")
+    expert = lax.axis_index("expert") * lax.axis_size("dp") + lax.axis_index("dp")
+    expert_info = jnp.stack([expert, jnp.int32(top_count)]).astype(jnp.int32)
+    packed = pack(layer_input, output_grad, routes, routing_weight)
+    columns, across = {}, {}
+    gate_w, up_w, packed = together(gate_proj, up_proj, packed)
+    columns[1] = far(packed, "expert", 1)
+    columns[2] = far(packed, "expert", 2)
+    across[0] = swap(packed, "dp")
+    wide_w = stage(gate_w, up_w)
+    columns[0], columns[1], columns[2], across[0], wide_w = together(packed, columns[1], columns[2], across[0], wide_w)
+    columns[3] = far(columns[0], "expert", 3)
+    across[2] = swap(columns[2], "dp")
+    across[1] = swap(columns[1], "dp")
+    columns[3], across[1], across[2] = together(columns[3], across[1], across[2])
+    across[3] = swap(columns[3], "dp")
+    weights = (wide_w, down_proj)
+
+    chunk = (2, 1, 0)
+    shards = [columns[k] for k in chunk] + [across[k] for k in chunk]
+    shards += [swap(shard, "sub") for shard in shards]
+    keep, send, xe_0, diff_0 = expert_rows_chunk("rows_0", shards, expert_info, weights)
+    diff_0, columns[3], across[3] = together(diff_0, columns[3], across[3])
+    send, across[3] = together(send, across[3])
+    paired = keep + swap(send, "sub").astype(F32)
+    size = len(chunk) * tok_count
+    own_0 = paired[2 * tok_count : size]
+    away_0 = paired[size + 2 * tok_count :].astype(BF16)
+    home_21 = paired[: 2 * tok_count] + swap(paired[size : size + 2 * tok_count].astype(BF16), "dp").astype(F32)
+
+    shards = [columns[3], across[3]]
+    shards += [swap(shard, "sub") for shard in shards]
+    keep, send, xe_3, diff_3 = expert_rows_chunk("rows_3", shards, expert_info, weights)
+    send, home_21 = together(send, home_21)
+    back_2 = far(home_21[:tok_count].astype(BF16), "expert", 2)
+    paired = keep + swap(send, "sub").astype(F32)
+    home_3 = paired[:tok_count] + swap(paired[tok_count:].astype(BF16), "dp").astype(F32)
+    home_3, away_0 = together(home_3, away_0)
+    own_sum = own_0 + swap(away_0, "dp").astype(F32)
+    back_3 = far(home_3.astype(BF16), "expert", 3)
+    back_1 = far(home_21[tok_count:].astype(BF16), "expert", 1)
+    gate_grads, up_grads, down_grads = weight_grads("grads", 0, width, (xe_0, xe_3), (diff_0, diff_3), ())
+    gate_grads, back_1, back_2, back_3 = together(gate_grads, back_1, back_2, back_3)
+    arrived = (back_1, back_2, back_3)
+    total = own_sum
+    for block in arrived:
+        total = total + block.astype(F32)
+    input_grad = total[:, :width].astype(BF16)
+    products = total[:, width : width + top_count] + total[:, width + top_count : width + 2 * top_count]
+    chosen = routes[:, :, None] == jnp.arange(top_count, dtype=jnp.int32)[None, None, :]
+    routing_grad = jnp.sum(jnp.where(chosen, products[:, None, :], 0.0), axis=2)
+    return (input_grad, routing_grad, gate_grads, up_grads, down_grads)
 
 
 def expert_rows(inputs, gate_w, up_w, down_w):
@@ -37,7 +378,7 @@
     )
 
 
-def per_device(layer_input, output_grad, routes, routing_weight, gate_proj, up_proj, down_proj):
+def chosen_experts(layer_input, output_grad, routes, routing_weight, gate_proj, up_proj, down_proj):
     tok_count, model_width = layer_input.shape
     top_count = routes.shape[1]
     positions = lax.axis_size(("expert", "dp"))
@@ -121,6 +462,15 @@
     return (input_grad, routing_grad, gate_grads, up_grads, down_grads)
 
 
+def per_device(layer_input, output_grad, routes, routing_weight, gate_proj, up_proj, down_proj):
+    args = (layer_input, output_grad, routes, routing_weight, gate_proj, up_proj, down_proj)
+    lines = lax.axis_size("expert")
+    pairs = lax.axis_size("dp") == 2 and lax.axis_size("sub") == 2 and lines & (lines - 1) == 0
+    if pairs and lines == 4 and 2 * lines == routes.shape[1] and gate_proj.shape[0] == 1:
+        return every_token_to_every_expert(*args)
+    return chosen_experts(*args)
+
+
 def solution(mesh):
     placed = (
         P(("group", "expert", "dp", "sub"), None),

time: 287 us -> 74.4 us (0.26)
  waiting for transfers between devices: 184 us -> 27.3 us
  matrix products: 27.7 us -> 0 us
  Pallas kernels: 0 us -> 21.3 us
  local copies, waits for them, and re-layouts: 18.7 us -> 0.83 us
  blocking collectives: 15.1 us -> 0 us
  between operations: 14.3 us -> 0.81 us
  other arithmetic: 6.49 us -> 1.15 us
  starting transfers between devices: 19 us -> 22.8 us
    all_to_all x4 -> x0, waiting for transfers between devices: 159 us -> none  [the longest x1 78.7 us: per_device(): lax.all_to_all(row_part, ('expert', 'dp'), split_axis=0, concat_axis=0, t...]
    dot_general x8 -> x0, matrix products: 27.7 us -> none  [the longest x1 4.48 us: expert_rows(): pre_gate = jnp.dot(flat_x, gate_w, preferred_element_type=jnp.float32)]
    ppermute x0 -> x23, waiting for transfers between devices: none -> 27.3 us  [the longest x17 14.7 us: swap(): return lax.ppermute(value, axis, [(0, 1), (1, 0)])]
    all_gather x2 -> x0, waiting for transfers between devices: 25.6 us -> none  [the longest x1 13.4 us: per_device(): lax.all_gather(send_x, 'sub', axis=1, tiled=True)]
    ppermute x0 -> x23, starting transfers between devices: none -> 22.8 us  [the longest x6 11.7 us: far(): lax.ppermute(value, axis, [(i, i ^ distance) for i in range(lax.axis_size...]
    pallas_call x0 -> x5, Pallas kernels: none -> 21.3 us  [the longest x2 11.2 us: expert_rows_chunk(): pl.pallas_call(functools.partial(rows_kernel, count), in_specs=[pl.BlockS...]
    all_to_all x4 -> x0, starting transfers between devices: 18.9 us -> none  [the longest x1 5.77 us: per_device(): lax.all_to_all(paired[0], ('expert', 'dp'), split_axis=0, concat_axis=0,...]
    unnamed x1 -> x0, blocking collectives: 15.1 us -> none
  transfers between devices with their start and end apart: 6 -> 23, of which waited for: 6 -> 11; matrix products, arithmetic and copies ran while one was open for 8% -> 0% of each run, Pallas kernels for 0% -> 27%
where the time goes in v2:
time: 74.4 us; the launch traced here: 74.2 us
  waiting for transfers between devices  27.3 us (37%)
  starting transfers between devices  22.8 us (31%)
  Pallas kernels  21.3 us (29%)
  other arithmetic  1.15 us (2%)
  local copies, waits for them, and re-layouts  0.83 us (1%)
  between operations  0.81 us (1%)
    ppermute x17, waiting for transfers between devices, swap(): return lax.ppermute(value, axis, [(0, 1), (1, 0)])  14.7 us
    ppermute x6, waiting for transfers between devices, far(): lax.ppermute(value, axis, [(i, i ^ distance) for i in range(lax.axis_size...  12.6 us
    ppermute x6, starting transfers between devices, far(): lax.ppermute(value, axis, [(i, i ^ distance) for i in range(lax.axis_size...  11.7 us
    pallas_call x2, Pallas kernels, expert_rows_chunk(): pl.pallas_call(functools.partial(rows_kernel, count), in_specs=[pl.BlockS...  11.2 us
    ppermute x17, starting transfers between devices, swap(): return lax.ppermute(value, axis, [(0, 1), (1, 0)])  11.1 us
    pallas_call x1, Pallas kernels, weight_grads(): pl.pallas_call(functools.partial(grads_kernel, count, first), in_specs=in...  7.18 us
    pallas_call x1, Pallas kernels, stage(): pl.pallas_call(stage_kernel, in_specs=in_hbm(2), out_specs=in_vmem(1)[0],...  1.89 us
  transfers between devices with their start and end apart: 23, of which 11 were waited for; matrix products, arithmetic and copies ran while one was open for 0% of the time, Pallas kernels for 27%

profile of v2, /device:TPU:0, one launch (start us, length us, event | category | flops | bytes accessed | tf_op | source)
XLA Modules:
  0.0 74.2 jit_solution(10823602829349931951)
XLA Ops:
  0.6 1.0 %pack_tokens.1.refs_2_ = bf16[64,2176]{1,0:T(8,128)(2,1)S(1)} custom-call(bf16[32,2048]{1,0:T(8,128)(2,1)} %x_ref.1, bf16[32,2048]{1,0:T(8,128)(2,1)} %e_ref.1, s32[8,32]{1,0:T(8,128)} %bitcast.3, f32[8,32]{1,0:T(8,128)} %bitcast.4), custom_call_target="tpu_custom_call" | custom-call | tf_op jit(solution)/shard_map/pack_tokens/pallas_call | solution.py:70
  1.7 3.1 %collective-permute-start = (bf16[64,2176]{1,0:T(8,128)(2,1)S(1)}, bf16[64,2176]{1,0:T(8,128)(2,1)S(1)}, u32[]{:S(2)}, u32[]{:S(2)}) collective-permute-start(bf16[64,2176]{1,0:T(8,128)(2,1)S(1)} %pack_tokens.1.refs_2_), channel_id=1, source_target_pairs={{0,4},{4,0},{8,12},{12,8},{1,5},{5,1},{9,13},{13,9},{2,6},{6,2},{1... | collective-permute-start | bytes 835592 | tf_op jit(solution)/shard_map/ppermute | solution.py:282
  4.8 2.6 %collective-permute-start.1 = (bf16[64,2176]{1,0:T(8,128)(2,1)S(1)}, bf16[64,2176]{1,0:T(8,128)(2,1)S(1)}, u32[]{:S(2)}, u32[]{:S(2)}) collective-permute-start(bf16[64,2176]{1,0:T(8,128)(2,1)S(1)} %pack_tokens.1.refs_2_), channel_id=1, source_target_pairs={{0,8},{4,12},{8,0},{12,4},{1,9},{5,13},{9,1},{13,5},{2,10},{6,14},... | collective-permute-start | bytes 835592 | tf_op jit(solution)/shard_map/ppermute | solution.py:282
  7.4 1.5 %collective-permute-start.2 = (bf16[64,2176]{1,0:T(8,128)(2,1)S(1)}, bf16[64,2176]{1,0:T(8,128)(2,1)}, u32[]{:S(2)}, u32[]{:S(2)}) collective-permute-start(bf16[64,2176]{1,0:T(8,128)(2,1)S(1)} %pack_tokens.1.refs_2_), channel_id=1, source_target_pairs={{0,2},{2,0},{1,3},{3,1},{4,6},{6,4},{5,7},{7,5},{8,10},{10,8},{9,1... | collective-permute-start | bytes 835592 | tf_op jit(solution)/shard_map/ppermute | solution.py:278
  8.9 1.9 %stage_weights.1.refs_12_.refs_4_ = bf16[2048,768]{1,0:T(8,128)(2,1)S(1)} custom-call(bf16[1,2048,384]{2,1,0:T(8,128)(2,1)} %gate_ref, bf16[1,2048,384]{2,1,0:T(8,128)(2,1)} %up_ref), custom_call_target="tpu_custom_call" | custom-call | flops 1 | bytes 1 | tf_op jit(solution)/shard_map/stage_weights/pallas_call | solution.py:104
  10.8 6.5 %collective-permute-done.refs_1_ = bf16[64,2176]{1,0:T(8,128)(2,1)S(1)} collective-permute-done((bf16[64,2176]{1,0:T(8,128)(2,1)S(1)}, bf16[64,2176]{1,0:T(8,128)(2,1)S(1)}, u32[]{:S(2)}, u32[]{:S(2)}) %collective-permute-start) | collective-permute-done | bytes 278560 | tf_op jit(solution)/shard_map/ppermute | solution.py:282
  17.3 2.5 %collective-permute-done.1.refs_0_ = bf16[64,2176]{1,0:T(8,128)(2,1)S(1)} collective-permute-done((bf16[64,2176]{1,0:T(8,128)(2,1)S(1)}, bf16[64,2176]{1,0:T(8,128)(2,1)S(1)}, u32[]{:S(2)}, u32[]{:S(2)}) %collective-permute-start.1) | collective-permute-done | bytes 278560 | tf_op jit(solution)/shard_map/ppermute | solution.py:282
  19.8 2.5 %collective-permute-start.3 = (bf16[64,2176]{1,0:T(8,128)(2,1)S(1)}, bf16[64,2176]{1,0:T(8,128)(2,1)}, u32[]{:S(2)}, u32[]{:S(2)}) collective-permute-start(bf16[64,2176]{1,0:T(8,128)(2,1)S(1)} %pack_tokens.1.refs_2_), channel_id=1, source_target_pairs={{0,12},{4,8},{8,4},{12,0},{1,13},{5,9},{9,5},{13,1},{2,14},{6,10},... | collective-permute-start | bytes 835592 | tf_op jit(solution)/shard_map/ppermute | solution.py:282
  22.3 1.5 %collective-permute-start.4 = (bf16[64,2176]{1,0:T(8,128)(2,1)S(1)}, bf16[64,2176]{1,0:T(8,128)(2,1)}, u32[]{:S(2)}, u32[]{:S(2)}) collective-permute-start(bf16[64,2176]{1,0:T(8,128)(2,1)S(1)} %collective-permute-done.refs_1_), channel_id=1, source_target_pairs={{0,2},{2,0},{1,3},{3,1},{4,6},{6,4},{5,7},{7,5},{8,10},{10,8},{9,1... | collective-permute-start | bytes 835592 | tf_op jit(solution)/shard_map/ppermute | solution.py:278
  23.8 0.5 collective-permute-start.5
  24.3 0.5 collective-permute-start.7
  24.8 3.5 %collective-permute-done.3.refs_0_ = bf16[64,2176]{1,0:T(8,128)(2,1)} collective-permute-done((bf16[64,2176]{1,0:T(8,128)(2,1)S(1)}, bf16[64,2176]{1,0:T(8,128)(2,1)}, u32[]{:S(2)}, u32[]{:S(2)}) %collective-permute-start.3) | collective-permute-done | bytes 278560 | tf_op jit(solution)/shard_map/ppermute | solution.py:282
  28.4 2.0 %collective-permute-done.4.refs_4_ = bf16[64,2176]{1,0:T(8,128)(2,1)} collective-permute-done((bf16[64,2176]{1,0:T(8,128)(2,1)S(1)}, bf16[64,2176]{1,0:T(8,128)(2,1)}, u32[]{:S(2)}, u32[]{:S(2)}) %collective-permute-start.4) | collective-permute-done | bytes 278560 | tf_op jit(solution)/shard_map/ppermute | solution.py:278
  30.4 3.0 %collective-permute-done.5.refs_3_ = bf16[64,2176]{1,0:T(8,128)(2,1)} collective-permute-done((bf16[64,2176]{1,0:T(8,128)(2,1)S(1)}, bf16[64,2176]{1,0:T(8,128)(2,1)}, u32[]{:S(2)}, u32[]{:S(2)}) %collective-permute-start.5) | collective-permute-done | bytes 278560 | tf_op jit(solution)/shard_map/ppermute | solution.py:278
  33.4 0.5 collective-permute-start.9
  33.9 1.6 %collective-permute-start.12 = (bf16[64,2176]{1,0:T(8,128)(2,1)}, bf16[64,2176]{1,0:T(8,128)(2,1)}, u32[]{:S(2)}, u32[]{:S(2)}) collective-permute-start(bf16[64,2176]{1,0:T(8,128)(2,1)} %collective-permute-done.3.refs_0_), channel_id=1, source_target_pairs={{0,2},{2,0},{1,3},{3,1},{4,6},{6,4},{5,7},{7,5},{8,10},{10,8},{9,1... | collective-permute-start | bytes 835592 | tf_op jit(solution)/shard_map/ppermute | solution.py:278
  35.6 6.9 %rows_0.1 = (f32[192,2176]{1,0:T(8,128)S(1)}, bf16[192,2176]{1,0:T(8,128)(2,1)S(1)}, bf16[768,2048]{1,0:T(8,128)(2,1)S(1)}, bf16[384,1152]{1,0:T(8,128)(2,1)S(1)}) custom-call(s32[2]{0:T(128)S(1)} %pad_add_fusion.expert_ref, bf16[64,2176]{1,0:T(8,128)(2,1)} %copy-done.2, bf16[64,2176]{1,0:T(8,128)(2,1)} %copy-done.1, bf16[64,2176]{1,0:T(8,128)(2,1)} %copy-done, ...), custom_call_target="tpu_custom_call" | custom-call | flops 1 | bytes 1 | tf_op jit(solution)/shard_map/rows_0/pallas_call | solution.py:174
  42.5 0.3 collective-permute-done.12.refs_1_
  42.9 0.5 collective-permute-start.15
  43.4 2.6 %collective-permute-done.13 = bf16[192,2176]{1,0:T(8,128)(2,1)S(1)} collective-permute-done((bf16[192,2176]{1,0:T(8,128)(2,1)S(1)}, bf16[192,2176]{1,0:T(8,128)(2,1)S(1)}, u32[]{:S(2)}, u32[]{:S(2)}) %collective-permute-start.13) | collective-permute-done | bytes 835616 | tf_op jit(solution)/shard_map/ppermute | solution.py:278
  46.2 1.6 %collective-permute-start.16 = (bf16[64,2176]{1,0:T(8,128)(2,1)S(1)}, bf16[64,2176]{1,0:T(8,128)(2,1)S(1)}, u32[]{:S(2)}, u32[]{:S(2)}) collective-permute-start(bf16[64,2176]{1,0:T(8,128)(2,1)S(1)} %slice.52), channel_id=1, source_target_pairs={{0,2},{2,0},{1,3},{3,1},{4,6},{6,4},{5,7},{7,5},{8,10},{10,8},{9,1... | collective-permute-start | bytes 835592 | tf_op jit(solution)/shard_map/ppermute | solution.py:278
  47.8 4.3 %rows_3.1 = (f32[64,2176]{1,0:T(8,128)S(1)}, bf16[64,2176]{1,0:T(8,128)(2,1)S(1)}, bf16[256,2048]{1,0:T(8,128)(2,1)S(1)}, bf16[128,1152]{1,0:T(8,128)(2,1)S(1)}) custom-call(s32[2]{0:T(128)S(1)} %pad_add_fusion.expert_ref, bf16[64,2176]{1,0:T(8,128)(2,1)} %collective-permute-done.3.refs_0_, bf16[64,2176]{1,0:T(8,128)(2,1)} %collective-permute-done.12.refs_1_, ...), custom_call_target="tpu_custom_call" | custom-call | flops 1 | bytes 1 | tf_op jit(solution)/shard_map/rows_3/pallas_call | solution.py:174
  52.1 2.9 %collective-permute-done.16 = bf16[64,2176]{1,0:T(8,128)(2,1)S(1)} collective-permute-done((bf16[64,2176]{1,0:T(8,128)(2,1)S(1)}, bf16[64,2176]{1,0:T(8,128)(2,1)S(1)}, u32[]{:S(2)}, u32[]{:S(2)}) %collective-permute-start.16) | collective-permute-done | bytes 278560 | tf_op jit(solution)/shard_map/ppermute | solution.py:278
  55.1 1.5 %collective-permute-done.17 = bf16[64,2176]{1,0:T(8,128)(2,1)S(1)} collective-permute-done((bf16[64,2176]{1,0:T(8,128)(2,1)S(1)}, bf16[64,2176]{1,0:T(8,128)(2,1)S(1)}, u32[]{:S(2)}, u32[]{:S(2)}) %collective-permute-start.17) | collective-permute-done | bytes 278560 | tf_op jit(solution)/shard_map/ppermute | solution.py:278
  56.7 1.6 %collective-permute-start.18 = (bf16[32,2176]{1,0:T(8,128)(2,1)S(1)}, bf16[32,2176]{1,0:T(8,128)(2,1)S(1)}, u32[]{:S(2)}, u32[]{:S(2)}) collective-permute-start(bf16[32,2176]{1,0:T(8,128)(2,1)S(1)} %slice.74), channel_id=1, source_target_pairs={{0,2},{2,0},{1,3},{3,1},{4,6},{6,4},{5,7},{7,5},{8,10},{10,8},{9,1... | collective-permute-start | bytes 417800 | tf_op jit(solution)/shard_map/ppermute | solution.py:278
  58.4 1.9 %collective-permute-start.21 = (bf16[32,2176]{1,0:T(8,128)(2,1)S(1)}, bf16[32,2176]{1,0:T(8,128)(2,1)S(1)}, u32[]{:S(2)}, u32[]{:S(2)}) collective-permute-start(bf16[32,2176]{1,0:T(8,128)(2,1)S(1)} %get-tuple-element.77), channel_id=1, source_target_pairs={{0,8},{4,12},{8,0},{12,4},{1,9},{5,13},{9,1},{13,5},{2,10},{6,14},... | collective-permute-start | bytes 417800 | tf_op jit(solution)/shard_map/ppermute | solution.py:282
  60.3 2.2 %collective-permute-done.18 = bf16[32,2176]{1,0:T(8,128)(2,1)S(1)} collective-permute-done((bf16[32,2176]{1,0:T(8,128)(2,1)S(1)}, bf16[32,2176]{1,0:T(8,128)(2,1)S(1)}, u32[]{:S(2)}, u32[]{:S(2)}) %collective-permute-start.18) | collective-permute-done | bytes 139296 | tf_op jit(solution)/shard_map/ppermute | solution.py:278
  62.6 1.6 %collective-permute-start.22 = (bf16[32,2176]{1,0:T(8,128)(2,1)S(1)}, bf16[32,2176]{1,0:T(8,128)(2,1)S(1)}, u32[]{:S(2)}, u32[]{:S(2)}) collective-permute-start(bf16[32,2176]{1,0:T(8,128)(2,1)S(1)} %slice_add_fusion.1), channel_id=1, source_target_pairs={{0,12},{4,8},{8,4},{12,0},{1,13},{5,9},{9,5},{13,1},{2,14},{6,10},... | collective-permute-start | bytes 417800 | tf_op jit(solution)/shard_map/ppermute | solution.py:282
  64.1 1.3 %collective-permute-start.19 = (bf16[32,2176]{1,0:T(8,128)(2,1)S(1)}, bf16[32,2176]{1,0:T(8,128)(2,1)S(1)}, u32[]{:S(2)}, u32[]{:S(2)}) collective-permute-start(bf16[32,2176]{1,0:T(8,128)(2,1)S(1)} %slice.55), channel_id=1, source_target_pairs={{0,2},{2,0},{1,3},{3,1},{4,6},{6,4},{5,7},{7,5},{8,10},{10,8},{9,1... | collective-permute-start | bytes 417800 | tf_op jit(solution)/shard_map/ppermute | solution.py:278
  65.5 7.2 %grads.1 = (bf16[1,2048,384]{2,1,0:T(8,128)(2,1)}, bf16[1,2048,384]{2,1,0:T(8,128)(2,1)}, bf16[1,384,2048]{2,1,0:T(8,128)(2,1)}) custom-call(bf16[768,2048]{1,0:T(8,128)(2,1)S(1)} %get-tuple-element.62.refs_0_, bf16[256,2048]{1,0:T(8,128)(2,1)S(1)} %get-tuple-element.63.refs_1_, bf16[384,1152]{1,0:T(8,128)(2,1)S(1)} %get-tuple-element.64.refs_2_, ...), custom_call_target="tpu_custom_call" | custom-call | flops 2415919104 | bytes 8912896 | tf_op jit(solution)/shard_map/grads/pallas_call | solution.py:251
  72.8 0.7 slice.75
  73.6 0.6 select_reduce_fusion
  (45 shorter events, 1.0 us)
Async XLA Ops:
  1.7 26.7 %copy-start = (bf16[64,2176]{1,0:T(8,128)(2,1)}, bf16[64,2176]{1,0:T(8,128)(2,1)S(1)}, u32[]{:S(2)}) copy-start(bf16[64,2176]{1,0:T(8,128)(2,1)S(1)} %pack_tokens.1.refs_2_) | copy-start | bytes 835588
  1.7 15.6 %collective-permute-start = (bf16[64,2176]{1,0:T(8,128)(2,1)S(1)}, bf16[64,2176]{1,0:T(8,128)(2,1)S(1)}, u32[]{:S(2)}, u32[]{:S(2)}) collective-permute-start(bf16[64,2176]{1,0:T(8,128)(2,1)S(1)} %pack_tokens.1.refs_2_), channel_id=1, source_target_pairs={{0,4},{4,0},{8,12},{12,8},{1,5},{5,1},{9,13},{13,9},{2,6},{6,2},{1... | collective-permute-start | bytes 835592 | tf_op jit(solution)/shard_map/ppermute | solution.py:282
  4.8 15.0 %collective-permute-start.1 = (bf16[64,2176]{1,0:T(8,128)(2,1)S(1)}, bf16[64,2176]{1,0:T(8,128)(2,1)S(1)}, u32[]{:S(2)}, u32[]{:S(2)}) collective-permute-start(bf16[64,2176]{1,0:T(8,128)(2,1)S(1)} %pack_tokens.1.refs_2_), channel_id=1, source_target_pairs={{0,8},{4,12},{8,0},{12,4},{1,9},{5,13},{9,1},{13,5},{2,10},{6,14},... | collective-permute-start | bytes 835592 | tf_op jit(solution)/shard_map/ppermute | solution.py:282
  7.4 12.4 %collective-permute-start.2 = (bf16[64,2176]{1,0:T(8,128)(2,1)S(1)}, bf16[64,2176]{1,0:T(8,128)(2,1)}, u32[]{:S(2)}, u32[]{:S(2)}) collective-permute-start(bf16[64,2176]{1,0:T(8,128)(2,1)S(1)} %pack_tokens.1.refs_2_), channel_id=1, source_target_pairs={{0,2},{2,0},{1,3},{3,1},{4,6},{6,4},{5,7},{7,5},{8,10},{10,8},{9,1... | collective-permute-start | bytes 835592 | tf_op jit(solution)/shard_map/ppermute | solution.py:278
  17.3 11.1 %copy-start.1 = (bf16[64,2176]{1,0:T(8,128)(2,1)}, bf16[64,2176]{1,0:T(8,128)(2,1)S(1)}, u32[]{:S(2)}) copy-start(bf16[64,2176]{1,0:T(8,128)(2,1)S(1)} %collective-permute-done.refs_1_) | copy-start | bytes 835588
  19.8 14.1 %copy-start.2 = (bf16[64,2176]{1,0:T(8,128)(2,1)}, bf16[64,2176]{1,0:T(8,128)(2,1)S(1)}, u32[]{:S(2)}) copy-start(bf16[64,2176]{1,0:T(8,128)(2,1)S(1)} %collective-permute-done.1.refs_0_) | copy-start | bytes 835588
  19.8 8.6 %collective-permute-start.3 = (bf16[64,2176]{1,0:T(8,128)(2,1)S(1)}, bf16[64,2176]{1,0:T(8,128)(2,1)}, u32[]{:S(2)}, u32[]{:S(2)}) collective-permute-start(bf16[64,2176]{1,0:T(8,128)(2,1)S(1)} %pack_tokens.1.refs_2_), channel_id=1, source_target_pairs={{0,12},{4,8},{8,4},{12,0},{1,13},{5,9},{9,5},{13,1},{2,14},{6,10},... | collective-permute-start | bytes 835592 | tf_op jit(solution)/shard_map/ppermute | solution.py:282
  22.3 8.1 %collective-permute-start.4 = (bf16[64,2176]{1,0:T(8,128)(2,1)S(1)}, bf16[64,2176]{1,0:T(8,128)(2,1)}, u32[]{:S(2)}, u32[]{:S(2)}) collective-permute-start(bf16[64,2176]{1,0:T(8,128)(2,1)S(1)} %collective-permute-done.refs_1_), channel_id=1, source_target_pairs={{0,2},{2,0},{1,3},{3,1},{4,6},{6,4},{5,7},{7,5},{8,10},{10,8},{9,1... | collective-permute-start | bytes 835592 | tf_op jit(solution)/shard_map/ppermute | solution.py:278
  23.8 9.6 %collective-permute-start.5 = (bf16[64,2176]{1,0:T(8,128)(2,1)S(1)}, bf16[64,2176]{1,0:T(8,128)(2,1)}, u32[]{:S(2)}, u32[]{:S(2)}) collective-permute-start(bf16[64,2176]{1,0:T(8,128)(2,1)S(1)} %collective-permute-done.1.refs_0_), channel_id=1, source_target_pairs={{0,2},{2,0},{1,3},{3,1},{4,6},{6,4},{5,7},{7,5},{8,10},{10,8},{9,1... | collective-permute-start | bytes 835592 | tf_op jit(solution)/shard_map/ppermute | solution.py:278
  24.3 9.0 %collective-permute-start.6 = (bf16[64,2176]{1,0:T(8,128)(2,1)S(1)}, bf16[64,2176]{1,0:T(8,128)(2,1)S(1)}, u32[]{:S(2)}, u32[]{:S(2)}) collective-permute-start(bf16[64,2176]{1,0:T(8,128)(2,1)S(1)} %collective-permute-done.1.refs_0_), channel_id=1, source_target_pairs={{0,1},{1,0},{2,3},{3,2},{4,5},{5,4},{6,7},{7,6},{8,9},{9,8},{10,11... | collective-permute-start | bytes 835592 | tf_op jit(solution)/shard_map/ppermute | solution.py:278
  24.3 9.5 %collective-permute-start.7 = (bf16[64,2176]{1,0:T(8,128)(2,1)S(1)}, bf16[64,2176]{1,0:T(8,128)(2,1)S(1)}, u32[]{:S(2)}, u32[]{:S(2)}) collective-permute-start(bf16[64,2176]{1,0:T(8,128)(2,1)S(1)} %collective-permute-done.refs_1_), channel_id=1, source_target_pairs={{0,1},{1,0},{2,3},{3,2},{4,5},{5,4},{6,7},{7,6},{8,9},{9,8},{10,11... | collective-permute-start | bytes 835592 | tf_op jit(solution)/shard_map/ppermute | solution.py:278
  28.4 7.1 %collective-permute-start.8 = (bf16[64,2176]{1,0:T(8,128)(2,1)S(1)}, bf16[64,2176]{1,0:T(8,128)(2,1)}, u32[]{:S(2)}, u32[]{:S(2)}) collective-permute-start(bf16[64,2176]{1,0:T(8,128)(2,1)S(1)} %pack_tokens.1.refs_2_), channel_id=1, source_target_pairs={{0,1},{1,0},{2,3},{3,2},{4,5},{5,4},{6,7},{7,6},{8,9},{9,8},{10,11... | collective-permute-start | bytes 835592 | tf_op jit(solution)/shard_map/ppermute | solution.py:278
  30.4 5.1 %collective-permute-start.11 = (bf16[64,2176]{1,0:T(8,128)(2,1)}, bf16[64,2176]{1,0:T(8,128)(2,1)}, u32[]{:S(2)}, u32[]{:S(2)}) collective-permute-start(bf16[64,2176]{1,0:T(8,128)(2,1)} %collective-permute-done.2.refs_5_), channel_id=1, source_target_pairs={{0,1},{1,0},{2,3},{3,2},{4,5},{5,4},{6,7},{7,6},{8,9},{9,8},{10,11... | collective-permute-start | bytes 835592 | tf_op jit(solution)/shard_map/ppermute | solution.py:278
  33.3 2.2 %collective-permute-start.10 = (bf16[64,2176]{1,0:T(8,128)(2,1)}, bf16[64,2176]{1,0:T(8,128)(2,1)}, u32[]{:S(2)}, u32[]{:S(2)}) collective-permute-start(bf16[64,2176]{1,0:T(8,128)(2,1)} %collective-permute-done.4.refs_4_), channel_id=1, source_target_pairs={{0,1},{1,0},{2,3},{3,2},{4,5},{5,4},{6,7},{7,6},{8,9},{9,8},{10,11... | collective-permute-start | bytes 835592 | tf_op jit(solution)/shard_map/ppermute | solution.py:278
  33.3 2.1 %copy-start.3 = (bf16[64,2176]{1,0:T(8,128)(2,1)}, bf16[64,2176]{1,0:T(8,128)(2,1)S(1)}, u32[]{:S(2)}) copy-start(bf16[64,2176]{1,0:T(8,128)(2,1)S(1)} %collective-permute-done.6.refs_6_) | copy-start | bytes 835588
  33.4 2.3 %collective-permute-start.9 = (bf16[64,2176]{1,0:T(8,128)(2,1)}, bf16[64,2176]{1,0:T(8,128)(2,1)}, u32[]{:S(2)}, u32[]{:S(2)}) collective-permute-start(bf16[64,2176]{1,0:T(8,128)(2,1)} %collective-permute-done.5.refs_3_), channel_id=1, source_target_pairs={{0,1},{1,0},{2,3},{3,2},{4,5},{5,4},{6,7},{7,6},{8,9},{9,8},{10,11... | collective-permute-start | bytes 835592 | tf_op jit(solution)/shard_map/ppermute | solution.py:278
  33.9 1.6 %copy-start.4 = (bf16[64,2176]{1,0:T(8,128)(2,1)}, bf16[64,2176]{1,0:T(8,128)(2,1)S(1)}, u32[]{:S(2)}) copy-start(bf16[64,2176]{1,0:T(8,128)(2,1)S(1)} %collective-permute-done.7.refs_7_) | copy-start | bytes 835588
  33.9 9.0 %collective-permute-start.12 = (bf16[64,2176]{1,0:T(8,128)(2,1)}, bf16[64,2176]{1,0:T(8,128)(2,1)}, u32[]{:S(2)}, u32[]{:S(2)}) collective-permute-start(bf16[64,2176]{1,0:T(8,128)(2,1)} %collective-permute-done.3.refs_0_), channel_id=1, source_target_pairs={{0,2},{2,0},{1,3},{3,1},{4,6},{6,4},{5,7},{7,5},{8,10},{10,8},{9,1... | collective-permute-start | bytes 835592 | tf_op jit(solution)/shard_map/ppermute | solution.py:278
  42.9 3.2 %collective-permute-start.13 = (bf16[192,2176]{1,0:T(8,128)(2,1)S(1)}, bf16[192,2176]{1,0:T(8,128)(2,1)S(1)}, u32[]{:S(2)}, u32[]{:S(2)}) collective-permute-start(bf16[192,2176]{1,0:T(8,128)(2,1)S(1)} %get-tuple-element.55), channel_id=1, source_target_pairs={{0,1},{1,0},{2,3},{3,2},{4,5},{5,4},{6,7},{7,6},{8,9},{9,8},{10,11... | collective-permute-start | bytes 2506760 | tf_op jit(solution)/shard_map/ppermute | solution.py:278
  42.9 4.9 %collective-permute-start.15 = (bf16[64,2176]{1,0:T(8,128)(2,1)}, bf16[64,2176]{1,0:T(8,128)(2,1)S(1)}, u32[]{:S(2)}, u32[]{:S(2)}) collective-permute-start(bf16[64,2176]{1,0:T(8,128)(2,1)} %collective-permute-done.12.refs_1_), channel_id=1, source_target_pairs={{0,1},{1,0},{2,3},{3,2},{4,5},{5,4},{6,7},{7,6},{8,9},{9,8},{10,11... | collective-permute-start | bytes 835592 | tf_op jit(solution)/shard_map/ppermute | solution.py:278
  43.4 4.4 %collective-permute-start.14 = (bf16[64,2176]{1,0:T(8,128)(2,1)}, bf16[64,2176]{1,0:T(8,128)(2,1)S(1)}, u32[]{:S(2)}, u32[]{:S(2)}) collective-permute-start(bf16[64,2176]{1,0:T(8,128)(2,1)} %collective-permute-done.3.refs_0_), channel_id=1, source_target_pairs={{0,1},{1,0},{2,3},{3,2},{4,5},{5,4},{6,7},{7,6},{8,9},{9,8},{10,11... | collective-permute-start | bytes 835592 | tf_op jit(solution)/shard_map/ppermute | solution.py:278
  46.2 8.8 %collective-permute-start.16 = (bf16[64,2176]{1,0:T(8,128)(2,1)S(1)}, bf16[64,2176]{1,0:T(8,128)(2,1)S(1)}, u32[]{:S(2)}, u32[]{:S(2)}) collective-permute-start(bf16[64,2176]{1,0:T(8,128)(2,1)S(1)} %slice.52), channel_id=1, source_target_pairs={{0,2},{2,0},{1,3},{3,1},{4,6},{6,4},{5,7},{7,5},{8,10},{10,8},{9,1... | collective-permute-start | bytes 835592 | tf_op jit(solution)/shard_map/ppermute | solution.py:278
  55.0 1.6 %collective-permute-start.17 = (bf16[64,2176]{1,0:T(8,128)(2,1)S(1)}, bf16[64,2176]{1,0:T(8,128)(2,1)S(1)}, u32[]{:S(2)}, u32[]{:S(2)}) collective-permute-start(bf16[64,2176]{1,0:T(8,128)(2,1)S(1)} %get-tuple-element.60), channel_id=1, source_target_pairs={{0,1},{1,0},{2,3},{3,2},{4,5},{5,4},{6,7},{7,6},{8,9},{9,8},{10,11... | collective-permute-start | bytes 835592 | tf_op jit(solution)/shard_map/ppermute | solution.py:278
  56.7 5.8 %collective-permute-start.18 = (bf16[32,2176]{1,0:T(8,128)(2,1)S(1)}, bf16[32,2176]{1,0:T(8,128)(2,1)S(1)}, u32[]{:S(2)}, u32[]{:S(2)}) collective-permute-start(bf16[32,2176]{1,0:T(8,128)(2,1)S(1)} %slice.74), channel_id=1, source_target_pairs={{0,2},{2,0},{1,3},{3,1},{4,6},{6,4},{5,7},{7,5},{8,10},{10,8},{9,1... | collective-permute-start | bytes 417800 | tf_op jit(solution)/shard_map/ppermute | solution.py:278
  58.3 14.3 %collective-permute-start.20 = (bf16[32,2176]{1,0:T(8,128)(2,1)S(1)}, bf16[32,2176]{1,0:T(8,128)(2,1)S(1)}, u32[]{:S(2)}, u32[]{:S(2)}) collective-permute-start(bf16[32,2176]{1,0:T(8,128)(2,1)S(1)} %get-tuple-element.78), channel_id=1, source_target_pairs={{0,4},{4,0},{8,12},{12,8},{1,5},{5,1},{9,13},{13,9},{2,6},{6,2},{1... | collective-permute-start | bytes 417800 | tf_op jit(solution)/shard_map/ppermute | solution.py:282
  58.4 14.3 %collective-permute-start.21 = (bf16[32,2176]{1,0:T(8,128)(2,1)S(1)}, bf16[32,2176]{1,0:T(8,128)(2,1)S(1)}, u32[]{:S(2)}, u32[]{:S(2)}) collective-permute-start(bf16[32,2176]{1,0:T(8,128)(2,1)S(1)} %get-tuple-element.77), channel_id=1, source_target_pairs={{0,8},{4,12},{8,0},{12,4},{1,9},{5,13},{9,1},{13,5},{2,10},{6,14},... | collective-permute-start | bytes 417800 | tf_op jit(solution)/shard_map/ppermute | solution.py:282
  62.6 10.1 %collective-permute-start.22 = (bf16[32,2176]{1,0:T(8,128)(2,1)S(1)}, bf16[32,2176]{1,0:T(8,128)(2,1)S(1)}, u32[]{:S(2)}, u32[]{:S(2)}) collective-permute-start(bf16[32,2176]{1,0:T(8,128)(2,1)S(1)} %slice_add_fusion.1), channel_id=1, source_target_pairs={{0,12},{4,8},{8,4},{12,0},{1,13},{5,9},{9,5},{13,1},{2,14},{6,10},... | collective-permute-start | bytes 417800 | tf_op jit(solution)/shard_map/ppermute | solution.py:282
  64.1 8.6 %collective-permute-start.19 = (bf16[32,2176]{1,0:T(8,128)(2,1)S(1)}, bf16[32,2176]{1,0:T(8,128)(2,1)S(1)}, u32[]{:S(2)}, u32[]{:S(2)}) collective-permute-start(bf16[32,2176]{1,0:T(8,128)(2,1)S(1)} %slice.55), channel_id=1, source_target_pairs={{0,2},{2,0},{1,3},{3,1},{4,6},{6,4},{5,7},{7,5},{8,10},{10,8},{9,1... | collective-permute-start | bytes 417800 | tf_op jit(solution)/shard_map/ppermute | solution.py:278
  65.5 8.1 %copy-start.5 = (s32[32,8]{0,1:T(8,128)S(1)}, s32[32,8]{0,1:T(8,128)}, u32[]{:S(2)}) copy-start(s32[32,8]{0,1:T(8,128)} %param.9) | copy-start | bytes 3076

commit v3 on v2

--- a/solution.py
+++ b/solution.py
@@ -113,14 +113,18 @@
     )(*left(gate_w, up_w))
 
 
-def rows_kernel(shards, expert_ref, *refs):
+def rows_kernel(shards, experts, expert_ref, *refs):
     shard_refs = refs[:shards]
     wide_ref, down_ref, keep_ref, send_ref, xe_ref, diff_ref, tall_ref, table_ref, sems = refs[shards:]
     tok_count = shard_refs[0].shape[0] // 2
     rows = shards * tok_count
     half = rows // 2
     hidden, width = tall_ref.shape
-    experts = expert_ref[1]
+    pieces = 4
+    block = hidden // pieces
+    down_copies = [
+        (down_ref.at[0, pl.ds(i * block, block)], tall_ref.at[pl.ds(i * block, block)]) for i in range(pieces)
+    ]
     x_copies, e_copies = [], []
     for i, ref in enumerate(shard_refs):
         here = pl.ds(i * tok_count, tok_count)
@@ -129,18 +133,18 @@
             (ref.at[pl.ds(tok_count, tok_count), pl.ds(0, width)], xe_ref.at[pl.ds(rows + i * tok_count, tok_count)])
         )
         e_copies.append((ref.at[pl.ds(0, tok_count), pl.ds(width, SIDE)], table_ref.at[here]))
-    e_copies.append((down_ref.at[0], tall_ref))
-    copies = [pltpu.make_async_copy(src, dst, sems.at[i]) for i, (src, dst) in enumerate(x_copies + e_copies)]
+    copies = [
+        pltpu.make_async_copy(src, dst, sems.at[i]) for i, (src, dst) in enumerate(x_copies + down_copies + e_copies)
+    ]
     for copy in copies:
         copy.start()
-    lane = lax.broadcasted_iota(jnp.int32, (rows, SIDE), 1)
-    wanted = (lane == expert_ref[0]) | (lane == expert_ref[0] + experts)
+    chosen = expert_ref[:1, :] != 0
     for copy in copies[:shards]:
         copy.wait()
     pre = jnp.dot(xe_ref[:rows, :], wide_ref[...], preferred_element_type=F32)
     for copy in copies[shards:]:
         copy.wait()
-    weight = jnp.sum(jnp.where(wanted, table_ref[...].astype(F32), 0.0), axis=1, keepdims=True)
+    weight = jnp.sum(jnp.where(chosen, table_ref[...].astype(F32), 0.0), axis=1, keepdims=True)
     back = lax.dot_general(xe_ref[rows:, :], tall_ref[...], NT, preferred_element_type=F32)
     pre_gate, pre_up = pre[:, :hidden], pre[:, hidden:]
     sig = jax.nn.sigmoid(pre_gate)
@@ -158,13 +162,13 @@
         part = lax.dot_general(diff, wide_ref[c : c + block, :], NT, preferred_element_type=F32)
         keep_ref[:, c : c + block] = part[:half]
         send_ref[:, c : c + block] = part[half:].astype(BF16)
-    place = lax.rem(lane, experts) == expert_ref[0]
-    side = split_columns(jnp.where(place, product, 0.0), experts, lane)
+    lane = lax.broadcasted_iota(jnp.int32, (rows, SIDE), 1)
+    side = split_columns(jnp.where(chosen, product, 0.0), experts, lane)
     keep_ref[:, width:] = side[:half].astype(F32)
     send_ref[:, width:] = side[half:]
 
 
-def expert_rows_chunk(name, shards, expert_info, weights):
+def expert_rows_chunk(name, shards, experts, expert_info, weights):
     count = len(shards)
     tok_count = shards[0].shape[0] // 2
     wide = shards[0].shape[1]
@@ -172,8 +176,8 @@
     rows = count * tok_count
     hidden = weights[1].shape[1]
     return pl.pallas_call(
-        functools.partial(rows_kernel, count),
-        in_specs=[pl.BlockSpec(memory_space=pltpu.SMEM)] + in_hbm(count) + in_vmem(1) + in_hbm(1),
+        functools.partial(rows_kernel, count, experts),
+        in_specs=in_vmem(1) + in_hbm(count) + in_vmem(1) + in_hbm(1),
         out_specs=in_vmem(4),
         out_shape=[
             pltpu.VMEM((rows // 2, wide), F32),
@@ -184,7 +188,7 @@
         scratch_shapes=[
             pltpu.VMEM((hidden, width), BF16),
             pltpu.VMEM((rows, SIDE), BF16),
-            pltpu.SemaphoreType.DMA((3 * count + 1,)),
+            pltpu.SemaphoreType.DMA((3 * count + 4,)),
         ],
         compiler_params=pltpu.CompilerParams(vmem_limit_bytes=16 * MIB),
         cost_estimate=pl.CostEstimate(flops=1, bytes_accessed=1, transcendentals=0),
@@ -192,48 +196,27 @@
     )(expert_info, *(left(*shards) if count > 4 else shards), weights[0], *left(weights[1]))
 
 
-def grads_kernel(parts, first, *refs):
+def grads_kernel(parts, *refs):
     xe_refs = refs[:parts]
     diff_refs = refs[parts : 2 * parts]
-    gate_out, up_out, down_out, x_ref, e_ref, both_ref, down_ref, in_sems, out_sems = refs[-9:]
+    gate_out, up_out, down_out, both_ref, down_ref, out_sems = refs[2 * parts :]
     hidden = gate_out.shape[2]
-    span = x_ref.shape[1]
-    block = span // in_sems.shape[0]
-    arriving = []
-    for i, c in enumerate(range(0, span, block)):
-        copies = []
-        start = 0
-        for j, ref in enumerate(xe_refs):
-            rows = ref.shape[0] // 2
-            for k, dst in enumerate((x_ref, e_ref)):
-                copies.append(
-                    pltpu.make_async_copy(
-                        ref.at[pl.ds(k * rows, rows), pl.ds(first + c, block)],
-                        dst.at[pl.ds(start, rows), pl.ds(c, block)],
-                        in_sems.at[i, 2 * j + k],
-                    )
-                )
-            start += rows
-        for copy in copies:
-            copy.start()
-        arriving.append(copies)
+    width = gate_out.shape[1]
+    block = width // out_sems.shape[0]
     diffs = jnp.concatenate([ref[:, : 2 * hidden] for ref in diff_refs], axis=0)
     hidden_t = jnp.concatenate([ref[:, 2 * hidden :] for ref in diff_refs], axis=0).T
     leaving = []
-    for i, c in enumerate(range(0, span, block)):
-        for copy in arriving[i]:
-            copy.wait()
-        here, there = pl.ds(c, block), pl.ds(first + c, block)
-        both_ref[c : c + block, :] = lax.dot_general(
-            x_ref[:, c : c + block], diffs, TN, preferred_element_type=F32
-        ).astype(BF16)
-        down_ref[:, c : c + block] = jnp.dot(
-            hidden_t, e_ref[:, c : c + block], preferred_element_type=F32
-        ).astype(BF16)
+    for i, c in enumerate(range(0, width, block)):
+        columns = slice(c, c + block)
+        here = pl.ds(c, block)
+        x = jnp.concatenate([ref[: ref.shape[0] // 2, columns] for ref in xe_refs], axis=0)
+        e = jnp.concatenate([ref[ref.shape[0] // 2 :, columns] for ref in xe_refs], axis=0)
+        both_ref[columns, :] = lax.dot_general(x, diffs, TN, preferred_element_type=F32).astype(BF16)
+        down_ref[:, columns] = jnp.dot(hidden_t, e, preferred_element_type=F32).astype(BF16)
         copies = [
-            pltpu.make_async_copy(both_ref.at[here, pl.ds(0, hidden)], gate_out.at[0, there], out_sems.at[i, 0]),
-            pltpu.make_async_copy(both_ref.at[here, pl.ds(hidden, hidden)], up_out.at[0, there], out_sems.at[i, 1]),
-            pltpu.make_async_copy(down_ref.at[:, here], down_out.at[0, :, there], out_sems.at[i, 2]),
+            pltpu.make_async_copy(both_ref.at[here, pl.ds(0, hidden)], gate_out.at[0, here], out_sems.at[i, 0]),
+            pltpu.make_async_copy(both_ref.at[here, pl.ds(hidden, hidden)], up_out.at[0, here], out_sems.at[i, 1]),
+            pltpu.make_async_copy(down_ref.at[:, here], down_out.at[0, :, here], out_sems.at[i, 2]),
         ]
         for copy in copies:
             copy.start()
@@ -242,36 +225,65 @@
         copy.wait()
 
 
-def weight_grads(name, first, span, xe_parts, diff_parts, grads):
+def weight_grads(xe_parts, diff_parts):
     count = len(xe_parts)
     width = xe_parts[0].shape[1]
     hidden = diff_parts[0].shape[1] // 3
     total = sum(part.shape[0] for part in diff_parts)
-    blocks = span // 256
     return pl.pallas_call(
-        functools.partial(grads_kernel, count, first),
-        in_specs=in_hbm(count) + in_vmem(count) + in_hbm(len(grads)),
+        functools.partial(grads_kernel, count),
+        in_specs=in_vmem(2 * count),
         out_specs=in_hbm(3),
         out_shape=[
             jax.ShapeDtypeStruct((1, width, hidden), BF16),
             jax.ShapeDtypeStruct((1, width, hidden), BF16),
             jax.ShapeDtypeStruct((1, hidden, width), BF16),
         ],
-        input_output_aliases={2 * count + i: i for i in range(len(grads))},
         scratch_shapes=[
-            pltpu.VMEM((total, span), BF16),
-            pltpu.VMEM((total, span), BF16),
-            pltpu.VMEM((span, 2 * hidden), BF16),
-            pltpu.VMEM((hidden, span), BF16),
-            pltpu.SemaphoreType.DMA((blocks, 2 * count)),
-            pltpu.SemaphoreType.DMA((blocks, 3)),
+            pltpu.VMEM((width, 2 * hidden), BF16),
+            pltpu.VMEM((hidden, width), BF16),
+            pltpu.SemaphoreType.DMA((2, 3)),
         ],
-        compiler_params=pltpu.CompilerParams(vmem_limit_bytes=16 * MIB),
+        compiler_params=pltpu.CompilerParams(vmem_limit_bytes=24 * MIB),
         cost_estimate=pl.CostEstimate(
-            flops=6 * total * span * hidden, bytes_accessed=4 * total * span + 6 * span * hidden, transcendentals=0
+            flops=6 * total * width * hidden, bytes_accessed=4 * total * width + 6 * width * hidden, transcendentals=0
         ),
-        name=name,
-    )(*xe_parts, *diff_parts, *grads)
+        name="weight_grads",
+    )(*xe_parts, *diff_parts)
+
+
+def finish_kernel(parts, own_ref, *refs):
+    routes_ref, input_ref, routing_ref = refs[parts:]
+    width = input_ref.shape[1]
+    top_count = routes_ref.shape[0]
+    total = own_ref[...]
+    for ref in refs[:parts]:
+        total = total + ref[...].astype(F32)
+    input_ref[...] = total[:, :width].astype(BF16)
+    side = total[:, width:].T
+    products = side[:top_count] + side[top_count : 2 * top_count]
+    routes = routes_ref[...]
+    picked = jnp.zeros(routes.shape, F32)
+    for e in range(top_count):
+        picked += jnp.where(routes == e, products[e : e + 1, :], 0.0)
+    routing_ref[...] = picked
+
+
+def finish(own_sum, arrived, routes):
+    tok_count, top_count = routes.shape
+    width = own_sum.shape[1] - SIDE
+    input_grad, routing_grad = pl.pallas_call(
+        functools.partial(finish_kernel, len(arrived)),
+        in_specs=in_vmem(2 + len(arrived)),
+        out_specs=in_vmem(2),
+        out_shape=[
+            jax.ShapeDtypeStruct((tok_count, width), BF16),
+            jax.ShapeDtypeStruct((top_count, tok_count), F32),
+        ],
+        compiler_params=pltpu.CompilerParams(vmem_limit_bytes=4 * MIB),
+        name="finish",
+    )(own_sum, *arrived, routes.T)
+    return input_grad, routing_grad.T
 
 
 def swap(value, axis):
@@ -293,7 +305,8 @@
     top_count = routes.shape[1]
     lines = lax.axis_size("expert")
     expert = lax.axis_index("expert") * lax.axis_size("dp") + lax.axis_index("dp")
-    expert_info = jnp.stack([expert, jnp.int32(top_count)]).astype(jnp.int32)
+    lane = lax.broadcasted_iota(jnp.int32, (8, SIDE), 1)
+    expert_info = ((lane == expert) | (lane == expert + top_count)).astype(jnp.int32)
     packed = pack(layer_input, output_grad, routes, routing_weight)
     columns, across = {}, {}
     gate_w, up_w, packed = together(gate_proj, up_proj, packed)
@@ -309,39 +322,33 @@
     across[3] = swap(columns[3], "dp")
     weights = (wide_w, down_proj)
 
-    chunk = (2, 1, 0)
-    shards = [columns[k] for k in chunk] + [across[k] for k in chunk]
+    shards = [columns[2], across[2], columns[1], columns[0], across[1], across[0]]
     shards += [swap(shard, "sub") for shard in shards]
-    keep, send, xe_0, diff_0 = expert_rows_chunk("rows_0", shards, expert_info, weights)
+    keep, send, xe_0, diff_0 = expert_rows_chunk("rows_0", shards, top_count, expert_info, weights)
     diff_0, columns[3], across[3] = together(diff_0, columns[3], across[3])
     send, across[3] = together(send, across[3])
-    paired = keep + swap(send, "sub").astype(F32)
-    size = len(chunk) * tok_count
-    own_0 = paired[2 * tok_count : size]
-    away_0 = paired[size + 2 * tok_count :].astype(BF16)
-    home_21 = paired[: 2 * tok_count] + swap(paired[size : size + 2 * tok_count].astype(BF16), "dp").astype(F32)
+    rows = tok_count
+    paired_2 = keep[: 2 * rows] + swap(send[: 2 * rows], "sub").astype(F32)
+    home_2 = paired_2[:rows] + swap(paired_2[rows:].astype(BF16), "dp").astype(F32)
+    paired_10 = keep[2 * rows :] + swap(send[2 * rows :], "sub").astype(F32)
+    away_1, away_0 = paired_10[2 * rows : 3 * rows].astype(BF16), paired_10[3 * rows :].astype(BF16)
 
     shards = [columns[3], across[3]]
     shards += [swap(shard, "sub") for shard in shards]
-    keep, send, xe_3, diff_3 = expert_rows_chunk("rows_3", shards, expert_info, weights)
-    send, home_21 = together(send, home_21)
-    back_2 = far(home_21[:tok_count].astype(BF16), "expert", 2)
-    paired = keep + swap(send, "sub").astype(F32)
-    home_3 = paired[:tok_count] + swap(paired[tok_count:].astype(BF16), "dp").astype(F32)
-    home_3, away_0 = together(home_3, away_0)
-    own_sum = own_0 + swap(away_0, "dp").astype(F32)
+    keep, send, xe_3, diff_3 = expert_rows_chunk("rows_3", shards, top_count, expert_info, weights)
+    send, home_2 = together(send, home_2)
+    back_2 = far(home_2.astype(BF16), "expert", 2)
+    paired_3 = keep + swap(send, "sub").astype(F32)
+    home_3 = paired_3[:rows] + swap(paired_3[rows:].astype(BF16), "dp").astype(F32)
+    home_1 = paired_10[:rows] + swap(away_1, "dp").astype(F32)
+    home_3, away_0, back_2 = together(home_3, away_0, back_2)
+    back_0 = swap(away_0, "dp")
     back_3 = far(home_3.astype(BF16), "expert", 3)
-    back_1 = far(home_21[tok_count:].astype(BF16), "expert", 1)
-    gate_grads, up_grads, down_grads = weight_grads("grads", 0, width, (xe_0, xe_3), (diff_0, diff_3), ())
+    back_1 = far(home_1.astype(BF16), "expert", 1)
+    gate_grads, up_grads, down_grads = weight_grads((xe_0, xe_3), (diff_0, diff_3))
     gate_grads, back_1, back_2, back_3 = together(gate_grads, back_1, back_2, back_3)
-    arrived = (back_1, back_2, back_3)
-    total = own_sum
-    for block in arrived:
-        total = total + block.astype(F32)
-    input_grad = total[:, :width].astype(BF16)
-    products = total[:, width : width + top_count] + total[:, width + top_count : width + 2 * top_count]
-    chosen = routes[:, :, None] == jnp.arange(top_count, dtype=jnp.int32)[None, None, :]
-    routing_grad = jnp.sum(jnp.where(chosen, products[:, None, :], 0.0), axis=2)
+    arrived = (back_0, back_1, back_2, back_3)
+    input_grad, routing_grad = finish(paired_10[rows : 2 * rows], arrived, routes)
     return (input_grad, routing_grad, gate_grads, up_grads, down_grads)
 
 

time: 74.4 us -> 69.2 us (0.930)
  Pallas kernels: 21.3 us -> 17.5 us
  waiting for transfers between devices: 27.3 us -> 26.2 us
  starting transfers between devices: 22.8 us -> 23.9 us
  other arithmetic: 1.15 us -> 0.37 us
    pallas_call x3 -> x4, Pallas kernels: 18.4 us -> 14.6 us  [the longest x2 9.94 us: expert_rows_chunk(): pl.pallas_call(functools.partial(rows_kernel, count, experts), in_specs=i...]
    ppermute x17 -> x19, waiting for transfers between devices: 14.7 us -> 13.5 us  [swap(): return lax.ppermute(value, axis, [(0, 1), (1, 0)])]
    ppermute x17 -> x19, starting transfers between devices: 11.1 us -> 12 us  [swap(): return lax.ppermute(value, axis, [(0, 1), (1, 0)])]
  transfers between devices with their start and end apart: 23 -> 25, of which waited for: 11 -> 12; matrix products, arithmetic and copies ran while one was open for 0% -> 1% of each run, Pallas kernels for 27% -> 23%
where the time goes in v3:
time: 69.2 us; the launch traced here: 69 us
  waiting for transfers between devices  26.2 us (38%)
  starting transfers between devices  23.9 us (35%)
  Pallas kernels  17.5 us (25%)
  between operations  0.83 us (1%)
    ppermute x19, waiting for transfers between devices, swap(): return lax.ppermute(value, axis, [(0, 1), (1, 0)])  13.5 us
    ppermute x6, waiting for transfers between devices, far(): lax.ppermute(value, axis, [(i, i ^ distance) for i in range(lax.axis_size...  12.7 us
    ppermute x19, starting transfers between devices, swap(): return lax.ppermute(value, axis, [(0, 1), (1, 0)])  12 us
    ppermute x6, starting transfers between devices, far(): lax.ppermute(value, axis, [(i, i ^ distance) for i in range(lax.axis_size...  11.9 us
    pallas_call x2, Pallas kernels, expert_rows_chunk(): pl.pallas_call(functools.partial(rows_kernel, count, experts), in_specs=i...  9.94 us
    pallas_call x1, Pallas kernels, weight_grads(): pl.pallas_call(functools.partial(grads_kernel, count), in_specs=in_vmem(2...  3.91 us
    pallas_call x1, Pallas kernels, stage(): pl.pallas_call(stage_kernel, in_specs=in_hbm(2), out_specs=in_vmem(1)[0],...  1.89 us
  transfers between devices with their start and end apart: 25, of which 12 were waited for; matrix products, arithmetic and copies ran while one was open for 1% of the time, Pallas kernels for 23%

profile of v3, /device:TPU:0, one launch (start us, length us, event | category | flops | bytes accessed | tf_op | source)
XLA Modules:
  0.0 69.0 jit_solution(14238564286942856151)
XLA Ops:
  0.6 1.0 %pack_tokens.1.refs_3_ = bf16[64,2176]{1,0:T(8,128)(2,1)S(1)} custom-call(bf16[32,2048]{1,0:T(8,128)(2,1)} %x_ref.1, bf16[32,2048]{1,0:T(8,128)(2,1)} %e_ref.1, s32[8,32]{1,0:T(8,128)} %bitcast.3, f32[8,32]{1,0:T(8,128)} %bitcast.5), custom_call_target="tpu_custom_call" | custom-call | tf_op jit(solution)/shard_map/pack_tokens/pallas_call | solution.py:70
  1.7 3.1 %collective-permute-start = (bf16[64,2176]{1,0:T(8,128)(2,1)S(1)}, bf16[64,2176]{1,0:T(8,128)(2,1)S(1)}, u32[]{:S(2)}, u32[]{:S(2)}) collective-permute-start(bf16[64,2176]{1,0:T(8,128)(2,1)S(1)} %pack_tokens.1.refs_3_), channel_id=1, source_target_pairs={{0,4},{4,0},{8,12},{12,8},{1,5},{5,1},{9,13},{13,9},{2,6},{6,2},{1... | collective-permute-start | bytes 835592 | tf_op jit(solution)/shard_map/ppermute | solution.py:294
  4.8 2.6 %collective-permute-start.1 = (bf16[64,2176]{1,0:T(8,128)(2,1)S(1)}, bf16[64,2176]{1,0:T(8,128)(2,1)S(1)}, u32[]{:S(2)}, u32[]{:S(2)}) collective-permute-start(bf16[64,2176]{1,0:T(8,128)(2,1)S(1)} %pack_tokens.1.refs_3_), channel_id=1, source_target_pairs={{0,8},{4,12},{8,0},{12,4},{1,9},{5,13},{9,1},{13,5},{2,10},{6,14},... | collective-permute-start | bytes 835592 | tf_op jit(solution)/shard_map/ppermute | solution.py:294
  7.4 1.5 %collective-permute-start.2 = (bf16[64,2176]{1,0:T(8,128)(2,1)S(1)}, bf16[64,2176]{1,0:T(8,128)(2,1)}, u32[]{:S(2)}, u32[]{:S(2)}) collective-permute-start(bf16[64,2176]{1,0:T(8,128)(2,1)S(1)} %pack_tokens.1.refs_3_), channel_id=1, source_target_pairs={{0,2},{2,0},{1,3},{3,1},{4,6},{6,4},{5,7},{7,5},{8,10},{10,8},{9,1... | collective-permute-start | bytes 835592 | tf_op jit(solution)/shard_map/ppermute | solution.py:290
  8.9 1.9 %stage_weights.1.refs_12_.refs_4_ = bf16[2048,768]{1,0:T(8,128)(2,1)S(1)} custom-call(bf16[1,2048,384]{2,1,0:T(8,128)(2,1)} %gate_ref, bf16[1,2048,384]{2,1,0:T(8,128)(2,1)} %up_ref), custom_call_target="tpu_custom_call" | custom-call | flops 1 | bytes 1 | tf_op jit(solution)/shard_map/stage_weights/pallas_call | solution.py:104
  10.8 6.5 %collective-permute-done.refs_2_ = bf16[64,2176]{1,0:T(8,128)(2,1)S(1)} collective-permute-done((bf16[64,2176]{1,0:T(8,128)(2,1)S(1)}, bf16[64,2176]{1,0:T(8,128)(2,1)S(1)}, u32[]{:S(2)}, u32[]{:S(2)}) %collective-permute-start) | collective-permute-done | bytes 278560 | tf_op jit(solution)/shard_map/ppermute | solution.py:294
  17.3 2.5 %collective-permute-done.1.refs_0_ = bf16[64,2176]{1,0:T(8,128)(2,1)S(1)} collective-permute-done((bf16[64,2176]{1,0:T(8,128)(2,1)S(1)}, bf16[64,2176]{1,0:T(8,128)(2,1)S(1)}, u32[]{:S(2)}, u32[]{:S(2)}) %collective-permute-start.1) | collective-permute-done | bytes 278560 | tf_op jit(solution)/shard_map/ppermute | solution.py:294
  19.8 2.5 %collective-permute-start.3 = (bf16[64,2176]{1,0:T(8,128)(2,1)S(1)}, bf16[64,2176]{1,0:T(8,128)(2,1)}, u32[]{:S(2)}, u32[]{:S(2)}) collective-permute-start(bf16[64,2176]{1,0:T(8,128)(2,1)S(1)} %pack_tokens.1.refs_3_), channel_id=1, source_target_pairs={{0,12},{4,8},{8,4},{12,0},{1,13},{5,9},{9,5},{13,1},{2,14},{6,10},... | collective-permute-start | bytes 835592 | tf_op jit(solution)/shard_map/ppermute | solution.py:294
  22.3 1.5 %collective-permute-start.4 = (bf16[64,2176]{1,0:T(8,128)(2,1)S(1)}, bf16[64,2176]{1,0:T(8,128)(2,1)}, u32[]{:S(2)}, u32[]{:S(2)}) collective-permute-start(bf16[64,2176]{1,0:T(8,128)(2,1)S(1)} %collective-permute-done.refs_2_), channel_id=1, source_target_pairs={{0,2},{2,0},{1,3},{3,1},{4,6},{6,4},{5,7},{7,5},{8,10},{10,8},{9,1... | collective-permute-start | bytes 835592 | tf_op jit(solution)/shard_map/ppermute | solution.py:290
  23.8 0.5 collective-permute-start.5
  24.3 0.5 collective-permute-start.8
  24.8 3.5 %collective-permute-done.3.refs_0_ = bf16[64,2176]{1,0:T(8,128)(2,1)} collective-permute-done((bf16[64,2176]{1,0:T(8,128)(2,1)S(1)}, bf16[64,2176]{1,0:T(8,128)(2,1)}, u32[]{:S(2)}, u32[]{:S(2)}) %collective-permute-start.3) | collective-permute-done | bytes 278560 | tf_op jit(solution)/shard_map/ppermute | solution.py:294
  28.4 2.0 %collective-permute-done.4.refs_4_ = bf16[64,2176]{1,0:T(8,128)(2,1)} collective-permute-done((bf16[64,2176]{1,0:T(8,128)(2,1)S(1)}, bf16[64,2176]{1,0:T(8,128)(2,1)}, u32[]{:S(2)}, u32[]{:S(2)}) %collective-permute-start.4) | collective-permute-done | bytes 278560 | tf_op jit(solution)/shard_map/ppermute | solution.py:290
  30.4 3.0 %collective-permute-done.5.refs_1_ = bf16[64,2176]{1,0:T(8,128)(2,1)} collective-permute-done((bf16[64,2176]{1,0:T(8,128)(2,1)S(1)}, bf16[64,2176]{1,0:T(8,128)(2,1)}, u32[]{:S(2)}, u32[]{:S(2)}) %collective-permute-start.5) | collective-permute-done | bytes 278560 | tf_op jit(solution)/shard_map/ppermute | solution.py:290
  33.4 0.5 collective-permute-start.7
  33.9 1.6 %collective-permute-start.12 = (bf16[64,2176]{1,0:T(8,128)(2,1)}, bf16[64,2176]{1,0:T(8,128)(2,1)}, u32[]{:S(2)}, u32[]{:S(2)}) collective-permute-start(bf16[64,2176]{1,0:T(8,128)(2,1)} %collective-permute-done.3.refs_0_), channel_id=1, source_target_pairs={{0,2},{2,0},{1,3},{3,1},{4,6},{6,4},{5,7},{7,5},{8,10},{10,8},{9,1... | collective-permute-start | bytes 835592 | tf_op jit(solution)/shard_map/ppermute | solution.py:290
  35.6 6.3 %rows_0.1 = (f32[192,2176]{1,0:T(8,128)S(1)}, bf16[192,2176]{1,0:T(8,128)(2,1)S(1)}, bf16[768,2048]{1,0:T(8,128)(2,1)S(1)}, bf16[384,1152]{1,0:T(8,128)(2,1)S(1)}) custom-call(s32[8,128]{1,0:T(8,128)S(1)} %iota.10.expert_ref, bf16[64,2176]{1,0:T(8,128)(2,1)} %copy-done.3, bf16[64,2176]{1,0:T(8,128)(2,1)} %collective-permute-done.5.refs_1_, ...), custom_call_target="tpu_custom_call" | custom-call | flops 1 | bytes 1 | tf_op jit(solution)/shard_map/rows_0/pallas_call | solution.py:178
  42.0 0.9 %collective-permute-done.12.refs_1_ = bf16[64,2176]{1,0:T(8,128)(2,1)} collective-permute-done((bf16[64,2176]{1,0:T(8,128)(2,1)}, bf16[64,2176]{1,0:T(8,128)(2,1)}, u32[]{:S(2)}, u32[]{:S(2)}) %collective-permute-start.12) | collective-permute-done | bytes 278560 | tf_op jit(solution)/shard_map/ppermute | solution.py:290
  43.0 0.5 collective-permute-start.15
  43.6 1.0 %collective-permute-done.16 = bf16[64,2176]{1,0:T(8,128)(2,1)S(1)} collective-permute-done((bf16[64,2176]{1,0:T(8,128)(2,1)S(1)}, bf16[64,2176]{1,0:T(8,128)(2,1)S(1)}, u32[]{:S(2)}, u32[]{:S(2)}) %collective-permute-start.16) | collective-permute-done | bytes 278560 | tf_op jit(solution)/shard_map/ppermute | solution.py:290
  44.6 1.6 %collective-permute-start.17 = (bf16[32,2176]{1,0:T(8,128)(2,1)S(1)}, bf16[32,2176]{1,0:T(8,128)(2,1)S(1)}, u32[]{:S(2)}, u32[]{:S(2)}) collective-permute-start(bf16[32,2176]{1,0:T(8,128)(2,1)S(1)} %slice.70), channel_id=1, source_target_pairs={{0,2},{2,0},{1,3},{3,1},{4,6},{6,4},{5,7},{7,5},{8,10},{10,8},{9,1... | collective-permute-start | bytes 417800 | tf_op jit(solution)/shard_map/ppermute | solution.py:290
  46.3 3.6 %rows_3.1 = (f32[64,2176]{1,0:T(8,128)S(1)}, bf16[64,2176]{1,0:T(8,128)(2,1)S(1)}, bf16[256,2048]{1,0:T(8,128)(2,1)S(1)}, bf16[128,1152]{1,0:T(8,128)(2,1)S(1)}) custom-call(s32[8,128]{1,0:T(8,128)S(1)} %iota.10.expert_ref, bf16[64,2176]{1,0:T(8,128)(2,1)} %collective-permute-done.3.refs_0_, bf16[64,2176]{1,0:T(8,128)(2,1)} %collective-permute-done.12.refs_1_, ...), custom_call_target="tpu_custom_call" | custom-call | flops 1 | bytes 1 | tf_op jit(solution)/shard_map/rows_3/pallas_call | solution.py:178
  50.5 1.7 %collective-permute-start.20 = (bf16[32,2176]{1,0:T(8,128)(2,1)S(1)}, bf16[32,2176]{1,0:T(8,128)(2,1)S(1)}, u32[]{:S(2)}, u32[]{:S(2)}) collective-permute-start(bf16[32,2176]{1,0:T(8,128)(2,1)S(1)} %slice_add_fusion.2), channel_id=1, source_target_pairs={{0,8},{4,12},{8,0},{12,4},{1,9},{5,13},{9,1},{13,5},{2,10},{6,14},... | collective-permute-start | bytes 417800 | tf_op jit(solution)/shard_map/ppermute | solution.py:294
  52.4 1.6 %collective-permute-start.22 = (bf16[32,2176]{1,0:T(8,128)(2,1)S(1)}, bf16[32,2176]{1,0:T(8,128)(2,1)S(1)}, u32[]{:S(2)}, u32[]{:S(2)}) collective-permute-start(bf16[32,2176]{1,0:T(8,128)(2,1)S(1)} %get-tuple-element.85), channel_id=1, source_target_pairs={{0,2},{2,0},{1,3},{3,1},{4,6},{6,4},{5,7},{7,5},{8,10},{10,8},{9,1... | collective-permute-start | bytes 417800 | tf_op jit(solution)/shard_map/ppermute | solution.py:290
  54.0 0.6 collective-permute-start.19
  54.6 4.3 %collective-permute-done.22 = bf16[32,2176]{1,0:T(8,128)(2,1)S(1)} collective-permute-done((bf16[32,2176]{1,0:T(8,128)(2,1)S(1)}, bf16[32,2176]{1,0:T(8,128)(2,1)S(1)}, u32[]{:S(2)}, u32[]{:S(2)}) %collective-permute-start.22) | collective-permute-done | bytes 139296 | tf_op jit(solution)/shard_map/ppermute | solution.py:290
  59.0 0.5 collective-permute-start.23
  59.5 1.7 %collective-permute-done.19 = bf16[32,2176]{1,0:T(8,128)(2,1)S(1)} collective-permute-done((bf16[32,2176]{1,0:T(8,128)(2,1)S(1)}, bf16[32,2176]{1,0:T(8,128)(2,1)S(1)}, u32[]{:S(2)}, u32[]{:S(2)}) %collective-permute-start.19) | collective-permute-done | bytes 139296 | tf_op jit(solution)/shard_map/ppermute | solution.py:290
  61.2 1.6 %collective-permute-start.24 = (bf16[32,2176]{1,0:T(8,128)(2,1)S(1)}, bf16[32,2176]{1,0:T(8,128)(2,1)S(1)}, u32[]{:S(2)}, u32[]{:S(2)}) collective-permute-start(bf16[32,2176]{1,0:T(8,128)(2,1)S(1)} %slice_add_fusion.1), channel_id=1, source_target_pairs={{0,12},{4,8},{8,4},{12,0},{1,13},{5,9},{9,5},{13,1},{2,14},{6,10},... | collective-permute-start | bytes 417800 | tf_op jit(solution)/shard_map/ppermute | solution.py:294
  62.8 1.3 %collective-permute-start.21 = (bf16[32,2176]{1,0:T(8,128)(2,1)S(1)}, bf16[32,2176]{1,0:T(8,128)(2,1)S(1)}, u32[]{:S(2)}, u32[]{:S(2)}) collective-permute-start(bf16[32,2176]{1,0:T(8,128)(2,1)S(1)} %get-tuple-element.65), channel_id=1, source_target_pairs={{0,2},{2,0},{1,3},{3,1},{4,6},{6,4},{5,7},{7,5},{8,10},{10,8},{9,1... | collective-permute-start | bytes 417800 | tf_op jit(solution)/shard_map/ppermute | solution.py:290
  64.2 3.9 %weight_grads.1 = (bf16[1,2048,384]{2,1,0:T(8,128)(2,1)}, bf16[1,2048,384]{2,1,0:T(8,128)(2,1)}, bf16[1,384,2048]{2,1,0:T(8,128)(2,1)}) custom-call(bf16[768,2048]{1,0:T(8,128)(2,1)S(1)} %get-tuple-element.66.refs_0_, bf16[256,2048]{1,0:T(8,128)(2,1)S(1)} %get-tuple-element.67.refs_1_, bf16[384,1152]{1,0:T(8,128)(2,1)S(1)} %get-tuple-element.68.refs_2_, ...), custom_call_target="tpu_custom_call" | custom-call | flops 2415919104 | bytes 8912896 | tf_op jit(solution)/shard_map/weight_grads/pallas_call | solution.py:233
  68.2 0.8 %finish.1 = (bf16[32,2048]{1,0:T(8,128)(2,1)}, f32[8,32]{1,0:T(8,128)}) custom-call(f32[32,2176]{1,0:T(8,128)S(1)} %get-tuple-element.84.own_ref, bf16[32,2176]{1,0:T(8,128)(2,1)S(1)} %collective-permute-done.21.refs_0_, bf16[32,2176]{1,0:T(8,128)(2,1)S(1)} %collective-permute-done.23.refs_1_, bf16[32,2176]{1,0:T(8,128)(2,1)S(1)} %collective-permute-done.20.refs_2_, ...), custom_call_target="tpu_custom_call" | custom-call | tf_op jit(solution)/shard_map/finish/pallas_call | solution.py:275
  (49 shorter events, 1.6 us)
Async XLA Ops:
  1.7 26.7 %copy-start = (bf16[64,2176]{1,0:T(8,128)(2,1)}, bf16[64,2176]{1,0:T(8,128)(2,1)S(1)}, u32[]{:S(2)}) copy-start(bf16[64,2176]{1,0:T(8,128)(2,1)S(1)} %pack_tokens.1.refs_3_) | copy-start | bytes 835588
  1.7 15.6 %collective-permute-start = (bf16[64,2176]{1,0:T(8,128)(2,1)S(1)}, bf16[64,2176]{1,0:T(8,128)(2,1)S(1)}, u32[]{:S(2)}, u32[]{:S(2)}) collective-permute-start(bf16[64,2176]{1,0:T(8,128)(2,1)S(1)} %pack_tokens.1.refs_3_), channel_id=1, source_target_pairs={{0,4},{4,0},{8,12},{12,8},{1,5},{5,1},{9,13},{13,9},{2,6},{6,2},{1... | collective-permute-start | bytes 835592 | tf_op jit(solution)/shard_map/ppermute | solution.py:294
  4.8 15.0 %collective-permute-start.1 = (bf16[64,2176]{1,0:T(8,128)(2,1)S(1)}, bf16[64,2176]{1,0:T(8,128)(2,1)S(1)}, u32[]{:S(2)}, u32[]{:S(2)}) collective-permute-start(bf16[64,2176]{1,0:T(8,128)(2,1)S(1)} %pack_tokens.1.refs_3_), channel_id=1, source_target_pairs={{0,8},{4,12},{8,0},{12,4},{1,9},{5,13},{9,1},{13,5},{2,10},{6,14},... | collective-permute-start | bytes 835592 | tf_op jit(solution)/shard_map/ppermute | solution.py:294
  7.4 12.4 %collective-permute-start.2 = (bf16[64,2176]{1,0:T(8,128)(2,1)S(1)}, bf16[64,2176]{1,0:T(8,128)(2,1)}, u32[]{:S(2)}, u32[]{:S(2)}) collective-permute-start(bf16[64,2176]{1,0:T(8,128)(2,1)S(1)} %pack_tokens.1.refs_3_), channel_id=1, source_target_pairs={{0,2},{2,0},{1,3},{3,1},{4,6},{6,4},{5,7},{7,5},{8,10},{10,8},{9,1... | collective-permute-start | bytes 835592 | tf_op jit(solution)/shard_map/ppermute | solution.py:290
  17.3 11.1 %copy-start.2 = (bf16[64,2176]{1,0:T(8,128)(2,1)}, bf16[64,2176]{1,0:T(8,128)(2,1)S(1)}, u32[]{:S(2)}) copy-start(bf16[64,2176]{1,0:T(8,128)(2,1)S(1)} %collective-permute-done.refs_2_) | copy-start | bytes 835588
  19.8 14.1 %copy-start.3 = (bf16[64,2176]{1,0:T(8,128)(2,1)}, bf16[64,2176]{1,0:T(8,128)(2,1)S(1)}, u32[]{:S(2)}) copy-start(bf16[64,2176]{1,0:T(8,128)(2,1)S(1)} %collective-permute-done.1.refs_0_) | copy-start | bytes 835588
  19.8 8.6 %collective-permute-start.3 = (bf16[64,2176]{1,0:T(8,128)(2,1)S(1)}, bf16[64,2176]{1,0:T(8,128)(2,1)}, u32[]{:S(2)}, u32[]{:S(2)}) collective-permute-start(bf16[64,2176]{1,0:T(8,128)(2,1)S(1)} %pack_tokens.1.refs_3_), channel_id=1, source_target_pairs={{0,12},{4,8},{8,4},{12,0},{1,13},{5,9},{9,5},{13,1},{2,14},{6,10},... | collective-permute-start | bytes 835592 | tf_op jit(solution)/shard_map/ppermute | solution.py:294
  22.3 8.1 %collective-permute-start.4 = (bf16[64,2176]{1,0:T(8,128)(2,1)S(1)}, bf16[64,2176]{1,0:T(8,128)(2,1)}, u32[]{:S(2)}, u32[]{:S(2)}) collective-permute-start(bf16[64,2176]{1,0:T(8,128)(2,1)S(1)} %collective-permute-done.refs_2_), channel_id=1, source_target_pairs={{0,2},{2,0},{1,3},{3,1},{4,6},{6,4},{5,7},{7,5},{8,10},{10,8},{9,1... | collective-permute-start | bytes 835592 | tf_op jit(solution)/shard_map/ppermute | solution.py:290
  23.8 9.6 %collective-permute-start.5 = (bf16[64,2176]{1,0:T(8,128)(2,1)S(1)}, bf16[64,2176]{1,0:T(8,128)(2,1)}, u32[]{:S(2)}, u32[]{:S(2)}) collective-permute-start(bf16[64,2176]{1,0:T(8,128)(2,1)S(1)} %collective-permute-done.1.refs_0_), channel_id=1, source_target_pairs={{0,2},{2,0},{1,3},{3,1},{4,6},{6,4},{5,7},{7,5},{8,10},{10,8},{9,1... | collective-permute-start | bytes 835592 | tf_op jit(solution)/shard_map/ppermute | solution.py:290
  24.3 9.0 %collective-permute-start.6 = (bf16[64,2176]{1,0:T(8,128)(2,1)S(1)}, bf16[64,2176]{1,0:T(8,128)(2,1)S(1)}, u32[]{:S(2)}, u32[]{:S(2)}) collective-permute-start(bf16[64,2176]{1,0:T(8,128)(2,1)S(1)} %collective-permute-done.1.refs_0_), channel_id=1, source_target_pairs={{0,1},{1,0},{2,3},{3,2},{4,5},{5,4},{6,7},{7,6},{8,9},{9,8},{10,11... | collective-permute-start | bytes 835592 | tf_op jit(solution)/shard_map/ppermute | solution.py:290
  24.3 9.5 %collective-permute-start.8 = (bf16[64,2176]{1,0:T(8,128)(2,1)S(1)}, bf16[64,2176]{1,0:T(8,128)(2,1)S(1)}, u32[]{:S(2)}, u32[]{:S(2)}) collective-permute-start(bf16[64,2176]{1,0:T(8,128)(2,1)S(1)} %collective-permute-done.refs_2_), channel_id=1, source_target_pairs={{0,1},{1,0},{2,3},{3,2},{4,5},{5,4},{6,7},{7,6},{8,9},{9,8},{10,11... | collective-permute-start | bytes 835592 | tf_op jit(solution)/shard_map/ppermute | solution.py:290
  28.4 7.1 %collective-permute-start.9 = (bf16[64,2176]{1,0:T(8,128)(2,1)S(1)}, bf16[64,2176]{1,0:T(8,128)(2,1)}, u32[]{:S(2)}, u32[]{:S(2)}) collective-permute-start(bf16[64,2176]{1,0:T(8,128)(2,1)S(1)} %pack_tokens.1.refs_3_), channel_id=1, source_target_pairs={{0,1},{1,0},{2,3},{3,2},{4,5},{5,4},{6,7},{7,6},{8,9},{9,8},{10,11... | collective-permute-start | bytes 835592 | tf_op jit(solution)/shard_map/ppermute | solution.py:290
  30.4 5.1 %collective-permute-start.11 = (bf16[64,2176]{1,0:T(8,128)(2,1)}, bf16[64,2176]{1,0:T(8,128)(2,1)}, u32[]{:S(2)}, u32[]{:S(2)}) collective-permute-start(bf16[64,2176]{1,0:T(8,128)(2,1)} %collective-permute-done.2.refs_5_), channel_id=1, source_target_pairs={{0,1},{1,0},{2,3},{3,2},{4,5},{5,4},{6,7},{7,6},{8,9},{9,8},{10,11... | collective-permute-start | bytes 835592 | tf_op jit(solution)/shard_map/ppermute | solution.py:290
  33.3 2.1 %collective-permute-start.10 = (bf16[64,2176]{1,0:T(8,128)(2,1)}, bf16[64,2176]{1,0:T(8,128)(2,1)}, u32[]{:S(2)}, u32[]{:S(2)}) collective-permute-start(bf16[64,2176]{1,0:T(8,128)(2,1)} %collective-permute-done.4.refs_4_), channel_id=1, source_target_pairs={{0,1},{1,0},{2,3},{3,2},{4,5},{5,4},{6,7},{7,6},{8,9},{9,8},{10,11... | collective-permute-start | bytes 835592 | tf_op jit(solution)/shard_map/ppermute | solution.py:290
  33.3 2.1 %copy-start.4 = (bf16[64,2176]{1,0:T(8,128)(2,1)}, bf16[64,2176]{1,0:T(8,128)(2,1)S(1)}, u32[]{:S(2)}) copy-start(bf16[64,2176]{1,0:T(8,128)(2,1)S(1)} %collective-permute-done.6.refs_6_) | copy-start | bytes 835588
  33.4 2.3 %collective-permute-start.7 = (bf16[64,2176]{1,0:T(8,128)(2,1)}, bf16[64,2176]{1,0:T(8,128)(2,1)}, u32[]{:S(2)}, u32[]{:S(2)}) collective-permute-start(bf16[64,2176]{1,0:T(8,128)(2,1)} %collective-permute-done.5.refs_1_), channel_id=1, source_target_pairs={{0,1},{1,0},{2,3},{3,2},{4,5},{5,4},{6,7},{7,6},{8,9},{9,8},{10,11... | collective-permute-start | bytes 835592 | tf_op jit(solution)/shard_map/ppermute | solution.py:290
  33.9 1.6 %copy-start.5 = (bf16[64,2176]{1,0:T(8,128)(2,1)}, bf16[64,2176]{1,0:T(8,128)(2,1)S(1)}, u32[]{:S(2)}) copy-start(bf16[64,2176]{1,0:T(8,128)(2,1)S(1)} %collective-permute-done.8.refs_8_) | copy-start | bytes 835588
  33.9 9.0 %collective-permute-start.12 = (bf16[64,2176]{1,0:T(8,128)(2,1)}, bf16[64,2176]{1,0:T(8,128)(2,1)}, u32[]{:S(2)}, u32[]{:S(2)}) collective-permute-start(bf16[64,2176]{1,0:T(8,128)(2,1)} %collective-permute-done.3.refs_0_), channel_id=1, source_target_pairs={{0,2},{2,0},{1,3},{3,1},{4,6},{6,4},{5,7},{7,5},{8,10},{10,8},{9,1... | collective-permute-start | bytes 835592 | tf_op jit(solution)/shard_map/ppermute | solution.py:290
  42.9 1.6 %collective-permute-start.16 = (bf16[64,2176]{1,0:T(8,128)(2,1)S(1)}, bf16[64,2176]{1,0:T(8,128)(2,1)S(1)}, u32[]{:S(2)}, u32[]{:S(2)}) collective-permute-start(bf16[64,2176]{1,0:T(8,128)(2,1)S(1)} %slice.44), channel_id=1, source_target_pairs={{0,1},{1,0},{2,3},{3,2},{4,5},{5,4},{6,7},{7,6},{8,9},{9,8},{10,11... | collective-permute-start | bytes 835592 | tf_op jit(solution)/shard_map/ppermute | solution.py:290
  43.0 3.3 %collective-permute-start.15 = (bf16[64,2176]{1,0:T(8,128)(2,1)}, bf16[64,2176]{1,0:T(8,128)(2,1)S(1)}, u32[]{:S(2)}, u32[]{:S(2)}) collective-permute-start(bf16[64,2176]{1,0:T(8,128)(2,1)} %collective-permute-done.12.refs_1_), channel_id=1, source_target_pairs={{0,1},{1,0},{2,3},{3,2},{4,5},{5,4},{6,7},{7,6},{8,9},{9,8},{10,11... | collective-permute-start | bytes 835592 | tf_op jit(solution)/shard_map/ppermute | solution.py:290
  43.5 2.8 %collective-permute-start.14 = (bf16[64,2176]{1,0:T(8,128)(2,1)}, bf16[64,2176]{1,0:T(8,128)(2,1)S(1)}, u32[]{:S(2)}, u32[]{:S(2)}) collective-permute-start(bf16[64,2176]{1,0:T(8,128)(2,1)} %collective-permute-done.3.refs_0_), channel_id=1, source_target_pairs={{0,1},{1,0},{2,3},{3,2},{4,5},{5,4},{6,7},{7,6},{8,9},{9,8},{10,11... | collective-permute-start | bytes 835592 | tf_op jit(solution)/shard_map/ppermute | solution.py:290
  44.6 5.8 %collective-permute-start.17 = (bf16[32,2176]{1,0:T(8,128)(2,1)S(1)}, bf16[32,2176]{1,0:T(8,128)(2,1)S(1)}, u32[]{:S(2)}, u32[]{:S(2)}) collective-permute-start(bf16[32,2176]{1,0:T(8,128)(2,1)S(1)} %slice.70), channel_id=1, source_target_pairs={{0,2},{2,0},{1,3},{3,1},{4,6},{6,4},{5,7},{7,5},{8,10},{10,8},{9,1... | collective-permute-start | bytes 417800 | tf_op jit(solution)/shard_map/ppermute | solution.py:290
  46.2 6.0 %collective-permute-start.13 = (bf16[128,2176]{1,0:T(8,128)(2,1)S(1)}, bf16[128,2176]{1,0:T(8,128)(2,1)S(1)}, u32[]{:S(2)}, u32[]{:S(2)}) collective-permute-start(bf16[128,2176]{1,0:T(8,128)(2,1)S(1)} %slice.41), channel_id=1, source_target_pairs={{0,1},{1,0},{2,3},{3,2},{4,5},{5,4},{6,7},{7,6},{8,9},{9,8},{10,11... | collective-permute-start | bytes 1671176 | tf_op jit(solution)/shard_map/ppermute | solution.py:290
  50.4 3.5 %collective-permute-start.18 = (bf16[64,2176]{1,0:T(8,128)(2,1)S(1)}, bf16[64,2176]{1,0:T(8,128)(2,1)S(1)}, u32[]{:S(2)}, u32[]{:S(2)}) collective-permute-start(bf16[64,2176]{1,0:T(8,128)(2,1)S(1)} %get-tuple-element.63), channel_id=1, source_target_pairs={{0,1},{1,0},{2,3},{3,2},{4,5},{5,4},{6,7},{7,6},{8,9},{9,8},{10,11... | collective-permute-start | bytes 835592 | tf_op jit(solution)/shard_map/ppermute | solution.py:290
  50.5 10.7 %collective-permute-start.20 = (bf16[32,2176]{1,0:T(8,128)(2,1)S(1)}, bf16[32,2176]{1,0:T(8,128)(2,1)S(1)}, u32[]{:S(2)}, u32[]{:S(2)}) collective-permute-start(bf16[32,2176]{1,0:T(8,128)(2,1)S(1)} %slice_add_fusion.2), channel_id=1, source_target_pairs={{0,8},{4,12},{8,0},{12,4},{1,9},{5,13},{9,1},{13,5},{2,10},{6,14},... | collective-permute-start | bytes 417800 | tf_op jit(solution)/shard_map/ppermute | solution.py:294
  52.4 6.6 %collective-permute-start.22 = (bf16[32,2176]{1,0:T(8,128)(2,1)S(1)}, bf16[32,2176]{1,0:T(8,128)(2,1)S(1)}, u32[]{:S(2)}, u32[]{:S(2)}) collective-permute-start(bf16[32,2176]{1,0:T(8,128)(2,1)S(1)} %get-tuple-element.85), channel_id=1, source_target_pairs={{0,2},{2,0},{1,3},{3,1},{4,6},{6,4},{5,7},{7,5},{8,10},{10,8},{9,1... | collective-permute-start | bytes 417800 | tf_op jit(solution)/shard_map/ppermute | solution.py:290
  54.0 7.1 %collective-permute-start.19 = (bf16[32,2176]{1,0:T(8,128)(2,1)S(1)}, bf16[32,2176]{1,0:T(8,128)(2,1)S(1)}, u32[]{:S(2)}, u32[]{:S(2)}) collective-permute-start(bf16[32,2176]{1,0:T(8,128)(2,1)S(1)} %slice.69), channel_id=1, source_target_pairs={{0,2},{2,0},{1,3},{3,1},{4,6},{6,4},{5,7},{7,5},{8,10},{10,8},{9,1... | collective-permute-start | bytes 417800 | tf_op jit(solution)/shard_map/ppermute | solution.py:290
  59.0 9.1 %collective-permute-start.23 = (bf16[32,2176]{1,0:T(8,128)(2,1)S(1)}, bf16[32,2176]{1,0:T(8,128)(2,1)S(1)}, u32[]{:S(2)}, u32[]{:S(2)}) collective-permute-start(bf16[32,2176]{1,0:T(8,128)(2,1)S(1)} %get-tuple-element.83), channel_id=1, source_target_pairs={{0,4},{4,0},{8,12},{12,8},{1,5},{5,1},{9,13},{13,9},{2,6},{6,2},{1... | collective-permute-start | bytes 417800 | tf_op jit(solution)/shard_map/ppermute | solution.py:294
  61.2 7.0 %collective-permute-start.24 = (bf16[32,2176]{1,0:T(8,128)(2,1)S(1)}, bf16[32,2176]{1,0:T(8,128)(2,1)S(1)}, u32[]{:S(2)}, u32[]{:S(2)}) collective-permute-start(bf16[32,2176]{1,0:T(8,128)(2,1)S(1)} %slice_add_fusion.1), channel_id=1, source_target_pairs={{0,12},{4,8},{8,4},{12,0},{1,13},{5,9},{9,5},{13,1},{2,14},{6,10},... | collective-permute-start | bytes 417800 | tf_op jit(solution)/shard_map/ppermute | solution.py:294
  62.8 5.4 %collective-permute-start.21 = (bf16[32,2176]{1,0:T(8,128)(2,1)S(1)}, bf16[32,2176]{1,0:T(8,128)(2,1)S(1)}, u32[]{:S(2)}, u32[]{:S(2)}) collective-permute-start(bf16[32,2176]{1,0:T(8,128)(2,1)S(1)} %get-tuple-element.65), channel_id=1, source_target_pairs={{0,2},{2,0},{1,3},{3,1},{4,6},{6,4},{5,7},{7,5},{8,10},{10,8},{9,1... | collective-permute-start | bytes 417800 | tf_op jit(solution)/shard_map/ppermute | solution.py:290
  64.2 4.0 %copy-start.1 = (s32[32,8]{0,1:T(8,128)S(1)}, s32[32,8]{0,1:T(8,128)}, u32[]{:S(2)}) copy-start(s32[32,8]{0,1:T(8,128)} %param.9) | copy-start | bytes 3076

commit v4 on v3

--- a/solution.py
+++ b/solution.py
@@ -10,6 +10,7 @@
 F32 = jnp.float32
 BF16 = jnp.bfloat16
 SIDE = 128
+FOLD = 16
 NT = (((1,), (1,)), ((), ()))
 TN = (((0,), (0,)), ((), ()))
 MIB = 1024 * 1024
@@ -41,16 +42,17 @@
 def pack_kernel(x_ref, e_ref, routes_ref, weight_ref, out_ref, routes_held, weight_held, sems):
     tok_count, width = x_ref.shape
     top_count = routes_ref.shape[0]
+    folds = tok_count // FOLD
     copies = [
         pltpu.make_async_copy(routes_ref, routes_held, sems.at[0]),
         pltpu.make_async_copy(weight_ref, weight_held, sems.at[1]),
-        pltpu.make_async_copy(x_ref, out_ref.at[pl.ds(0, tok_count), pl.ds(0, width)], sems.at[2]),
-        pltpu.make_async_copy(e_ref, out_ref.at[pl.ds(tok_count, tok_count), pl.ds(0, width)], sems.at[3]),
     ]
+    for i in range(2 * folds):
+        source = (x_ref, e_ref)[i // folds].at[pl.ds(i % folds * FOLD, FOLD)]
+        copies.append(pltpu.make_async_copy(source, out_ref.at[:, pl.ds(i * width, width)], sems.at[2 + i]))
     for copy in copies:
         copy.start()
-    out_ref[tok_count:, width:] = jnp.zeros((tok_count, SIDE), BF16)
-    lane = lax.broadcasted_iota(jnp.int32, (tok_count, SIDE), 1)
+    lane = lax.broadcasted_iota(jnp.int32, (FOLD, SIDE), 1)
     expert = lax.rem(lax.broadcasted_iota(jnp.int32, (SIDE, tok_count), 0), top_count)
     copies[0].wait()
     copies[1].wait()
@@ -59,23 +61,29 @@
     table = jnp.zeros((SIDE, tok_count), F32)
     for k in range(top_count):
         table += jnp.where(routes[k : k + 1, :] == expert, weight[k : k + 1, :], 0.0)
-    out_ref[:tok_count, width:] = split_columns(table.T, top_count, lane)
-    copies[2].wait()
-    copies[3].wait()
+    table = table.T
+    side = jnp.zeros((FOLD, SIDE), BF16)
+    for i in range(folds):
+        here = split_columns(table[i * FOLD : (i + 1) * FOLD], top_count, lane - 2 * i * top_count)
+        side = jnp.where(lane < 2 * i * top_count, side, here)
+    out_ref[:, 2 * folds * width :] = side
+    for copy in copies[2:]:
+        copy.wait()
 
 
 def pack(x, e, routes, weight):
     tok_count, width = x.shape
     top_count = routes.shape[1]
+    blocks = 2 * tok_count // FOLD
     return pl.pallas_call(
         pack_kernel,
         in_specs=in_hbm(4),
         out_specs=in_vmem(1)[0],
-        out_shape=pltpu.VMEM((2 * tok_count, width + SIDE), BF16),
+        out_shape=pltpu.VMEM((FOLD, blocks * width + SIDE), BF16),
         scratch_shapes=[
             pltpu.VMEM((top_count, tok_count), jnp.int32),
             pltpu.VMEM((top_count, tok_count), F32),
-            pltpu.SemaphoreType.DMA((4,)),
+            pltpu.SemaphoreType.DMA((2 + blocks,)),
         ],
         compiler_params=pltpu.CompilerParams(vmem_limit_bytes=4 * MIB),
         name="pack_tokens",
@@ -113,39 +121,66 @@
     )(*left(gate_w, up_w))
 
 
-def rows_kernel(shards, experts, expert_ref, *refs):
+def rows_kernel(shards, experts, first, expert_ref, *refs):
     shard_refs = refs[:shards]
-    wide_ref, down_ref, keep_ref, send_ref, xe_ref, diff_ref, tall_ref, table_ref, sems = refs[shards:]
-    tok_count = shard_refs[0].shape[0] // 2
-    rows = shards * tok_count
+    wide_ref, down_ref, keep_ref, send_ref, xe_ref, diff_ref = refs[shards : shards + 6]
+    width = xe_ref.shape[1]
+    rows = xe_ref.shape[0] // 2
+    tok_count = rows // shards
+    folds = tok_count // FOLD
     half = rows // 2
-    hidden, width = tall_ref.shape
-    pieces = 4
-    block = hidden // pieces
-    down_copies = [
-        (down_ref.at[0, pl.ds(i * block, block)], tall_ref.at[pl.ds(i * block, block)]) for i in range(pieces)
-    ]
-    x_copies, e_copies = [], []
-    for i, ref in enumerate(shard_refs):
-        here = pl.ds(i * tok_count, tok_count)
-        x_copies.append((ref.at[pl.ds(0, tok_count), pl.ds(0, width)], xe_ref.at[here]))
-        e_copies.append(
-            (ref.at[pl.ds(tok_count, tok_count), pl.ds(0, width)], xe_ref.at[pl.ds(rows + i * tok_count, tok_count)])
-        )
-        e_copies.append((ref.at[pl.ds(0, tok_count), pl.ds(width, SIDE)], table_ref.at[here]))
-    copies = [
-        pltpu.make_async_copy(src, dst, sems.at[i]) for i, (src, dst) in enumerate(x_copies + down_copies + e_copies)
-    ]
-    for copy in copies:
-        copy.start()
+    hidden = diff_ref.shape[1] // 3
     chosen = expert_ref[:1, :] != 0
-    for copy in copies[:shards]:
-        copy.wait()
-    pre = jnp.dot(xe_ref[:rows, :], wide_ref[...], preferred_element_type=F32)
-    for copy in copies[shards:]:
-        copy.wait()
-    weight = jnp.sum(jnp.where(chosen, table_ref[...].astype(F32), 0.0), axis=1, keepdims=True)
-    back = lax.dot_general(xe_ref[rows:, :], tall_ref[...], NT, preferred_element_type=F32)
+    lane = lax.broadcasted_iota(jnp.int32, (1, SIDE), 1)
+    if first:
+        tall_ref, table_ref, sems = refs[shards + 6 :]
+        pieces = 4
+        block = hidden // pieces
+        copies = []
+        for i, ref in enumerate(shard_refs):
+            for j in range(folds):
+                here = pl.ds(i * tok_count + j * FOLD, FOLD)
+                copies.append((ref.at[:, pl.ds(j * width, width)], xe_ref.at[here]))
+        count = len(copies)
+        for i in range(pieces):
+            here = pl.ds(i * block, block)
+            copies.append((down_ref.at[0, here], tall_ref.at[here]))
+        for i, ref in enumerate(shard_refs):
+            for j in range(folds):
+                here = pl.ds(rows + i * tok_count + j * FOLD, FOLD)
+                copies.append((ref.at[:, pl.ds((folds + j) * width, width)], xe_ref.at[here]))
+            copies.append((ref.at[:, pl.ds(2 * folds * width, SIDE)], table_ref.at[pl.ds(i * FOLD, FOLD)]))
+        copies = [pltpu.make_async_copy(src, dst, sems.at[i]) for i, (src, dst) in enumerate(copies)]
+        for copy in copies:
+            copy.start()
+        for copy in copies[:count]:
+            copy.wait()
+        pre = jnp.dot(xe_ref[:rows, :], wide_ref[...], preferred_element_type=F32)
+        for copy in copies[count:]:
+            copy.wait()
+        e = xe_ref[rows:, :]
+        table = table_ref[...].astype(F32)
+    else:
+        tall_ref = down_ref
+
+        def pick(start):
+            return jnp.concatenate(
+                [ref[:, (start + j) * width : (start + j + 1) * width] for ref in shard_refs for j in range(folds)], axis=0
+            )
+
+        x, e = pick(0), pick(folds)
+        xe_ref[:rows, :] = x
+        xe_ref[rows:, :] = e
+        pre = jnp.dot(x, wide_ref[...], preferred_element_type=F32)
+        table = jnp.concatenate([ref[:, 2 * folds * width :] for ref in shard_refs], axis=0).astype(F32)
+    weights = []
+    for j in range(folds):
+        mine = chosen & (lane >= 2 * j * experts) & (lane < 2 * (j + 1) * experts)
+        weights.append(jnp.sum(jnp.where(mine, table, 0.0), axis=1, keepdims=True))
+    weight = jnp.concatenate(
+        [weights[j][i * FOLD : (i + 1) * FOLD] for i in range(shards) for j in range(folds)], axis=0
+    )
+    back = lax.dot_general(e, tall_ref[...], NT, preferred_element_type=F32)
     pre_gate, pre_up = pre[:, :hidden], pre[:, hidden:]
     sig = jax.nn.sigmoid(pre_gate)
     silu = pre_gate * sig
@@ -168,32 +203,35 @@
     send_ref[:, width:] = side[half:]
 
 
-def expert_rows_chunk(name, shards, experts, expert_info, weights):
+def expert_rows_chunk(name, shards, tok_count, experts, expert_info, weights):
     count = len(shards)
-    tok_count = shards[0].shape[0] // 2
-    wide = shards[0].shape[1]
-    width = wide - SIDE
+    first = weights[1].ndim == 3
+    width = (shards[0].shape[1] - SIDE) * FOLD // (2 * tok_count)
     rows = count * tok_count
-    hidden = weights[1].shape[1]
+    hidden = weights[0].shape[1] // 2
+    out_shape = [
+        pltpu.VMEM((rows // 2, width + SIDE), F32),
+        pltpu.VMEM((rows // 2, width + SIDE), BF16),
+        pltpu.VMEM((2 * rows, width), BF16),
+        pltpu.VMEM((rows, 3 * hidden), BF16),
+    ]
+    scratch_shapes = []
+    if first:
+        out_shape.append(pltpu.VMEM((hidden, width), BF16))
+        scratch_shapes = [
+            pltpu.VMEM((count * FOLD, SIDE), BF16),
+            pltpu.SemaphoreType.DMA((count * (2 * tok_count // FOLD + 1) + 4,)),
+        ]
     return pl.pallas_call(
-        functools.partial(rows_kernel, count, experts),
-        in_specs=in_vmem(1) + in_hbm(count) + in_vmem(1) + in_hbm(1),
-        out_specs=in_vmem(4),
-        out_shape=[
-            pltpu.VMEM((rows // 2, wide), F32),
-            pltpu.VMEM((rows // 2, wide), BF16),
-            pltpu.VMEM((2 * rows, width), BF16),
-            pltpu.VMEM((rows, 3 * hidden), BF16),
-        ],
-        scratch_shapes=[
-            pltpu.VMEM((hidden, width), BF16),
-            pltpu.VMEM((rows, SIDE), BF16),
-            pltpu.SemaphoreType.DMA((3 * count + 4,)),
-        ],
+        functools.partial(rows_kernel, count, experts, first),
+        in_specs=in_vmem(1) + (in_hbm(count) + in_vmem(1) + in_hbm(1) if first else in_vmem(count + 2)),
+        out_specs=in_vmem(len(out_shape)),
+        out_shape=out_shape,
+        scratch_shapes=scratch_shapes,
         compiler_params=pltpu.CompilerParams(vmem_limit_bytes=16 * MIB),
         cost_estimate=pl.CostEstimate(flops=1, bytes_accessed=1, transcendentals=0),
         name=name,
-    )(expert_info, *(left(*shards) if count > 4 else shards), weights[0], *left(weights[1]))
+    )(expert_info, *(left(*shards) if first else shards), weights[0], *(left(weights[1]) if first else (weights[1],)))
 
 
 def grads_kernel(parts, *refs):
@@ -306,7 +344,7 @@
     lines = lax.axis_size("expert")
     expert = lax.axis_index("expert") * lax.axis_size("dp") + lax.axis_index("dp")
     lane = lax.broadcasted_iota(jnp.int32, (8, SIDE), 1)
-    expert_info = ((lane == expert) | (lane == expert + top_count)).astype(jnp.int32)
+    expert_info = (lax.rem(lane, top_count) == expert).astype(jnp.int32)
     packed = pack(layer_input, output_grad, routes, routing_weight)
     columns, across = {}, {}
     gate_w, up_w, packed = together(gate_proj, up_proj, packed)
@@ -320,11 +358,12 @@
     across[1] = swap(columns[1], "dp")
     columns[3], across[1], across[2] = together(columns[3], across[1], across[2])
     across[3] = swap(columns[3], "dp")
-    weights = (wide_w, down_proj)
 
     shards = [columns[2], across[2], columns[1], columns[0], across[1], across[0]]
     shards += [swap(shard, "sub") for shard in shards]
-    keep, send, xe_0, diff_0 = expert_rows_chunk("rows_0", shards, top_count, expert_info, weights)
+    keep, send, xe_0, diff_0, tall_w = expert_rows_chunk(
+        "rows_0", shards, tok_count, top_count, expert_info, (wide_w, down_proj)
+    )
     diff_0, columns[3], across[3] = together(diff_0, columns[3], across[3])
     send, across[3] = together(send, across[3])
     rows = tok_count
@@ -335,18 +374,21 @@
 
     shards = [columns[3], across[3]]
     shards += [swap(shard, "sub") for shard in shards]
-    keep, send, xe_3, diff_3 = expert_rows_chunk("rows_3", shards, top_count, expert_info, weights)
+    keep, send, xe_3, diff_3 = expert_rows_chunk(
+        "rows_3", shards, tok_count, top_count, expert_info, (wide_w, tall_w)
+    )
     send, home_2 = together(send, home_2)
     back_2 = far(home_2.astype(BF16), "expert", 2)
     paired_3 = keep + swap(send, "sub").astype(F32)
+    paired_3, away_1, diff_3 = together(paired_3, away_1, diff_3)
     home_3 = paired_3[:rows] + swap(paired_3[rows:].astype(BF16), "dp").astype(F32)
+    gate_grads, up_grads, down_grads = weight_grads((xe_0, xe_3), (diff_0, diff_3))
     home_1 = paired_10[:rows] + swap(away_1, "dp").astype(F32)
-    home_3, away_0, back_2 = together(home_3, away_0, back_2)
+    home_3, gate_grads = together(home_3, gate_grads)
+    home_1, away_0 = together(home_1, away_0)
+    back_3 = far(home_3.astype(BF16), "expert", 3)
     back_0 = swap(away_0, "dp")
-    back_3 = far(home_3.astype(BF16), "expert", 3)
     back_1 = far(home_1.astype(BF16), "expert", 1)
-    gate_grads, up_grads, down_grads = weight_grads((xe_0, xe_3), (diff_0, diff_3))
-    gate_grads, back_1, back_2, back_3 = together(gate_grads, back_1, back_2, back_3)
     arrived = (back_0, back_1, back_2, back_3)
     input_grad, routing_grad = finish(paired_10[rows : 2 * rows], arrived, routes)
     return (input_grad, routing_grad, gate_grads, up_grads, down_grads)
@@ -473,7 +515,8 @@
     args = (layer_input, output_grad, routes, routing_weight, gate_proj, up_proj, down_proj)
     lines = lax.axis_size("expert")
     pairs = lax.axis_size("dp") == 2 and lax.axis_size("sub") == 2 and lines & (lines - 1) == 0
-    if pairs and lines == 4 and 2 * lines == routes.shape[1] and gate_proj.shape[0] == 1:
+    fits = layer_input.shape[0] % FOLD == 0 and 2 * routes.shape[1] * layer_input.shape[0] <= FOLD * SIDE
+    if fits and pairs and lines == 4 and 2 * lines == routes.shape[1] and gate_proj.shape[0] == 1:
         return every_token_to_every_expert(*args)
     return chosen_experts(*args)
 

time: 69.2 us -> 68.7 us (level)
    ppermute x19, waiting for transfers between devices: 13.5 us -> 8.19 us  [swap(): return lax.ppermute(value, axis, [(0, 1), (1, 0)])]
    ppermute x6, waiting for transfers between devices: 12.7 us -> 17.7 us  [far(): lax.ppermute(value, axis, [(i, i ^ distance) for i in range(lax.axis_size...]
  transfers between devices with their start and end apart: 25 -> 25, of which waited for: 12 -> 13; matrix products, arithmetic and copies ran while one was open for 1% -> 1% of each run, Pallas kernels for 23% -> 23%
where the time goes in v4:
time: 68.7 us; the launch traced here: 68.4 us
  waiting for transfers between devices  25.9 us (38%)
  starting transfers between devices  23.9 us (35%)
  Pallas kernels  17.3 us (25%)
  between operations  0.85 us (1%)
    ppermute x6, waiting for transfers between devices, far(): lax.ppermute(value, axis, [(i, i ^ distance) for i in range(lax.axis_size...  17.7 us
    ppermute x19, starting transfers between devices, swap(): return lax.ppermute(value, axis, [(0, 1), (1, 0)])  12.1 us
    ppermute x6, starting transfers between devices, far(): lax.ppermute(value, axis, [(i, i ^ distance) for i in range(lax.axis_size...  11.8 us
    pallas_call x2, Pallas kernels, expert_rows_chunk(): pl.pallas_call(functools.partial(rows_kernel, count, experts, first), in_...  9.69 us
    ppermute x19, waiting for transfers between devices, swap(): return lax.ppermute(value, axis, [(0, 1), (1, 0)])  8.19 us
    pallas_call x1, Pallas kernels, weight_grads(): pl.pallas_call(functools.partial(grads_kernel, count), in_specs=in_vmem(2...  3.93 us
    pallas_call x1, Pallas kernels, stage(): pl.pallas_call(stage_kernel, in_specs=in_hbm(2), out_specs=in_vmem(1)[0],...  1.89 us
  transfers between devices with their start and end apart: 25, of which 13 were waited for; matrix products, arithmetic and copies ran while one was open for 1% of the time, Pallas kernels for 23%

profile of v4, /device:TPU:0, one launch (start us, length us, event | category | flops | bytes accessed | tf_op | source)
XLA Modules:
  0.0 68.4 jit_solution(6895696539031858574)
XLA Ops:
  0.6 1.0 %pack_tokens.1.refs_3_ = bf16[16,8320]{1,0:T(8,128)(2,1)S(1)} custom-call(bf16[32,2048]{1,0:T(8,128)(2,1)} %x_ref.1, bf16[32,2048]{1,0:T(8,128)(2,1)} %e_ref.1, s32[8,32]{1,0:T(8,128)} %bitcast.3, f32[8,32]{1,0:T(8,128)} %bitcast.5), custom_call_target="tpu_custom_call" | custom-call | tf_op jit(solution)/shard_map/pack_tokens/pallas_call | solution.py:78
  1.7 3.1 %collective-permute-start = (bf16[16,8320]{1,0:T(8,128)(2,1)S(1)}, bf16[16,8320]{1,0:T(8,128)(2,1)S(1)}, u32[]{:S(2)}, u32[]{:S(2)}) collective-permute-start(bf16[16,8320]{1,0:T(8,128)(2,1)S(1)} %pack_tokens.1.refs_3_), channel_id=1, source_target_pairs={{0,4},{4,0},{8,12},{12,8},{1,5},{5,1},{9,13},{13,9},{2,6},{6,2},{1... | collective-permute-start | bytes 798728 | tf_op jit(solution)/shard_map/ppermute | solution.py:332
  4.8 2.6 %collective-permute-start.1 = (bf16[16,8320]{1,0:T(8,128)(2,1)S(1)}, bf16[16,8320]{1,0:T(8,128)(2,1)S(1)}, u32[]{:S(2)}, u32[]{:S(2)}) collective-permute-start(bf16[16,8320]{1,0:T(8,128)(2,1)S(1)} %pack_tokens.1.refs_3_), channel_id=1, source_target_pairs={{0,8},{4,12},{8,0},{12,4},{1,9},{5,13},{9,1},{13,5},{2,10},{6,14},... | collective-permute-start | bytes 798728 | tf_op jit(solution)/shard_map/ppermute | solution.py:332
  7.4 1.5 %collective-permute-start.2 = (bf16[16,8320]{1,0:T(8,128)(2,1)S(1)}, bf16[16,8320]{1,0:T(8,128)(2,1)}, u32[]{:S(2)}, u32[]{:S(2)}) collective-permute-start(bf16[16,8320]{1,0:T(8,128)(2,1)S(1)} %pack_tokens.1.refs_3_), channel_id=1, source_target_pairs={{0,2},{2,0},{1,3},{3,1},{4,6},{6,4},{5,7},{7,5},{8,10},{10,8},{9,1... | collective-permute-start | bytes 798728 | tf_op jit(solution)/shard_map/ppermute | solution.py:328
  8.8 1.9 %stage_weights.1.refs_12_.refs_4_ = bf16[2048,768]{1,0:T(8,128)(2,1)S(1)} custom-call(bf16[1,2048,384]{2,1,0:T(8,128)(2,1)} %gate_ref, bf16[1,2048,384]{2,1,0:T(8,128)(2,1)} %up_ref), custom_call_target="tpu_custom_call" | custom-call | flops 1 | bytes 1 | tf_op jit(solution)/shard_map/stage_weights/pallas_call | solution.py:112
  10.7 6.0 %collective-permute-done.refs_2_ = bf16[16,8320]{1,0:T(8,128)(2,1)S(1)} collective-permute-done((bf16[16,8320]{1,0:T(8,128)(2,1)S(1)}, bf16[16,8320]{1,0:T(8,128)(2,1)S(1)}, u32[]{:S(2)}, u32[]{:S(2)}) %collective-permute-start) | collective-permute-done | bytes 266272 | tf_op jit(solution)/shard_map/ppermute | solution.py:332
  16.7 2.5 %collective-permute-done.1.refs_0_ = bf16[16,8320]{1,0:T(8,128)(2,1)S(1)} collective-permute-done((bf16[16,8320]{1,0:T(8,128)(2,1)S(1)}, bf16[16,8320]{1,0:T(8,128)(2,1)S(1)}, u32[]{:S(2)}, u32[]{:S(2)}) %collective-permute-start.1) | collective-permute-done | bytes 266272 | tf_op jit(solution)/shard_map/ppermute | solution.py:332
  19.3 2.5 %collective-permute-start.3 = (bf16[16,8320]{1,0:T(8,128)(2,1)S(1)}, bf16[16,8320]{1,0:T(8,128)(2,1)}, u32[]{:S(2)}, u32[]{:S(2)}) collective-permute-start(bf16[16,8320]{1,0:T(8,128)(2,1)S(1)} %pack_tokens.1.refs_3_), channel_id=1, source_target_pairs={{0,12},{4,8},{8,4},{12,0},{1,13},{5,9},{9,5},{13,1},{2,14},{6,10},... | collective-permute-start | bytes 798728 | tf_op jit(solution)/shard_map/ppermute | solution.py:332
  21.7 1.5 %collective-permute-start.4 = (bf16[16,8320]{1,0:T(8,128)(2,1)S(1)}, bf16[16,8320]{1,0:T(8,128)(2,1)}, u32[]{:S(2)}, u32[]{:S(2)}) collective-permute-start(bf16[16,8320]{1,0:T(8,128)(2,1)S(1)} %collective-permute-done.refs_2_), channel_id=1, source_target_pairs={{0,2},{2,0},{1,3},{3,1},{4,6},{6,4},{5,7},{7,5},{8,10},{10,8},{9,1... | collective-permute-start | bytes 798728 | tf_op jit(solution)/shard_map/ppermute | solution.py:328
  23.2 0.5 collective-permute-start.5
  23.8 0.5 collective-permute-start.8
  24.3 3.4 %collective-permute-done.3.refs_0_ = bf16[16,8320]{1,0:T(8,128)(2,1)} collective-permute-done((bf16[16,8320]{1,0:T(8,128)(2,1)S(1)}, bf16[16,8320]{1,0:T(8,128)(2,1)}, u32[]{:S(2)}, u32[]{:S(2)}) %collective-permute-start.3) | collective-permute-done | bytes 266272 | tf_op jit(solution)/shard_map/ppermute | solution.py:332
  27.7 1.7 %collective-permute-done.4.refs_4_ = bf16[16,8320]{1,0:T(8,128)(2,1)} collective-permute-done((bf16[16,8320]{1,0:T(8,128)(2,1)S(1)}, bf16[16,8320]{1,0:T(8,128)(2,1)}, u32[]{:S(2)}, u32[]{:S(2)}) %collective-permute-start.4) | collective-permute-done | bytes 266272 | tf_op jit(solution)/shard_map/ppermute | solution.py:328
  29.4 2.8 %collective-permute-done.5.refs_1_ = bf16[16,8320]{1,0:T(8,128)(2,1)} collective-permute-done((bf16[16,8320]{1,0:T(8,128)(2,1)S(1)}, bf16[16,8320]{1,0:T(8,128)(2,1)}, u32[]{:S(2)}, u32[]{:S(2)}) %collective-permute-start.5) | collective-permute-done | bytes 266272 | tf_op jit(solution)/shard_map/ppermute | solution.py:328
  32.3 0.5 collective-permute-start.7
  32.8 1.6 %collective-permute-start.12 = (bf16[16,8320]{1,0:T(8,128)(2,1)}, bf16[16,8320]{1,0:T(8,128)(2,1)}, u32[]{:S(2)}, u32[]{:S(2)}) collective-permute-start(bf16[16,8320]{1,0:T(8,128)(2,1)} %collective-permute-done.3.refs_0_), channel_id=1, source_target_pairs={{0,2},{2,0},{1,3},{3,1},{4,6},{6,4},{5,7},{7,5},{8,10},{10,8},{9,1... | collective-permute-start | bytes 798728 | tf_op jit(solution)/shard_map/ppermute | solution.py:328
  34.5 6.5 %rows_0.1 = (f32[192,2176]{1,0:T(8,128)S(1)}, bf16[192,2176]{1,0:T(8,128)(2,1)S(1)}, bf16[768,2048]{1,0:T(8,128)(2,1)S(1)}, bf16[384,1152]{1,0:T(8,128)(2,1)S(1)}, bf16[384,2048]{1,0:T(8,128)(2,1)S(1)}) custom-call(s32[8,128]{1,0:T(8,128)S(1)} %iota.7.expert_ref, bf16[16,8320]{1,0:T(8,128)(2,1)} %copy-done.3, ...), custom_call_target="tpu_custom_call" | custom-call | flops 1 | bytes 1 | tf_op jit(solution)/shard_map/rows_0/pallas_call | solution.py:225
  42.2 1.0 %collective-permute-done.16 = bf16[64,2176]{1,0:T(8,128)(2,1)S(1)} collective-permute-done((bf16[64,2176]{1,0:T(8,128)(2,1)S(1)}, bf16[64,2176]{1,0:T(8,128)(2,1)S(1)}, u32[]{:S(2)}, u32[]{:S(2)}) %collective-permute-start.16) | collective-permute-done | bytes 278560 | tf_op jit(solution)/shard_map/ppermute | solution.py:328
  43.3 1.6 %collective-permute-start.17 = (bf16[32,2176]{1,0:T(8,128)(2,1)S(1)}, bf16[32,2176]{1,0:T(8,128)(2,1)S(1)}, u32[]{:S(2)}, u32[]{:S(2)}) collective-permute-start(bf16[32,2176]{1,0:T(8,128)(2,1)S(1)} %slice.67), channel_id=1, source_target_pairs={{0,2},{2,0},{1,3},{3,1},{4,6},{6,4},{5,7},{7,5},{8,10},{10,8},{9,1... | collective-permute-start | bytes 417800 | tf_op jit(solution)/shard_map/ppermute | solution.py:328
  45.0 3.2 %rows_3.1 = (f32[64,2176]{1,0:T(8,128)S(1)}, bf16[64,2176]{1,0:T(8,128)(2,1)S(1)}, bf16[256,2048]{1,0:T(8,128)(2,1)S(1)}, bf16[128,1152]{1,0:T(8,128)(2,1)S(1)}) custom-call(s32[8,128]{1,0:T(8,128)S(1)} %iota.7.expert_ref, bf16[16,8320]{1,0:T(8,128)(2,1)} %collective-permute-done.3.refs_0_, bf16[16,8320]{1,0:T(8,128)(2,1)} %collective-permute-done.12.refs_1_, ...), custom_call_target="tpu_custom_call" | custom-call | flops 1 | bytes 1 | tf_op jit(solution)/shard_map/rows_3/pallas_call | solution.py:225
  48.1 0.9 %collective-permute-done.17 = bf16[32,2176]{1,0:T(8,128)(2,1)S(1)} collective-permute-done((bf16[32,2176]{1,0:T(8,128)(2,1)S(1)}, bf16[32,2176]{1,0:T(8,128)(2,1)S(1)}, u32[]{:S(2)}, u32[]{:S(2)}) %collective-permute-start.17) | collective-permute-done | bytes 139296 | tf_op jit(solution)/shard_map/ppermute | solution.py:328
  49.2 1.7 %collective-permute-start.22 = (bf16[32,2176]{1,0:T(8,128)(2,1)S(1)}, bf16[32,2176]{1,0:T(8,128)(2,1)S(1)}, u32[]{:S(2)}, u32[]{:S(2)}) collective-permute-start(bf16[32,2176]{1,0:T(8,128)(2,1)S(1)} %slice_add_fusion), channel_id=1, source_target_pairs={{0,8},{4,12},{8,0},{12,4},{1,9},{5,13},{9,1},{13,5},{2,10},{6,14},... | collective-permute-start | bytes 417800 | tf_op jit(solution)/shard_map/ppermute | solution.py:332
  51.2 1.6 %collective-permute-start.23 = (bf16[32,2176]{1,0:T(8,128)(2,1)S(1)}, bf16[32,2176]{1,0:T(8,128)(2,1)S(1)}, u32[]{:S(2)}, u32[]{:S(2)}) collective-permute-start(bf16[32,2176]{1,0:T(8,128)(2,1)S(1)} %slice.66), channel_id=1, source_target_pairs={{0,2},{2,0},{1,3},{3,1},{4,6},{6,4},{5,7},{7,5},{8,10},{10,8},{9,1... | collective-permute-start | bytes 417800 | tf_op jit(solution)/shard_map/ppermute | solution.py:328
  52.7 0.5 collective-permute-start.19
  53.3 3.9 %weight_grads.1 = (bf16[1,2048,384]{2,1,0:T(8,128)(2,1)}, bf16[1,2048,384]{2,1,0:T(8,128)(2,1)}, bf16[1,384,2048]{2,1,0:T(8,128)(2,1)}) custom-call(bf16[768,2048]{1,0:T(8,128)(2,1)S(1)} %get-tuple-element.72.refs_0_, bf16[256,2048]{1,0:T(8,128)(2,1)S(1)} %get-tuple-element.73.refs_1_, bf16[384,1152]{1,0:T(8,128)(2,1)S(1)} %get-tuple-element.74.refs_2_, ...), custom_call_target="tpu_custom_call" | custom-call | flops 2415919104 | bytes 8912896 | tf_op jit(solution)/shard_map/weight_grads/pallas_call | solution.py:271
  57.2 0.5 collective-permute-done.23
  57.8 1.6 %collective-permute-start.24 = (bf16[32,2176]{1,0:T(8,128)(2,1)S(1)}, bf16[32,2176]{1,0:T(8,128)(2,1)S(1)}, u32[]{:S(2)}, u32[]{:S(2)}) collective-permute-start(bf16[32,2176]{1,0:T(8,128)(2,1)S(1)} %convert_add_fusion.3), channel_id=1, source_target_pairs={{0,12},{4,8},{8,4},{12,0},{1,13},{5,9},{9,5},{13,1},{2,14},{6,10},... | collective-permute-start | bytes 417800 | tf_op jit(solution)/shard_map/ppermute | solution.py:332
  59.4 0.6 collective-permute-done.19
  60.0 1.6 %collective-permute-start.20 = (bf16[32,2176]{1,0:T(8,128)(2,1)S(1)}, bf16[32,2176]{1,0:T(8,128)(2,1)S(1)}, u32[]{:S(2)}, u32[]{:S(2)}) collective-permute-start(bf16[32,2176]{1,0:T(8,128)(2,1)S(1)} %get-tuple-element.68), channel_id=1, source_target_pairs={{0,2},{2,0},{1,3},{3,1},{4,6},{6,4},{5,7},{7,5},{8,10},{10,8},{9,1... | collective-permute-start | bytes 417800 | tf_op jit(solution)/shard_map/ppermute | solution.py:328
  61.9 3.7 %collective-permute-done.24.refs_3_ = bf16[32,2176]{1,0:T(8,128)(2,1)S(1)} collective-permute-done((bf16[32,2176]{1,0:T(8,128)(2,1)S(1)}, bf16[32,2176]{1,0:T(8,128)(2,1)S(1)}, u32[]{:S(2)}, u32[]{:S(2)}) %collective-permute-start.24) | collective-permute-done | bytes 139296 | tf_op jit(solution)/shard_map/ppermute | solution.py:332
  65.6 2.1 %collective-permute-done.21.refs_1_ = bf16[32,2176]{1,0:T(8,128)(2,1)S(1)} collective-permute-done((bf16[32,2176]{1,0:T(8,128)(2,1)S(1)}, bf16[32,2176]{1,0:T(8,128)(2,1)S(1)}, u32[]{:S(2)}, u32[]{:S(2)}) %collective-permute-start.21) | collective-permute-done | bytes 139296 | tf_op jit(solution)/shard_map/ppermute | solution.py:332
  67.7 0.8 %finish.1 = (bf16[32,2048]{1,0:T(8,128)(2,1)}, f32[8,32]{1,0:T(8,128)}) custom-call(f32[32,2176]{1,0:T(8,128)S(1)} %slice.52.own_ref, bf16[32,2176]{1,0:T(8,128)(2,1)S(1)} %collective-permute-done.20.refs_0_, bf16[32,2176]{1,0:T(8,128)(2,1)S(1)} %collective-permute-done.21.refs_1_, bf16[32,2176]{1,0:T(8,128)(2,1)S(1)} %collective-permute-done.22.refs_2_, ...), custom_call_target="tpu_custom_call" | custom-call | tf_op jit(solution)/shard_map/finish/pallas_call | solution.py:313
  (50 shorter events, 2.3 us)
Async XLA Ops:
  1.7 26.0 %copy-start = (bf16[16,8320]{1,0:T(8,128)(2,1)}, bf16[16,8320]{1,0:T(8,128)(2,1)S(1)}, u32[]{:S(2)}) copy-start(bf16[16,8320]{1,0:T(8,128)(2,1)S(1)} %pack_tokens.1.refs_3_) | copy-start | bytes 798724
  1.7 15.1 %collective-permute-start = (bf16[16,8320]{1,0:T(8,128)(2,1)S(1)}, bf16[16,8320]{1,0:T(8,128)(2,1)S(1)}, u32[]{:S(2)}, u32[]{:S(2)}) collective-permute-start(bf16[16,8320]{1,0:T(8,128)(2,1)S(1)} %pack_tokens.1.refs_3_), channel_id=1, source_target_pairs={{0,4},{4,0},{8,12},{12,8},{1,5},{5,1},{9,13},{13,9},{2,6},{6,2},{1... | collective-permute-start | bytes 798728 | tf_op jit(solution)/shard_map/ppermute | solution.py:332
  4.8 14.5 %collective-permute-start.1 = (bf16[16,8320]{1,0:T(8,128)(2,1)S(1)}, bf16[16,8320]{1,0:T(8,128)(2,1)S(1)}, u32[]{:S(2)}, u32[]{:S(2)}) collective-permute-start(bf16[16,8320]{1,0:T(8,128)(2,1)S(1)} %pack_tokens.1.refs_3_), channel_id=1, source_target_pairs={{0,8},{4,12},{8,0},{12,4},{1,9},{5,13},{9,1},{13,5},{2,10},{6,14},... | collective-permute-start | bytes 798728 | tf_op jit(solution)/shard_map/ppermute | solution.py:332
  7.4 11.9 %collective-permute-start.2 = (bf16[16,8320]{1,0:T(8,128)(2,1)S(1)}, bf16[16,8320]{1,0:T(8,128)(2,1)}, u32[]{:S(2)}, u32[]{:S(2)}) collective-permute-start(bf16[16,8320]{1,0:T(8,128)(2,1)S(1)} %pack_tokens.1.refs_3_), channel_id=1, source_target_pairs={{0,2},{2,0},{1,3},{3,1},{4,6},{6,4},{5,7},{7,5},{8,10},{10,8},{9,1... | collective-permute-start | bytes 798728 | tf_op jit(solution)/shard_map/ppermute | solution.py:328
  16.7 11.0 %copy-start.2 = (bf16[16,8320]{1,0:T(8,128)(2,1)}, bf16[16,8320]{1,0:T(8,128)(2,1)S(1)}, u32[]{:S(2)}) copy-start(bf16[16,8320]{1,0:T(8,128)(2,1)S(1)} %collective-permute-done.refs_2_) | copy-start | bytes 798724
  19.3 13.5 %copy-start.3 = (bf16[16,8320]{1,0:T(8,128)(2,1)}, bf16[16,8320]{1,0:T(8,128)(2,1)S(1)}, u32[]{:S(2)}) copy-start(bf16[16,8320]{1,0:T(8,128)(2,1)S(1)} %collective-permute-done.1.refs_0_) | copy-start | bytes 798724
  19.3 8.4 %collective-permute-start.3 = (bf16[16,8320]{1,0:T(8,128)(2,1)S(1)}, bf16[16,8320]{1,0:T(8,128)(2,1)}, u32[]{:S(2)}, u32[]{:S(2)}) collective-permute-start(bf16[16,8320]{1,0:T(8,128)(2,1)S(1)} %pack_tokens.1.refs_3_), channel_id=1, source_target_pairs={{0,12},{4,8},{8,4},{12,0},{1,13},{5,9},{9,5},{13,1},{2,14},{6,10},... | collective-permute-start | bytes 798728 | tf_op jit(solution)/shard_map/ppermute | solution.py:332
  21.7 7.7 %collective-permute-start.4 = (bf16[16,8320]{1,0:T(8,128)(2,1)S(1)}, bf16[16,8320]{1,0:T(8,128)(2,1)}, u32[]{:S(2)}, u32[]{:S(2)}) collective-permute-start(bf16[16,8320]{1,0:T(8,128)(2,1)S(1)} %collective-permute-done.refs_2_), channel_id=1, source_target_pairs={{0,2},{2,0},{1,3},{3,1},{4,6},{6,4},{5,7},{7,5},{8,10},{10,8},{9,1... | collective-permute-start | bytes 798728 | tf_op jit(solution)/shard_map/ppermute | solution.py:328
  23.2 9.0 %collective-permute-start.5 = (bf16[16,8320]{1,0:T(8,128)(2,1)S(1)}, bf16[16,8320]{1,0:T(8,128)(2,1)}, u32[]{:S(2)}, u32[]{:S(2)}) collective-permute-start(bf16[16,8320]{1,0:T(8,128)(2,1)S(1)} %collective-permute-done.1.refs_0_), channel_id=1, source_target_pairs={{0,2},{2,0},{1,3},{3,1},{4,6},{6,4},{5,7},{7,5},{8,10},{10,8},{9,1... | collective-permute-start | bytes 798728 | tf_op jit(solution)/shard_map/ppermute | solution.py:328
  23.8 8.5 %collective-permute-start.6 = (bf16[16,8320]{1,0:T(8,128)(2,1)S(1)}, bf16[16,8320]{1,0:T(8,128)(2,1)S(1)}, u32[]{:S(2)}, u32[]{:S(2)}) collective-permute-start(bf16[16,8320]{1,0:T(8,128)(2,1)S(1)} %collective-permute-done.1.refs_0_), channel_id=1, source_target_pairs={{0,1},{1,0},{2,3},{3,2},{4,5},{5,4},{6,7},{7,6},{8,9},{9,8},{10,11... | collective-permute-start | bytes 798728 | tf_op jit(solution)/shard_map/ppermute | solution.py:328
  23.8 9.0 %collective-permute-start.8 = (bf16[16,8320]{1,0:T(8,128)(2,1)S(1)}, bf16[16,8320]{1,0:T(8,128)(2,1)S(1)}, u32[]{:S(2)}, u32[]{:S(2)}) collective-permute-start(bf16[16,8320]{1,0:T(8,128)(2,1)S(1)} %collective-permute-done.refs_2_), channel_id=1, source_target_pairs={{0,1},{1,0},{2,3},{3,2},{4,5},{5,4},{6,7},{7,6},{8,9},{9,8},{10,11... | collective-permute-start | bytes 798728 | tf_op jit(solution)/shard_map/ppermute | solution.py:328
  27.7 6.7 %collective-permute-start.9 = (bf16[16,8320]{1,0:T(8,128)(2,1)S(1)}, bf16[16,8320]{1,0:T(8,128)(2,1)}, u32[]{:S(2)}, u32[]{:S(2)}) collective-permute-start(bf16[16,8320]{1,0:T(8,128)(2,1)S(1)} %pack_tokens.1.refs_3_), channel_id=1, source_target_pairs={{0,1},{1,0},{2,3},{3,2},{4,5},{5,4},{6,7},{7,6},{8,9},{9,8},{10,11... | collective-permute-start | bytes 798728 | tf_op jit(solution)/shard_map/ppermute | solution.py:328
  29.4 5.0 %collective-permute-start.11 = (bf16[16,8320]{1,0:T(8,128)(2,1)}, bf16[16,8320]{1,0:T(8,128)(2,1)}, u32[]{:S(2)}, u32[]{:S(2)}) collective-permute-start(bf16[16,8320]{1,0:T(8,128)(2,1)} %collective-permute-done.2.refs_5_), channel_id=1, source_target_pairs={{0,1},{1,0},{2,3},{3,2},{4,5},{5,4},{6,7},{7,6},{8,9},{9,8},{10,11... | collective-permute-start | bytes 798728 | tf_op jit(solution)/shard_map/ppermute | solution.py:328
  32.3 2.1 %collective-permute-start.10 = (bf16[16,8320]{1,0:T(8,128)(2,1)}, bf16[16,8320]{1,0:T(8,128)(2,1)}, u32[]{:S(2)}, u32[]{:S(2)}) collective-permute-start(bf16[16,8320]{1,0:T(8,128)(2,1)} %collective-permute-done.4.refs_4_), channel_id=1, source_target_pairs={{0,1},{1,0},{2,3},{3,2},{4,5},{5,4},{6,7},{7,6},{8,9},{9,8},{10,11... | collective-permute-start | bytes 798728 | tf_op jit(solution)/shard_map/ppermute | solution.py:328
  32.3 2.1 %copy-start.4 = (bf16[16,8320]{1,0:T(8,128)(2,1)}, bf16[16,8320]{1,0:T(8,128)(2,1)S(1)}, u32[]{:S(2)}) copy-start(bf16[16,8320]{1,0:T(8,128)(2,1)S(1)} %collective-permute-done.6.refs_6_) | copy-start | bytes 798724
  32.3 2.3 %collective-permute-start.7 = (bf16[16,8320]{1,0:T(8,128)(2,1)}, bf16[16,8320]{1,0:T(8,128)(2,1)}, u32[]{:S(2)}, u32[]{:S(2)}) collective-permute-start(bf16[16,8320]{1,0:T(8,128)(2,1)} %collective-permute-done.5.refs_1_), channel_id=1, source_target_pairs={{0,1},{1,0},{2,3},{3,2},{4,5},{5,4},{6,7},{7,6},{8,9},{9,8},{10,11... | collective-permute-start | bytes 798728 | tf_op jit(solution)/shard_map/ppermute | solution.py:328
  32.8 1.6 %copy-start.5 = (bf16[16,8320]{1,0:T(8,128)(2,1)}, bf16[16,8320]{1,0:T(8,128)(2,1)S(1)}, u32[]{:S(2)}) copy-start(bf16[16,8320]{1,0:T(8,128)(2,1)S(1)} %collective-permute-done.8.refs_8_) | copy-start | bytes 798724
  32.8 8.7 %collective-permute-start.12 = (bf16[16,8320]{1,0:T(8,128)(2,1)}, bf16[16,8320]{1,0:T(8,128)(2,1)}, u32[]{:S(2)}, u32[]{:S(2)}) collective-permute-start(bf16[16,8320]{1,0:T(8,128)(2,1)} %collective-permute-done.3.refs_0_), channel_id=1, source_target_pairs={{0,2},{2,0},{1,3},{3,1},{4,6},{6,4},{5,7},{7,5},{8,10},{10,8},{9,1... | collective-permute-start | bytes 798728 | tf_op jit(solution)/shard_map/ppermute | solution.py:328
  41.6 1.6 %collective-permute-start.16 = (bf16[64,2176]{1,0:T(8,128)(2,1)S(1)}, bf16[64,2176]{1,0:T(8,128)(2,1)S(1)}, u32[]{:S(2)}, u32[]{:S(2)}) collective-permute-start(bf16[64,2176]{1,0:T(8,128)(2,1)S(1)} %slice.45), channel_id=1, source_target_pairs={{0,1},{1,0},{2,3},{3,2},{4,5},{5,4},{6,7},{7,6},{8,9},{9,8},{10,11... | collective-permute-start | bytes 835592 | tf_op jit(solution)/shard_map/ppermute | solution.py:328
  41.6 3.3 %collective-permute-start.15 = (bf16[16,8320]{1,0:T(8,128)(2,1)}, bf16[16,8320]{1,0:T(8,128)(2,1)S(1)}, u32[]{:S(2)}, u32[]{:S(2)}) collective-permute-start(bf16[16,8320]{1,0:T(8,128)(2,1)} %collective-permute-done.12.refs_1_), channel_id=1, source_target_pairs={{0,1},{1,0},{2,3},{3,2},{4,5},{5,4},{6,7},{7,6},{8,9},{9,8},{10,11... | collective-permute-start | bytes 798728 | tf_op jit(solution)/shard_map/ppermute | solution.py:328
  42.1 2.8 %collective-permute-start.14 = (bf16[16,8320]{1,0:T(8,128)(2,1)}, bf16[16,8320]{1,0:T(8,128)(2,1)S(1)}, u32[]{:S(2)}, u32[]{:S(2)}) collective-permute-start(bf16[16,8320]{1,0:T(8,128)(2,1)} %collective-permute-done.3.refs_0_), channel_id=1, source_target_pairs={{0,1},{1,0},{2,3},{3,2},{4,5},{5,4},{6,7},{7,6},{8,9},{9,8},{10,11... | collective-permute-start | bytes 798728 | tf_op jit(solution)/shard_map/ppermute | solution.py:328
  43.3 5.8 %collective-permute-start.17 = (bf16[32,2176]{1,0:T(8,128)(2,1)S(1)}, bf16[32,2176]{1,0:T(8,128)(2,1)S(1)}, u32[]{:S(2)}, u32[]{:S(2)}) collective-permute-start(bf16[32,2176]{1,0:T(8,128)(2,1)S(1)} %slice.67), channel_id=1, source_target_pairs={{0,2},{2,0},{1,3},{3,1},{4,6},{6,4},{5,7},{7,5},{8,10},{10,8},{9,1... | collective-permute-start | bytes 417800 | tf_op jit(solution)/shard_map/ppermute | solution.py:328
  44.9 6.0 %collective-permute-start.13 = (bf16[128,2176]{1,0:T(8,128)(2,1)S(1)}, bf16[128,2176]{1,0:T(8,128)(2,1)S(1)}, u32[]{:S(2)}, u32[]{:S(2)}) collective-permute-start(bf16[128,2176]{1,0:T(8,128)(2,1)S(1)} %slice.41), channel_id=1, source_target_pairs={{0,1},{1,0},{2,3},{3,2},{4,5},{5,4},{6,7},{7,6},{8,9},{9,8},{10,11... | collective-permute-start | bytes 1671176 | tf_op jit(solution)/shard_map/ppermute | solution.py:328
  49.1 2.0 %collective-permute-start.18 = (bf16[64,2176]{1,0:T(8,128)(2,1)S(1)}, bf16[64,2176]{1,0:T(8,128)(2,1)S(1)}, u32[]{:S(2)}, u32[]{:S(2)}) collective-permute-start(bf16[64,2176]{1,0:T(8,128)(2,1)S(1)} %get-tuple-element.65), channel_id=1, source_target_pairs={{0,1},{1,0},{2,3},{3,2},{4,5},{5,4},{6,7},{7,6},{8,9},{9,8},{10,11... | collective-permute-start | bytes 835592 | tf_op jit(solution)/shard_map/ppermute | solution.py:328
  49.2 12.7 %collective-permute-start.22 = (bf16[32,2176]{1,0:T(8,128)(2,1)S(1)}, bf16[32,2176]{1,0:T(8,128)(2,1)S(1)}, u32[]{:S(2)}, u32[]{:S(2)}) collective-permute-start(bf16[32,2176]{1,0:T(8,128)(2,1)S(1)} %slice_add_fusion), channel_id=1, source_target_pairs={{0,8},{4,12},{8,0},{12,4},{1,9},{5,13},{9,1},{13,5},{2,10},{6,14},... | collective-permute-start | bytes 417800 | tf_op jit(solution)/shard_map/ppermute | solution.py:332
  51.2 6.6 %collective-permute-start.23 = (bf16[32,2176]{1,0:T(8,128)(2,1)S(1)}, bf16[32,2176]{1,0:T(8,128)(2,1)S(1)}, u32[]{:S(2)}, u32[]{:S(2)}) collective-permute-start(bf16[32,2176]{1,0:T(8,128)(2,1)S(1)} %slice.66), channel_id=1, source_target_pairs={{0,2},{2,0},{1,3},{3,1},{4,6},{6,4},{5,7},{7,5},{8,10},{10,8},{9,1... | collective-permute-start | bytes 417800 | tf_op jit(solution)/shard_map/ppermute | solution.py:328
  52.7 7.2 %collective-permute-start.19 = (bf16[32,2176]{1,0:T(8,128)(2,1)S(1)}, bf16[32,2176]{1,0:T(8,128)(2,1)S(1)}, u32[]{:S(2)}, u32[]{:S(2)}) collective-permute-start(bf16[32,2176]{1,0:T(8,128)(2,1)S(1)} %get-tuple-element.67), channel_id=1, source_target_pairs={{0,2},{2,0},{1,3},{3,1},{4,6},{6,4},{5,7},{7,5},{8,10},{10,8},{9,1... | collective-permute-start | bytes 417800 | tf_op jit(solution)/shard_map/ppermute | solution.py:328
  57.2 10.5 %copy-start.1 = (s32[32,8]{0,1:T(8,128)S(1)}, s32[32,8]{0,1:T(8,128)}, u32[]{:S(2)}) copy-start(s32[32,8]{0,1:T(8,128)} %param.9) | copy-start | bytes 3076
  57.8 7.8 %collective-permute-start.24 = (bf16[32,2176]{1,0:T(8,128)(2,1)S(1)}, bf16[32,2176]{1,0:T(8,128)(2,1)S(1)}, u32[]{:S(2)}, u32[]{:S(2)}) collective-permute-start(bf16[32,2176]{1,0:T(8,128)(2,1)S(1)} %convert_add_fusion.3), channel_id=1, source_target_pairs={{0,12},{4,8},{8,4},{12,0},{1,13},{5,9},{9,5},{13,1},{2,14},{6,10},... | collective-permute-start | bytes 417800 | tf_op jit(solution)/shard_map/ppermute | solution.py:332
  60.0 5.6 %collective-permute-start.20 = (bf16[32,2176]{1,0:T(8,128)(2,1)S(1)}, bf16[32,2176]{1,0:T(8,128)(2,1)S(1)}, u32[]{:S(2)}, u32[]{:S(2)}) collective-permute-start(bf16[32,2176]{1,0:T(8,128)(2,1)S(1)} %get-tuple-element.68), channel_id=1, source_target_pairs={{0,2},{2,0},{1,3},{3,1},{4,6},{6,4},{5,7},{7,5},{8,10},{10,8},{9,1... | collective-permute-start | bytes 417800 | tf_op jit(solution)/shard_map/ppermute | solution.py:328
  61.6 6.1 %collective-permute-start.21 = (bf16[32,2176]{1,0:T(8,128)(2,1)S(1)}, bf16[32,2176]{1,0:T(8,128)(2,1)S(1)}, u32[]{:S(2)}, u32[]{:S(2)}) collective-permute-start(bf16[32,2176]{1,0:T(8,128)(2,1)S(1)} %slice_add_fusion.1), channel_id=1, source_target_pairs={{0,4},{4,0},{8,12},{12,8},{1,5},{5,1},{9,13},{13,9},{2,6},{6,2},{1... | collective-permute-start | bytes 417800 | tf_op jit(solution)/shard_map/ppermute | solution.py:332

commit v5 on v4

--- a/solution.py
+++ b/solution.py
@@ -355,8 +355,8 @@
     columns[0], columns[1], columns[2], across[0], wide_w = together(packed, columns[1], columns[2], across[0], wide_w)
     columns[3] = far(columns[0], "expert", 3)
     across[2] = swap(columns[2], "dp")
-    across[1] = swap(columns[1], "dp")
-    columns[3], across[1], across[2] = together(columns[3], across[1], across[2])
+    across[1] = far(across[0], "expert", 1)
+    columns[3], across[2], across[1] = together(columns[3], across[2], across[1])
     across[3] = swap(columns[3], "dp")
 
     shards = [columns[2], across[2], columns[1], columns[0], across[1], across[0]]
@@ -384,12 +384,11 @@
     home_3 = paired_3[:rows] + swap(paired_3[rows:].astype(BF16), "dp").astype(F32)
     gate_grads, up_grads, down_grads = weight_grads((xe_0, xe_3), (diff_0, diff_3))
     home_1 = paired_10[:rows] + swap(away_1, "dp").astype(F32)
-    home_3, gate_grads = together(home_3, gate_grads)
-    home_1, away_0 = together(home_1, away_0)
+    home_3, gate_grads, away_0 = together(home_3, gate_grads, away_0)
+    back_0 = swap(away_0, "dp")
     back_3 = far(home_3.astype(BF16), "expert", 3)
-    back_0 = swap(away_0, "dp")
     back_1 = far(home_1.astype(BF16), "expert", 1)
-    arrived = (back_0, back_1, back_2, back_3)
+    arrived = (back_2, back_3, back_1, back_0)
     input_grad, routing_grad = finish(paired_10[rows : 2 * rows], arrived, routes)
     return (input_grad, routing_grad, gate_grads, up_grads, down_grads)
 

time: 68.7 us -> 67.9 us (0.988)
  starting transfers between devices: 23.9 us -> 23.2 us
    ppermute x19 -> x18, waiting for transfers between devices: 8.19 us -> 3.81 us  [swap(): return lax.ppermute(value, axis, [(0, 1), (1, 0)])]
    ppermute x6 -> x7, waiting for transfers between devices: 17.7 us -> 22 us  [far(): lax.ppermute(value, axis, [(i, i ^ distance) for i in range(lax.axis_size...]
    ppermute x19 -> x18, starting transfers between devices: 12.1 us -> 11.1 us  [swap(): return lax.ppermute(value, axis, [(0, 1), (1, 0)])]
    ppermute x6 -> x7, starting transfers between devices: 11.8 us -> 12.1 us  [far(): lax.ppermute(value, axis, [(i, i ^ distance) for i in range(lax.axis_size...]
  transfers between devices with their start and end apart: 25 -> 25, of which waited for: 13 -> 12; matrix products, arithmetic and copies ran while one was open for 1% -> 1% of each run, Pallas kernels for 23% -> 23%
where the time goes in v5:
time: 67.9 us; the launch traced here: 67.7 us
  waiting for transfers between devices  25.8 us (38%)
  starting transfers between devices  23.2 us (34%)
  Pallas kernels  17.3 us (25%)
  between operations  0.84 us (1%)
    ppermute x7, waiting for transfers between devices, far(): lax.ppermute(value, axis, [(i, i ^ distance) for i in range(lax.axis_size...  22 us
    ppermute x7, starting transfers between devices, far(): lax.ppermute(value, axis, [(i, i ^ distance) for i in range(lax.axis_size...  12.1 us
    ppermute x18, starting transfers between devices, swap(): return lax.ppermute(value, axis, [(0, 1), (1, 0)])  11.1 us
    pallas_call x2, Pallas kernels, expert_rows_chunk(): pl.pallas_call(functools.partial(rows_kernel, count, experts, first), in_...  9.7 us
    pallas_call x1, Pallas kernels, weight_grads(): pl.pallas_call(functools.partial(grads_kernel, count), in_specs=in_vmem(2...  3.93 us
    ppermute x18, waiting for transfers between devices, swap(): return lax.ppermute(value, axis, [(0, 1), (1, 0)])  3.81 us
    pallas_call x1, Pallas kernels, stage(): pl.pallas_call(stage_kernel, in_specs=in_hbm(2), out_specs=in_vmem(1)[0],...  1.89 us
  transfers between devices with their start and end apart: 25, of which 12 were waited for; matrix products, arithmetic and copies ran while one was open for 1% of the time, Pallas kernels for 23%

profile of v5, /device:TPU:0, one launch (start us, length us, event | category | flops | bytes accessed | tf_op | source)
XLA Modules:
  0.0 67.7 jit_solution(12371497517097844567)
XLA Ops:
  0.6 1.0 %pack_tokens.1.refs_3_ = bf16[16,8320]{1,0:T(8,128)(2,1)S(1)} custom-call(bf16[32,2048]{1,0:T(8,128)(2,1)} %x_ref.1, bf16[32,2048]{1,0:T(8,128)(2,1)} %e_ref.1, s32[8,32]{1,0:T(8,128)} %bitcast.3, f32[8,32]{1,0:T(8,128)} %bitcast.5), custom_call_target="tpu_custom_call" | custom-call | tf_op jit(solution)/shard_map/pack_tokens/pallas_call | solution.py:78
  1.7 3.1 %collective-permute-start = (bf16[16,8320]{1,0:T(8,128)(2,1)S(1)}, bf16[16,8320]{1,0:T(8,128)(2,1)}, u32[]{:S(2)}, u32[]{:S(2)}) collective-permute-start(bf16[16,8320]{1,0:T(8,128)(2,1)S(1)} %pack_tokens.1.refs_3_), channel_id=1, source_target_pairs={{0,4},{4,0},{8,12},{12,8},{1,5},{5,1},{9,13},{13,9},{2,6},{6,2},{1... | collective-permute-start | bytes 798728 | tf_op jit(solution)/shard_map/ppermute | solution.py:332
  4.8 2.6 %collective-permute-start.1 = (bf16[16,8320]{1,0:T(8,128)(2,1)S(1)}, bf16[16,8320]{1,0:T(8,128)(2,1)S(1)}, u32[]{:S(2)}, u32[]{:S(2)}) collective-permute-start(bf16[16,8320]{1,0:T(8,128)(2,1)S(1)} %pack_tokens.1.refs_3_), channel_id=1, source_target_pairs={{0,8},{4,12},{8,0},{12,4},{1,9},{5,13},{9,1},{13,5},{2,10},{6,14},... | collective-permute-start | bytes 798728 | tf_op jit(solution)/shard_map/ppermute | solution.py:332
  7.4 1.5 %collective-permute-start.2 = (bf16[16,8320]{1,0:T(8,128)(2,1)S(1)}, bf16[16,8320]{1,0:T(8,128)(2,1)S(1)}, u32[]{:S(2)}, u32[]{:S(2)}) collective-permute-start(bf16[16,8320]{1,0:T(8,128)(2,1)S(1)} %pack_tokens.1.refs_3_), channel_id=1, source_target_pairs={{0,2},{2,0},{1,3},{3,1},{4,6},{6,4},{5,7},{7,5},{8,10},{10,8},{9,1... | collective-permute-start | bytes 798728 | tf_op jit(solution)/shard_map/ppermute | solution.py:328
  8.8 1.9 %stage_weights.1.refs_12_.refs_4_ = bf16[2048,768]{1,0:T(8,128)(2,1)S(1)} custom-call(bf16[1,2048,384]{2,1,0:T(8,128)(2,1)} %gate_ref, bf16[1,2048,384]{2,1,0:T(8,128)(2,1)} %up_ref), custom_call_target="tpu_custom_call" | custom-call | flops 1 | bytes 1 | tf_op jit(solution)/shard_map/stage_weights/pallas_call | solution.py:112
  10.7 6.1 %collective-permute-done.refs_2_ = bf16[16,8320]{1,0:T(8,128)(2,1)} collective-permute-done((bf16[16,8320]{1,0:T(8,128)(2,1)S(1)}, bf16[16,8320]{1,0:T(8,128)(2,1)}, u32[]{:S(2)}, u32[]{:S(2)}) %collective-permute-start) | collective-permute-done | bytes 266272 | tf_op jit(solution)/shard_map/ppermute | solution.py:332
  16.9 2.4 %collective-permute-done.1.refs_0_ = bf16[16,8320]{1,0:T(8,128)(2,1)S(1)} collective-permute-done((bf16[16,8320]{1,0:T(8,128)(2,1)S(1)}, bf16[16,8320]{1,0:T(8,128)(2,1)S(1)}, u32[]{:S(2)}, u32[]{:S(2)}) %collective-permute-start.1) | collective-permute-done | bytes 266272 | tf_op jit(solution)/shard_map/ppermute | solution.py:332
  19.3 2.5 %collective-permute-start.3 = (bf16[16,8320]{1,0:T(8,128)(2,1)S(1)}, bf16[16,8320]{1,0:T(8,128)(2,1)}, u32[]{:S(2)}, u32[]{:S(2)}) collective-permute-start(bf16[16,8320]{1,0:T(8,128)(2,1)S(1)} %pack_tokens.1.refs_3_), channel_id=1, source_target_pairs={{0,12},{4,8},{8,4},{12,0},{1,13},{5,9},{9,5},{13,1},{2,14},{6,10},... | collective-permute-start | bytes 798728 | tf_op jit(solution)/shard_map/ppermute | solution.py:332
  21.8 1.5 %collective-permute-start.4 = (bf16[16,8320]{1,0:T(8,128)(2,1)S(1)}, bf16[16,8320]{1,0:T(8,128)(2,1)}, u32[]{:S(2)}, u32[]{:S(2)}) collective-permute-start(bf16[16,8320]{1,0:T(8,128)(2,1)S(1)} %collective-permute-done.1.refs_0_), channel_id=1, source_target_pairs={{0,2},{2,0},{1,3},{3,1},{4,6},{6,4},{5,7},{7,5},{8,10},{10,8},{9,1... | collective-permute-start | bytes 798728 | tf_op jit(solution)/shard_map/ppermute | solution.py:328
  23.3 0.5 collective-permute-start.6
  23.8 5.7 %collective-permute-done.3.refs_0_ = bf16[16,8320]{1,0:T(8,128)(2,1)} collective-permute-done((bf16[16,8320]{1,0:T(8,128)(2,1)S(1)}, bf16[16,8320]{1,0:T(8,128)(2,1)}, u32[]{:S(2)}, u32[]{:S(2)}) %collective-permute-start.3) | collective-permute-done | bytes 266272 | tf_op jit(solution)/shard_map/ppermute | solution.py:332
  29.5 0.5 collective-permute-start.8
  30.0 2.2 %collective-permute-done.5.refs_4_ = bf16[16,8320]{1,0:T(8,128)(2,1)} collective-permute-done((bf16[16,8320]{1,0:T(8,128)(2,1)S(1)}, bf16[16,8320]{1,0:T(8,128)(2,1)}, u32[]{:S(2)}, u32[]{:S(2)}) %collective-permute-start.5) | collective-permute-done | bytes 266272 | tf_op jit(solution)/shard_map/ppermute | solution.py:332
  32.2 0.5 collective-permute-start.7
  32.8 1.3 %collective-permute-start.12 = (bf16[16,8320]{1,0:T(8,128)(2,1)}, bf16[16,8320]{1,0:T(8,128)(2,1)}, u32[]{:S(2)}, u32[]{:S(2)}) collective-permute-start(bf16[16,8320]{1,0:T(8,128)(2,1)} %collective-permute-done.3.refs_0_), channel_id=1, source_target_pairs={{0,2},{2,0},{1,3},{3,1},{4,6},{6,4},{5,7},{7,5},{8,10},{10,8},{9,1... | collective-permute-start | bytes 798728 | tf_op jit(solution)/shard_map/ppermute | solution.py:328
  34.5 6.5 %rows_0.1 = (f32[192,2176]{1,0:T(8,128)S(1)}, bf16[192,2176]{1,0:T(8,128)(2,1)S(1)}, bf16[768,2048]{1,0:T(8,128)(2,1)S(1)}, bf16[384,1152]{1,0:T(8,128)(2,1)S(1)}, bf16[384,2048]{1,0:T(8,128)(2,1)S(1)}) custom-call(s32[8,128]{1,0:T(8,128)S(1)} %iota.7.expert_ref, bf16[16,8320]{1,0:T(8,128)(2,1)} %copy-done.2, ...), custom_call_target="tpu_custom_call" | custom-call | flops 1 | bytes 1 | tf_op jit(solution)/shard_map/rows_0/pallas_call | solution.py:225
  41.0 0.5 collective-permute-done.12.refs_1_
  41.6 0.5 collective-permute-start.15
  42.2 1.0 %collective-permute-done.16 = bf16[64,2176]{1,0:T(8,128)(2,1)S(1)} collective-permute-done((bf16[64,2176]{1,0:T(8,128)(2,1)S(1)}, bf16[64,2176]{1,0:T(8,128)(2,1)S(1)}, u32[]{:S(2)}, u32[]{:S(2)}) %collective-permute-start.16) | collective-permute-done | bytes 278560 | tf_op jit(solution)/shard_map/ppermute | solution.py:328
  43.2 1.3 %collective-permute-start.17 = (bf16[32,2176]{1,0:T(8,128)(2,1)S(1)}, bf16[32,2176]{1,0:T(8,128)(2,1)S(1)}, u32[]{:S(2)}, u32[]{:S(2)}) collective-permute-start(bf16[32,2176]{1,0:T(8,128)(2,1)S(1)} %slice.69), channel_id=1, source_target_pairs={{0,2},{2,0},{1,3},{3,1},{4,6},{6,4},{5,7},{7,5},{8,10},{10,8},{9,1... | collective-permute-start | bytes 417800 | tf_op jit(solution)/shard_map/ppermute | solution.py:328
  44.7 3.2 %rows_3.1 = (f32[64,2176]{1,0:T(8,128)S(1)}, bf16[64,2176]{1,0:T(8,128)(2,1)S(1)}, bf16[256,2048]{1,0:T(8,128)(2,1)S(1)}, bf16[128,1152]{1,0:T(8,128)(2,1)S(1)}) custom-call(s32[8,128]{1,0:T(8,128)S(1)} %iota.7.expert_ref, bf16[16,8320]{1,0:T(8,128)(2,1)} %collective-permute-done.3.refs_0_, bf16[16,8320]{1,0:T(8,128)(2,1)} %collective-permute-done.12.refs_1_, ...), custom_call_target="tpu_custom_call" | custom-call | flops 1 | bytes 1 | tf_op jit(solution)/shard_map/rows_3/pallas_call | solution.py:225
  47.9 1.1 %collective-permute-done.17 = bf16[32,2176]{1,0:T(8,128)(2,1)S(1)} collective-permute-done((bf16[32,2176]{1,0:T(8,128)(2,1)S(1)}, bf16[32,2176]{1,0:T(8,128)(2,1)S(1)}, u32[]{:S(2)}, u32[]{:S(2)}) %collective-permute-start.17) | collective-permute-done | bytes 139296 | tf_op jit(solution)/shard_map/ppermute | solution.py:328
  49.1 1.1 %collective-permute-start.18 = (bf16[32,2176]{1,0:T(8,128)(2,1)S(1)}, bf16[32,2176]{1,0:T(8,128)(2,1)S(1)}, u32[]{:S(2)}, u32[]{:S(2)}) collective-permute-start(bf16[32,2176]{1,0:T(8,128)(2,1)S(1)} %slice_add_fusion.1), channel_id=1, source_target_pairs={{0,8},{4,12},{8,0},{12,4},{1,9},{5,13},{9,1},{13,5},{2,10},{6,14},... | collective-permute-start | bytes 417800 | tf_op jit(solution)/shard_map/ppermute | solution.py:332
  50.8 1.3 %collective-permute-start.20 = (bf16[32,2176]{1,0:T(8,128)(2,1)S(1)}, bf16[32,2176]{1,0:T(8,128)(2,1)S(1)}, u32[]{:S(2)}, u32[]{:S(2)}) collective-permute-start(bf16[32,2176]{1,0:T(8,128)(2,1)S(1)} %slice.68), channel_id=1, source_target_pairs={{0,2},{2,0},{1,3},{3,1},{4,6},{6,4},{5,7},{7,5},{8,10},{10,8},{9,1... | collective-permute-start | bytes 417800 | tf_op jit(solution)/shard_map/ppermute | solution.py:328
  52.1 0.8 %collective-permute-start.22 = (bf16[32,2176]{1,0:T(8,128)(2,1)S(1)}, bf16[32,2176]{1,0:T(8,128)(2,1)S(1)}, u32[]{:S(2)}, u32[]{:S(2)}) collective-permute-start(bf16[32,2176]{1,0:T(8,128)(2,1)S(1)} %get-tuple-element.74), channel_id=1, source_target_pairs={{0,2},{2,0},{1,3},{3,1},{4,6},{6,4},{5,7},{7,5},{8,10},{10,8},{9,1... | collective-permute-start | bytes 417800 | tf_op jit(solution)/shard_map/ppermute | solution.py:328
  52.9 3.9 %weight_grads.1 = (bf16[1,2048,384]{2,1,0:T(8,128)(2,1)}, bf16[1,2048,384]{2,1,0:T(8,128)(2,1)}, bf16[1,384,2048]{2,1,0:T(8,128)(2,1)}) custom-call(bf16[768,2048]{1,0:T(8,128)(2,1)S(1)} %get-tuple-element.68.refs_0_, bf16[256,2048]{1,0:T(8,128)(2,1)S(1)} %get-tuple-element.69.refs_1_, bf16[384,1152]{1,0:T(8,128)(2,1)S(1)} %get-tuple-element.70.refs_2_, ...), custom_call_target="tpu_custom_call" | custom-call | flops 2415919104 | bytes 8912896 | tf_op jit(solution)/shard_map/weight_grads/pallas_call | solution.py:271
  56.8 0.5 collective-permute-done.20
  57.4 2.4 %collective-permute-start.21 = (bf16[32,2176]{1,0:T(8,128)(2,1)S(1)}, bf16[32,2176]{1,0:T(8,128)(2,1)S(1)}, u32[]{:S(2)}, u32[]{:S(2)}) collective-permute-start(bf16[32,2176]{1,0:T(8,128)(2,1)S(1)} %convert_add_fusion.3), channel_id=1, source_target_pairs={{0,12},{4,8},{8,4},{12,0},{1,13},{5,9},{9,5},{13,1},{2,14},{6,10},... | collective-permute-start | bytes 417800 | tf_op jit(solution)/shard_map/ppermute | solution.py:332
  59.8 1.1 %collective-permute-start.24 = (bf16[32,2176]{1,0:T(8,128)(2,1)S(1)}, bf16[32,2176]{1,0:T(8,128)(2,1)S(1)}, u32[]{:S(2)}, u32[]{:S(2)}) collective-permute-start(bf16[32,2176]{1,0:T(8,128)(2,1)S(1)} %get-tuple-element.75), channel_id=1, source_target_pairs={{0,2},{2,0},{1,3},{3,1},{4,6},{6,4},{5,7},{7,5},{8,10},{10,8},{9,1... | collective-permute-start | bytes 417800 | tf_op jit(solution)/shard_map/ppermute | solution.py:328
  61.3 4.3 %collective-permute-done.21.refs_1_ = bf16[32,2176]{1,0:T(8,128)(2,1)S(1)} collective-permute-done((bf16[32,2176]{1,0:T(8,128)(2,1)S(1)}, bf16[32,2176]{1,0:T(8,128)(2,1)S(1)}, u32[]{:S(2)}, u32[]{:S(2)}) %collective-permute-start.21) | collective-permute-done | bytes 139296 | tf_op jit(solution)/shard_map/ppermute | solution.py:332
  65.7 1.3 %collective-permute-done.23.refs_2_ = bf16[32,2176]{1,0:T(8,128)(2,1)S(1)} collective-permute-done((bf16[32,2176]{1,0:T(8,128)(2,1)S(1)}, bf16[32,2176]{1,0:T(8,128)(2,1)S(1)}, u32[]{:S(2)}, u32[]{:S(2)}) %collective-permute-start.23) | collective-permute-done | bytes 139296 | tf_op jit(solution)/shard_map/ppermute | solution.py:332
  67.0 0.8 %finish.1 = (bf16[32,2048]{1,0:T(8,128)(2,1)}, f32[8,32]{1,0:T(8,128)}) custom-call(f32[32,2176]{1,0:T(8,128)S(1)} %get-tuple-element.84.own_ref, bf16[32,2176]{1,0:T(8,128)(2,1)S(1)} %collective-permute-done.18.refs_0_, bf16[32,2176]{1,0:T(8,128)(2,1)S(1)} %collective-permute-done.21.refs_1_, bf16[32,2176]{1,0:T(8,128)(2,1)S(1)} %collective-permute-done.23.refs_2_, ...), custom_call_target="tpu_custom_call" | custom-call | tf_op jit(solution)/shard_map/finish/pallas_call | solution.py:313
  (49 shorter events, 2.0 us)
Async XLA Ops:
  1.7 27.8 %copy-start = (bf16[16,8320]{1,0:T(8,128)(2,1)}, bf16[16,8320]{1,0:T(8,128)(2,1)S(1)}, u32[]{:S(2)}) copy-start(bf16[16,8320]{1,0:T(8,128)(2,1)S(1)} %pack_tokens.1.refs_3_) | copy-start | bytes 798724
  1.7 15.2 %collective-permute-start = (bf16[16,8320]{1,0:T(8,128)(2,1)S(1)}, bf16[16,8320]{1,0:T(8,128)(2,1)}, u32[]{:S(2)}, u32[]{:S(2)}) collective-permute-start(bf16[16,8320]{1,0:T(8,128)(2,1)S(1)} %pack_tokens.1.refs_3_), channel_id=1, source_target_pairs={{0,4},{4,0},{8,12},{12,8},{1,5},{5,1},{9,13},{13,9},{2,6},{6,2},{1... | collective-permute-start | bytes 798728 | tf_op jit(solution)/shard_map/ppermute | solution.py:332
  4.8 14.5 %collective-permute-start.1 = (bf16[16,8320]{1,0:T(8,128)(2,1)S(1)}, bf16[16,8320]{1,0:T(8,128)(2,1)S(1)}, u32[]{:S(2)}, u32[]{:S(2)}) collective-permute-start(bf16[16,8320]{1,0:T(8,128)(2,1)S(1)} %pack_tokens.1.refs_3_), channel_id=1, source_target_pairs={{0,8},{4,12},{8,0},{12,4},{1,9},{5,13},{9,1},{13,5},{2,10},{6,14},... | collective-permute-start | bytes 798728 | tf_op jit(solution)/shard_map/ppermute | solution.py:332
  7.4 11.9 %collective-permute-start.2 = (bf16[16,8320]{1,0:T(8,128)(2,1)S(1)}, bf16[16,8320]{1,0:T(8,128)(2,1)S(1)}, u32[]{:S(2)}, u32[]{:S(2)}) collective-permute-start(bf16[16,8320]{1,0:T(8,128)(2,1)S(1)} %pack_tokens.1.refs_3_), channel_id=1, source_target_pairs={{0,2},{2,0},{1,3},{3,1},{4,6},{6,4},{5,7},{7,5},{8,10},{10,8},{9,1... | collective-permute-start | bytes 798728 | tf_op jit(solution)/shard_map/ppermute | solution.py:328
  19.3 10.2 %copy-start.2 = (bf16[16,8320]{1,0:T(8,128)(2,1)}, bf16[16,8320]{1,0:T(8,128)(2,1)S(1)}, u32[]{:S(2)}) copy-start(bf16[16,8320]{1,0:T(8,128)(2,1)S(1)} %collective-permute-done.1.refs_0_) | copy-start | bytes 798724
  19.3 13.5 %copy-start.3 = (bf16[16,8320]{1,0:T(8,128)(2,1)}, bf16[16,8320]{1,0:T(8,128)(2,1)S(1)}, u32[]{:S(2)}) copy-start(bf16[16,8320]{1,0:T(8,128)(2,1)S(1)} %collective-permute-done.2.refs_5_) | copy-start | bytes 798724
  19.3 10.2 %collective-permute-start.3 = (bf16[16,8320]{1,0:T(8,128)(2,1)S(1)}, bf16[16,8320]{1,0:T(8,128)(2,1)}, u32[]{:S(2)}, u32[]{:S(2)}) collective-permute-start(bf16[16,8320]{1,0:T(8,128)(2,1)S(1)} %pack_tokens.1.refs_3_), channel_id=1, source_target_pairs={{0,12},{4,8},{8,4},{12,0},{1,13},{5,9},{9,5},{13,1},{2,14},{6,10},... | collective-permute-start | bytes 798728 | tf_op jit(solution)/shard_map/ppermute | solution.py:332
  21.8 7.7 %collective-permute-start.4 = (bf16[16,8320]{1,0:T(8,128)(2,1)S(1)}, bf16[16,8320]{1,0:T(8,128)(2,1)}, u32[]{:S(2)}, u32[]{:S(2)}) collective-permute-start(bf16[16,8320]{1,0:T(8,128)(2,1)S(1)} %collective-permute-done.1.refs_0_), channel_id=1, source_target_pairs={{0,2},{2,0},{1,3},{3,1},{4,6},{6,4},{5,7},{7,5},{8,10},{10,8},{9,1... | collective-permute-start | bytes 798728 | tf_op jit(solution)/shard_map/ppermute | solution.py:328
  23.3 8.9 %collective-permute-start.5 = (bf16[16,8320]{1,0:T(8,128)(2,1)S(1)}, bf16[16,8320]{1,0:T(8,128)(2,1)}, u32[]{:S(2)}, u32[]{:S(2)}) collective-permute-start(bf16[16,8320]{1,0:T(8,128)(2,1)S(1)} %collective-permute-done.2.refs_5_), channel_id=1, source_target_pairs={{0,4},{4,0},{8,12},{12,8},{1,5},{5,1},{9,13},{13,9},{2,6},{6,2},{1... | collective-permute-start | bytes 798728 | tf_op jit(solution)/shard_map/ppermute | solution.py:332
  23.3 8.9 %collective-permute-start.11 = (bf16[16,8320]{1,0:T(8,128)(2,1)S(1)}, bf16[16,8320]{1,0:T(8,128)(2,1)S(1)}, u32[]{:S(2)}, u32[]{:S(2)}) collective-permute-start(bf16[16,8320]{1,0:T(8,128)(2,1)S(1)} %collective-permute-done.2.refs_5_), channel_id=1, source_target_pairs={{0,1},{1,0},{2,3},{3,2},{4,5},{5,4},{6,7},{7,6},{8,9},{9,8},{10,11... | collective-permute-start | bytes 798728 | tf_op jit(solution)/shard_map/ppermute | solution.py:328
  23.3 9.4 %collective-permute-start.6 = (bf16[16,8320]{1,0:T(8,128)(2,1)S(1)}, bf16[16,8320]{1,0:T(8,128)(2,1)S(1)}, u32[]{:S(2)}, u32[]{:S(2)}) collective-permute-start(bf16[16,8320]{1,0:T(8,128)(2,1)S(1)} %collective-permute-done.1.refs_0_), channel_id=1, source_target_pairs={{0,1},{1,0},{2,3},{3,2},{4,5},{5,4},{6,7},{7,6},{8,9},{9,8},{10,11... | collective-permute-start | bytes 798728 | tf_op jit(solution)/shard_map/ppermute | solution.py:328
  29.5 4.6 %collective-permute-start.9 = (bf16[16,8320]{1,0:T(8,128)(2,1)S(1)}, bf16[16,8320]{1,0:T(8,128)(2,1)}, u32[]{:S(2)}, u32[]{:S(2)}) collective-permute-start(bf16[16,8320]{1,0:T(8,128)(2,1)S(1)} %pack_tokens.1.refs_3_), channel_id=1, source_target_pairs={{0,1},{1,0},{2,3},{3,2},{4,5},{5,4},{6,7},{7,6},{8,9},{9,8},{10,11... | collective-permute-start | bytes 798728 | tf_op jit(solution)/shard_map/ppermute | solution.py:328
  29.5 4.6 %collective-permute-start.8 = (bf16[16,8320]{1,0:T(8,128)(2,1)}, bf16[16,8320]{1,0:T(8,128)(2,1)}, u32[]{:S(2)}, u32[]{:S(2)}) collective-permute-start(bf16[16,8320]{1,0:T(8,128)(2,1)} %collective-permute-done.refs_2_), channel_id=1, source_target_pairs={{0,1},{1,0},{2,3},{3,2},{4,5},{5,4},{6,7},{7,6},{8,9},{9,8},{10,11... | collective-permute-start | bytes 798728 | tf_op jit(solution)/shard_map/ppermute | solution.py:328
  32.2 1.9 %collective-permute-start.10 = (bf16[16,8320]{1,0:T(8,128)(2,1)}, bf16[16,8320]{1,0:T(8,128)(2,1)}, u32[]{:S(2)}, u32[]{:S(2)}) collective-permute-start(bf16[16,8320]{1,0:T(8,128)(2,1)} %collective-permute-done.5.refs_4_), channel_id=1, source_target_pairs={{0,1},{1,0},{2,3},{3,2},{4,5},{5,4},{6,7},{7,6},{8,9},{9,8},{10,11... | collective-permute-start | bytes 798728 | tf_op jit(solution)/shard_map/ppermute | solution.py:328
  32.2 1.9 %copy-start.4 = (bf16[16,8320]{1,0:T(8,128)(2,1)}, bf16[16,8320]{1,0:T(8,128)(2,1)S(1)}, u32[]{:S(2)}) copy-start(bf16[16,8320]{1,0:T(8,128)(2,1)S(1)} %collective-permute-done.11.refs_11_) | copy-start | bytes 798724
  32.2 2.3 %collective-permute-start.7 = (bf16[16,8320]{1,0:T(8,128)(2,1)}, bf16[16,8320]{1,0:T(8,128)(2,1)}, u32[]{:S(2)}, u32[]{:S(2)}) collective-permute-start(bf16[16,8320]{1,0:T(8,128)(2,1)} %collective-permute-done.4.refs_1_), channel_id=1, source_target_pairs={{0,1},{1,0},{2,3},{3,2},{4,5},{5,4},{6,7},{7,6},{8,9},{9,8},{10,11... | collective-permute-start | bytes 798728 | tf_op jit(solution)/shard_map/ppermute | solution.py:328
  32.8 1.3 %copy-start.5 = (bf16[16,8320]{1,0:T(8,128)(2,1)}, bf16[16,8320]{1,0:T(8,128)(2,1)S(1)}, u32[]{:S(2)}) copy-start(bf16[16,8320]{1,0:T(8,128)(2,1)S(1)} %collective-permute-done.6.refs_6_) | copy-start | bytes 798724
  32.8 8.7 %collective-permute-start.12 = (bf16[16,8320]{1,0:T(8,128)(2,1)}, bf16[16,8320]{1,0:T(8,128)(2,1)}, u32[]{:S(2)}, u32[]{:S(2)}) collective-permute-start(bf16[16,8320]{1,0:T(8,128)(2,1)} %collective-permute-done.3.refs_0_), channel_id=1, source_target_pairs={{0,2},{2,0},{1,3},{3,1},{4,6},{6,4},{5,7},{7,5},{8,10},{10,8},{9,1... | collective-permute-start | bytes 798728 | tf_op jit(solution)/shard_map/ppermute | solution.py:328
  41.5 1.6 %collective-permute-start.16 = (bf16[64,2176]{1,0:T(8,128)(2,1)S(1)}, bf16[64,2176]{1,0:T(8,128)(2,1)S(1)}, u32[]{:S(2)}, u32[]{:S(2)}) collective-permute-start(bf16[64,2176]{1,0:T(8,128)(2,1)S(1)} %slice.44), channel_id=1, source_target_pairs={{0,1},{1,0},{2,3},{3,2},{4,5},{5,4},{6,7},{7,6},{8,9},{9,8},{10,11... | collective-permute-start | bytes 835592 | tf_op jit(solution)/shard_map/ppermute | solution.py:328
  41.6 3.1 %collective-permute-start.15 = (bf16[16,8320]{1,0:T(8,128)(2,1)}, bf16[16,8320]{1,0:T(8,128)(2,1)S(1)}, u32[]{:S(2)}, u32[]{:S(2)}) collective-permute-start(bf16[16,8320]{1,0:T(8,128)(2,1)} %collective-permute-done.12.refs_1_), channel_id=1, source_target_pairs={{0,1},{1,0},{2,3},{3,2},{4,5},{5,4},{6,7},{7,6},{8,9},{9,8},{10,11... | collective-permute-start | bytes 798728 | tf_op jit(solution)/shard_map/ppermute | solution.py:328
  42.1 2.6 %collective-permute-start.14 = (bf16[16,8320]{1,0:T(8,128)(2,1)}, bf16[16,8320]{1,0:T(8,128)(2,1)S(1)}, u32[]{:S(2)}, u32[]{:S(2)}) collective-permute-start(bf16[16,8320]{1,0:T(8,128)(2,1)} %collective-permute-done.3.refs_0_), channel_id=1, source_target_pairs={{0,1},{1,0},{2,3},{3,2},{4,5},{5,4},{6,7},{7,6},{8,9},{9,8},{10,11... | collective-permute-start | bytes 798728 | tf_op jit(solution)/shard_map/ppermute | solution.py:328
  43.2 5.8 %collective-permute-start.17 = (bf16[32,2176]{1,0:T(8,128)(2,1)S(1)}, bf16[32,2176]{1,0:T(8,128)(2,1)S(1)}, u32[]{:S(2)}, u32[]{:S(2)}) collective-permute-start(bf16[32,2176]{1,0:T(8,128)(2,1)S(1)} %slice.69), channel_id=1, source_target_pairs={{0,2},{2,0},{1,3},{3,1},{4,6},{6,4},{5,7},{7,5},{8,10},{10,8},{9,1... | collective-permute-start | bytes 417800 | tf_op jit(solution)/shard_map/ppermute | solution.py:328
  44.6 5.6 %collective-permute-start.13 = (bf16[128,2176]{1,0:T(8,128)(2,1)S(1)}, bf16[128,2176]{1,0:T(8,128)(2,1)S(1)}, u32[]{:S(2)}, u32[]{:S(2)}) collective-permute-start(bf16[128,2176]{1,0:T(8,128)(2,1)S(1)} %slice.41), channel_id=1, source_target_pairs={{0,1},{1,0},{2,3},{3,2},{4,5},{5,4},{6,7},{7,6},{8,9},{9,8},{10,11... | collective-permute-start | bytes 1671176 | tf_op jit(solution)/shard_map/ppermute | solution.py:328
  49.1 1.6 %collective-permute-start.19 = (bf16[64,2176]{1,0:T(8,128)(2,1)S(1)}, bf16[64,2176]{1,0:T(8,128)(2,1)S(1)}, u32[]{:S(2)}, u32[]{:S(2)}) collective-permute-start(bf16[64,2176]{1,0:T(8,128)(2,1)S(1)} %get-tuple-element.65), channel_id=1, source_target_pairs={{0,1},{1,0},{2,3},{3,2},{4,5},{5,4},{6,7},{7,6},{8,9},{9,8},{10,11... | collective-permute-start | bytes 835592 | tf_op jit(solution)/shard_map/ppermute | solution.py:328
  49.1 12.2 %collective-permute-start.18 = (bf16[32,2176]{1,0:T(8,128)(2,1)S(1)}, bf16[32,2176]{1,0:T(8,128)(2,1)S(1)}, u32[]{:S(2)}, u32[]{:S(2)}) collective-permute-start(bf16[32,2176]{1,0:T(8,128)(2,1)S(1)} %slice_add_fusion.1), channel_id=1, source_target_pairs={{0,8},{4,12},{8,0},{12,4},{1,9},{5,13},{9,1},{13,5},{2,10},{6,14},... | collective-permute-start | bytes 417800 | tf_op jit(solution)/shard_map/ppermute | solution.py:332
  50.8 6.6 %collective-permute-start.20 = (bf16[32,2176]{1,0:T(8,128)(2,1)S(1)}, bf16[32,2176]{1,0:T(8,128)(2,1)S(1)}, u32[]{:S(2)}, u32[]{:S(2)}) collective-permute-start(bf16[32,2176]{1,0:T(8,128)(2,1)S(1)} %slice.68), channel_id=1, source_target_pairs={{0,2},{2,0},{1,3},{3,1},{4,6},{6,4},{5,7},{7,5},{8,10},{10,8},{9,1... | collective-permute-start | bytes 417800 | tf_op jit(solution)/shard_map/ppermute | solution.py:328
  52.1 8.7 %collective-permute-start.22 = (bf16[32,2176]{1,0:T(8,128)(2,1)S(1)}, bf16[32,2176]{1,0:T(8,128)(2,1)S(1)}, u32[]{:S(2)}, u32[]{:S(2)}) collective-permute-start(bf16[32,2176]{1,0:T(8,128)(2,1)S(1)} %get-tuple-element.74), channel_id=1, source_target_pairs={{0,2},{2,0},{1,3},{3,1},{4,6},{6,4},{5,7},{7,5},{8,10},{10,8},{9,1... | collective-permute-start | bytes 417800 | tf_op jit(solution)/shard_map/ppermute | solution.py:328
  56.8 10.2 %copy-start.1 = (s32[32,8]{0,1:T(8,128)S(1)}, s32[32,8]{0,1:T(8,128)}, u32[]{:S(2)}) copy-start(s32[32,8]{0,1:T(8,128)} %param.9) | copy-start | bytes 3076
  57.4 8.3 %collective-permute-start.21 = (bf16[32,2176]{1,0:T(8,128)(2,1)S(1)}, bf16[32,2176]{1,0:T(8,128)(2,1)S(1)}, u32[]{:S(2)}, u32[]{:S(2)}) collective-permute-start(bf16[32,2176]{1,0:T(8,128)(2,1)S(1)} %convert_add_fusion.3), channel_id=1, source_target_pairs={{0,12},{4,8},{8,4},{12,0},{1,13},{5,9},{9,5},{13,1},{2,14},{6,10},... | collective-permute-start | bytes 417800 | tf_op jit(solution)/shard_map/ppermute | solution.py:332
  59.8 5.9 %collective-permute-start.24 = (bf16[32,2176]{1,0:T(8,128)(2,1)S(1)}, bf16[32,2176]{1,0:T(8,128)(2,1)S(1)}, u32[]{:S(2)}, u32[]{:S(2)}) collective-permute-start(bf16[32,2176]{1,0:T(8,128)(2,1)S(1)} %get-tuple-element.75), channel_id=1, source_target_pairs={{0,2},{2,0},{1,3},{3,1},{4,6},{6,4},{5,7},{7,5},{8,10},{10,8},{9,1... | collective-permute-start | bytes 417800 | tf_op jit(solution)/shard_map/ppermute | solution.py:328
  60.9 6.1 %collective-permute-start.23 = (bf16[32,2176]{1,0:T(8,128)(2,1)S(1)}, bf16[32,2176]{1,0:T(8,128)(2,1)S(1)}, u32[]{:S(2)}, u32[]{:S(2)}) collective-permute-start(bf16[32,2176]{1,0:T(8,128)(2,1)S(1)} %get-tuple-element.83), channel_id=1, source_target_pairs={{0,4},{4,0},{8,12},{12,8},{1,5},{5,1},{9,13},{13,9},{2,6},{6,2},{1... | collective-permute-start | bytes 417800 | tf_op jit(solution)/shard_map/ppermute | solution.py:332
